TPU v7x, 128 devices: a whole 4x4x4 slice. The times are simulated.
128 devices in a mesh: vol: 8 (over z, core), ctl: 16 (over y, x).
Axes of the slice: x: 4, y: 4, z: 4, core: 2. Of those that a mesh axis runs over, the one named last changes fastest.
Arguments:
- sensitivity: float32 [3, 262144], P(None, ('vol', 'ctl')), may hold values from -24 to 24
- sens_ids: int32 [2048], P(('vol', 'ctl')), may hold values from 0 to 2047
- ctl_coords: float32 [3, 262144], P(None, 'ctl'), may hold values from -87 to 87
- partners: int32 [2048, 8], P('ctl'), may hold values from 0 to 2047, as said below
- node_coords: float32 [3, 1048576], P(None, ('vol', 'ctl')), may hold values from -87 to 87
- node_tiles: int32 [8192, 9], P(('vol', 'ctl')), may hold values from 0 to 2047, as said below
Outputs:
- control_weights: float32 [3, 262144], P(None, 'ctl')
- node_shift: float32 [3, 1048576], P(None, ('vol', 'ctl'))
Inputs may be any that keep to these rules, and one draw needn't show every extreme that they name: In each column the partners pair up the control blocks: if block b names block e, then e names b in the same column, and no block names itself. `node_tiles`: the 9 blocks of a row are distinct.
All inputs are finite; a program needn't handle non-finite values.
Results may differ from a plain program's by a relative error of at most 0.0003.
Values sent between devices are 32-bit elements; how exact they have to be, the bound alone decides.
No kernel may reach another device: no remote copies, remote signals or barrier semaphores. Data moves between devices by JAX's collectives and lax.ppermute only.
A program may use at most 64 MiB of HBM per device.

v0:
```python
import math

import jax
import jax.numpy as jnp
from jax import lax
from jax.sharding import PartitionSpec as P

BS = 128
ITERS = 2


highest = lax.Precision.HIGHEST
coupling = 0.0625
node_scale = 0.25


def wendland(dist_sq):
    ratio = jnp.sqrt(dist_sq)
    inner = jnp.maximum(1.0 - ratio, 0.0)
    return inner * inner * inner * inner * (4.0 * ratio + 1.0)


def local_dot(left, right):
    return jnp.sum(left * right, axis=(0, 2))


def residual_norm(vec):
    return lax.psum(local_dot(vec, vec), "ctl")


def spread_all(sensitivity, sens_ids, blocks_total):
    sens_blocks = sensitivity.reshape(3, -1, BS)
    onehot = (sens_ids[:, None] == jnp.arange(blocks_total, dtype=jnp.int32)[None, :]).astype(
        jnp.float32
    )
    return jnp.einsum("sq,csk->cqk", onehot, sens_blocks, precision=highest).reshape(
        3, blocks_total * BS
    )


def to_rows(array, blocks):
    return array.reshape(3, blocks, BS).transpose(1, 0, 2)


def body(sensitivity, sens_ids, ctl_coords, partners, node_coords, node_tiles):
    width = ctl_coords.shape[1]
    blocks_local = width // BS
    blocks_total = blocks_local * lax.axis_size("ctl")
    mates = partners.shape[1]
    spread = spread_all(sensitivity, sens_ids, blocks_total)
    summed = lax.psum(spread, "vol")
    forcing = lax.psum_scatter(summed, "ctl", scatter_dimension=1, tiled=True)
    forcing = to_rows(forcing, blocks_local)
    own_rows = to_rows(ctl_coords, blocks_local)
    all_rows = to_rows(lax.all_gather(ctl_coords, "ctl", axis=1, tiled=True), blocks_total)
    group_ctl = math.gcd(blocks_local, 16)
    count_ctl = blocks_local // group_ctl

    def apply_op(local_vec):
        full_vec = lax.all_gather(
            local_vec.reshape(blocks_local, 3 * BS), "ctl", axis=0, tiled=True
        ).reshape(blocks_total, 3, BS)

        def one_group(index, out):
            start = index * group_ctl
            vec_part = lax.dynamic_slice_in_dim(local_vec, start, group_ctl, 0)
            pts_part = lax.dynamic_slice_in_dim(own_rows, start, group_ctl, 0)
            lists = lax.dynamic_slice_in_dim(partners, start, group_ctl, 0)
            mate_pts = all_rows[lists]
            mate_vec = full_vec[lists]
            self_sq = jnp.zeros((group_ctl, BS, BS), jnp.float32)
            mate_sq = jnp.zeros((group_ctl, mates, BS, BS), jnp.float32)
            for comp in range(3):
                self_gap = pts_part[:, comp, :, None] - pts_part[:, comp, None, :]
                self_sq = self_sq + self_gap * self_gap
                mate_gap = pts_part[:, None, comp, :, None] - mate_pts[:, :, comp, None, :]
                mate_sq = mate_sq + mate_gap * mate_gap
            near = jnp.einsum("kij,kcj->kci", wendland(self_sq), vec_part, precision=highest)
            far = jnp.einsum("khij,khcj->kci", wendland(mate_sq), mate_vec, precision=highest)
            result = vec_part + (mates * near + far) * coupling
            return lax.dynamic_update_slice_in_dim(out, result, start, 0)

        out = lax.fori_loop(0, count_ctl, one_group, jnp.zeros_like(local_vec))
        return (out, full_vec)

    weights = jnp.zeros_like(forcing)
    full_weights = jnp.zeros((blocks_total, 3, BS), jnp.float32)
    residual = forcing
    direction = forcing
    norm_now = residual_norm(residual)
    for step in range(ITERS):
        image, full_dir = apply_op(direction)
        alpha = norm_now / lax.psum(local_dot(direction, image), "ctl")
        weights = weights + alpha[None, :, None] * direction
        residual = residual - alpha[None, :, None] * image
        norm_next = residual_norm(residual)
        direction = residual + (norm_next / norm_now)[None, :, None] * direction
        norm_now = norm_next
    full_weights = lax.all_gather(
        weights.reshape(blocks_local, 3 * BS), "ctl", axis=0, tiled=True
    ).reshape(blocks_total, 3, BS)
    own_weights = weights.transpose(1, 0, 2).reshape(3, width)
    node_blocks = node_coords.reshape(3, -1, BS)
    node_count = node_blocks.shape[1]
    group_node = math.gcd(node_count, 8)
    count_node = node_count // group_node

    def shift_group(index, out):
        start = index * group_node
        node_part = lax.dynamic_slice_in_dim(node_blocks, start, group_node, 1)
        lists = lax.dynamic_slice_in_dim(node_tiles, start, group_node, 0)
        near_pts = all_rows[lists]
        near_w = full_weights[lists]
        dist_sq = jnp.zeros((group_node, lists.shape[1], BS, BS), jnp.float32)
        for comp in range(3):
            gap = node_part[comp][:, None, :, None] - near_pts[:, :, comp, None, :]
            dist_sq = dist_sq + gap * gap
        result = (
            jnp.einsum("gtij,gtcj->cgi", wendland(dist_sq), near_w, precision=highest) * node_scale
        )
        return lax.dynamic_update_slice_in_dim(out, result, start, 1)

    shifted = lax.fori_loop(0, count_node, shift_group, jnp.zeros_like(node_blocks))
    node_shift = shifted.reshape(3, node_count * BS)
    return (own_weights, node_shift)


def solution(mesh):
    placed = (
        P(None, ("vol", "ctl")),
        P(("vol", "ctl")),
        P(None, "ctl"),
        P("ctl", None),
        P(None, ("vol", "ctl")),
        P(("vol", "ctl"), None),
    )
    return jax.shard_map(
        body,
        mesh=mesh,
        in_specs=placed,
        out_specs=(P(None, "ctl"), P(None, ("vol", "ctl"))),
        check_vma=False,
    )
```

profile of v0, /device:TPU:1, one launch (start us, length us, event | category | flops | bytes accessed | tf_op | source)
XLA Modules:
  0.0 990.2 jit_solution(2293425312437726235)
XLA Ops:
  9.6 10.0 %copy.121 = f32[1,3,2048,128]{3,1,2,0:T(4,128)} copy(f32[1,3,2048,128]{3,2,1,0:T(8,128)S(1)} %convolution_bitcast_fusion) | data formatting | bytes 6291456
  20.9 105.2 %all-reduce.7.cloned.1.call-done = f32[3,262144]{1,0:T(4,128)} async-done(((f32[3,262144]{1,0:T(4,128)}), f32[3,262144]{1,0:T(4,128)}) %all-reduce.7.cloned.1.call-update) | async-done | bytes 3145744
  127.9 59.0 %all-reduce.5.cloned.1.call-done = f32[3,16384]{1,0:T(4,128)} async-done(((f32[3,16384]{1,0:T(4,128)}), f32[3,16384]{1,0:T(4,128)}) %all-reduce.5.cloned.1.call-update) | async-done | bytes 196624 | tf_op jit(solution)/shard_map/psum | solution.py:51
  189.5 53.0 %all-gather.5.cloned.1.call-done = f32[2048,384]{0,1:T(8,128)} async-done(((f32[128,384]{0,1:T(8,128)}), f32[2048,384]{0,1:T(8,128)}) %all-gather.5.cloned.1.call-update) | async-done | bytes 3145744 | tf_op jit(solution)/shard_map/all_gather | solution.py:60
  247.4 48.9 %all-gather.7.cloned.1.call-done = f32[3,262144]{1,0:T(4,128)} async-done(((f32[3,16384]{1,0:T(4,128)}), f32[3,262144]{1,0:T(4,128)}) %all-gather.7.cloned.1.call-update) | async-done | bytes 3145744 | tf_op jit(solution)/shard_map/all_gather | solution.py:55
  296.4 177.4 %while.39 = (s32[]{:T(128)}, f32[128,3,128]{2,0,1:T(8,128)S(1)}, f32[128,3,128]{2,0,1:T(8,128)S(1)}, f32[128,3,128]{2,0,1:T(8,128)S(1)}, s32[128,8]{1,0:T(8,128)...) while((s32[]{:T(128)}, f32[128,3,128]{2,0,1:T(8,128)S(1)}, ...), condition=%wide.region_5.0_spmd, body=%wide.region_4.0_spmd.sunk | while | flops 122709384 | bytes 1883867 | solution.py:83
  302.6 13.3 %fusion.198 = f32[16,3,128]{2,1,0:T(4,128)S(1)} fusion(f32[16,8,3,128]{3,2,1,0:T(4,128)S(1)} %bitcast.184, f32[16,8,128]{2,1,0:T(8,128)S(1)} %bitcast.195, f32[16,128]{1,0:T(8,128)S(1)} %get-tuple-element.637, f32[16,8,128]{2,1,0:T(8,128)S(1)} %bitcast.194, f32[16,128]{1,0:T(8,128)S(1)} %get-tuple-element.639, f32[16,8,128]{2,1,0:T(8,128)S(1)} %bitcast.193, ...), kind=kOutput, calls=%fused_computation.32.clone.1 | convolution fusion | flops 109051904 | bytes 442368 | tf_op jit(solution)/shard_map/while/body/eval_jaxpr/khij,khcj->kci/dot_general | solution.py:79
  324.8 13.3 %fusion.198 = f32[16,3,128]{2,1,0:T(4,128)S(1)} fusion(f32[16,8,3,128]{3,2,1,0:T(4,128)S(1)} %bitcast.184, f32[16,8,128]{2,1,0:T(8,128)S(1)} %bitcast.195, f32[16,128]{1,0:T(8,128)S(1)} %get-tuple-element.637, f32[16,8,128]{2,1,0:T(8,128)S(1)} %bitcast.194, f32[16,128]{1,0:T(8,128)S(1)} %get-tuple-element.639, f32[16,8,128]{2,1,0:T(8,128)S(1)} %bitcast.193, ...), kind=kOutput, calls=%fused_computation.32.clone.1 | convolution fusion | flops 109051904 | bytes 442368 | tf_op jit(solution)/shard_map/while/body/eval_jaxpr/khij,khcj->kci/dot_general | solution.py:79
  347.0 13.3 %fusion.198 = f32[16,3,128]{2,1,0:T(4,128)S(1)} fusion(f32[16,8,3,128]{3,2,1,0:T(4,128)S(1)} %bitcast.184, f32[16,8,128]{2,1,0:T(8,128)S(1)} %bitcast.195, f32[16,128]{1,0:T(8,128)S(1)} %get-tuple-element.637, f32[16,8,128]{2,1,0:T(8,128)S(1)} %bitcast.194, f32[16,128]{1,0:T(8,128)S(1)} %get-tuple-element.639, f32[16,8,128]{2,1,0:T(8,128)S(1)} %bitcast.193, ...), kind=kOutput, calls=%fused_computation.32.clone.1 | convolution fusion | flops 109051904 | bytes 442368 | tf_op jit(solution)/shard_map/while/body/eval_jaxpr/khij,khcj->kci/dot_general | solution.py:79
  369.2 13.3 %fusion.198 = f32[16,3,128]{2,1,0:T(4,128)S(1)} fusion(f32[16,8,3,128]{3,2,1,0:T(4,128)S(1)} %bitcast.184, f32[16,8,128]{2,1,0:T(8,128)S(1)} %bitcast.195, f32[16,128]{1,0:T(8,128)S(1)} %get-tuple-element.637, f32[16,8,128]{2,1,0:T(8,128)S(1)} %bitcast.194, f32[16,128]{1,0:T(8,128)S(1)} %get-tuple-element.639, f32[16,8,128]{2,1,0:T(8,128)S(1)} %bitcast.193, ...), kind=kOutput, calls=%fused_computation.32.clone.1 | convolution fusion | flops 109051904 | bytes 442368 | tf_op jit(solution)/shard_map/while/body/eval_jaxpr/khij,khcj->kci/dot_general | solution.py:79
  391.3 13.3 %fusion.198 = f32[16,3,128]{2,1,0:T(4,128)S(1)} fusion(f32[16,8,3,128]{3,2,1,0:T(4,128)S(1)} %bitcast.184, f32[16,8,128]{2,1,0:T(8,128)S(1)} %bitcast.195, f32[16,128]{1,0:T(8,128)S(1)} %get-tuple-element.637, f32[16,8,128]{2,1,0:T(8,128)S(1)} %bitcast.194, f32[16,128]{1,0:T(8,128)S(1)} %get-tuple-element.639, f32[16,8,128]{2,1,0:T(8,128)S(1)} %bitcast.193, ...), kind=kOutput, calls=%fused_computation.32.clone.1 | convolution fusion | flops 109051904 | bytes 442368 | tf_op jit(solution)/shard_map/while/body/eval_jaxpr/khij,khcj->kci/dot_general | solution.py:79
  413.5 13.3 %fusion.198 = f32[16,3,128]{2,1,0:T(4,128)S(1)} fusion(f32[16,8,3,128]{3,2,1,0:T(4,128)S(1)} %bitcast.184, f32[16,8,128]{2,1,0:T(8,128)S(1)} %bitcast.195, f32[16,128]{1,0:T(8,128)S(1)} %get-tuple-element.637, f32[16,8,128]{2,1,0:T(8,128)S(1)} %bitcast.194, f32[16,128]{1,0:T(8,128)S(1)} %get-tuple-element.639, f32[16,8,128]{2,1,0:T(8,128)S(1)} %bitcast.193, ...), kind=kOutput, calls=%fused_computation.32.clone.1 | convolution fusion | flops 109051904 | bytes 442368 | tf_op jit(solution)/shard_map/while/body/eval_jaxpr/khij,khcj->kci/dot_general | solution.py:79
  435.7 13.3 %fusion.198 = f32[16,3,128]{2,1,0:T(4,128)S(1)} fusion(f32[16,8,3,128]{3,2,1,0:T(4,128)S(1)} %bitcast.184, f32[16,8,128]{2,1,0:T(8,128)S(1)} %bitcast.195, f32[16,128]{1,0:T(8,128)S(1)} %get-tuple-element.637, f32[16,8,128]{2,1,0:T(8,128)S(1)} %bitcast.194, f32[16,128]{1,0:T(8,128)S(1)} %get-tuple-element.639, f32[16,8,128]{2,1,0:T(8,128)S(1)} %bitcast.193, ...), kind=kOutput, calls=%fused_computation.32.clone.1 | convolution fusion | flops 109051904 | bytes 442368 | tf_op jit(solution)/shard_map/while/body/eval_jaxpr/khij,khcj->kci/dot_general | solution.py:79
  457.9 13.3 %fusion.198 = f32[16,3,128]{2,1,0:T(4,128)S(1)} fusion(f32[16,8,3,128]{3,2,1,0:T(4,128)S(1)} %bitcast.184, f32[16,8,128]{2,1,0:T(8,128)S(1)} %bitcast.195, f32[16,128]{1,0:T(8,128)S(1)} %get-tuple-element.637, f32[16,8,128]{2,1,0:T(8,128)S(1)} %bitcast.194, f32[16,128]{1,0:T(8,128)S(1)} %get-tuple-element.639, f32[16,8,128]{2,1,0:T(8,128)S(1)} %bitcast.193, ...), kind=kOutput, calls=%fused_computation.32.clone.1 | convolution fusion | flops 109051904 | bytes 442368 | tf_op jit(solution)/shard_map/while/body/eval_jaxpr/khij,khcj->kci/dot_general | solution.py:79
  474.0 31.2 %all-reduce.1 = (f32[3]{0:T(128)S(1)}, f32[3]{0:T(128)S(1)}) all-reduce(f32[3]{0:T(128)S(1)} %get-tuple-element.443, f32[3]{0:T(128)S(1)} %get-tuple-element.442), channel_id=1, replica_groups=mesh['vol'=8,'ctl'=16] {'ctl'}, use_global_device_ids=true, to_apply=%region_3.0 | all-reduce | flops 6 | bytes 48 | tf_op jit(solution)/shard_map/psum | solution.py:28
  505.4 28.7 %psum.38 = f32[3]{0:T(128)S(1)} all-reduce(f32[3]{0:T(128)S(1)} %multiply_reduce_fusion.1), channel_id=1, replica_groups=mesh['vol'=8,'ctl'=16] {'ctl'}, use_global_device_ids=true, to_apply=%region_9.0 | all-reduce | flops 3 | bytes 24 | tf_op jit(solution)/shard_map/psum | solution.py:28
  535.1 63.7 %all-gather.9.cloned.1.call-done = f32[2048,384]{0,1:T(8,128)} async-done(((f32[128,384]{0,1:T(8,128)}), f32[2048,384]{0,1:T(8,128)}) %all-gather.9.cloned.1.call-update) | async-done | bytes 3145744 | tf_op jit(solution)/shard_map/all_gather | solution.py:60
  603.8 177.4 %while.40 = (s32[]{:T(128)}, f32[128,3,128]{2,0,1:T(8,128)S(1)}, f32[128,3,128]{2,0,1:T(8,128)S(1)}, f32[128,3,128]{2,0,1:T(8,128)S(1)}, s32[128,8]{1,0:T(8,128)...) while((s32[]{:T(128)}, f32[128,3,128]{2,0,1:T(8,128)S(1)}, ...), condition=%wide.region_11.0_spmd, body=%wide.region_10.0_spmd.sunk | while | flops 122709384 | bytes 1883867 | solution.py:83
  610.0 13.3 %fusion.205 = f32[16,3,128]{2,1,0:T(4,128)S(1)} fusion(f32[16,8,3,128]{3,2,1,0:T(4,128)S(1)} %bitcast.185, f32[16,8,128]{2,1,0:T(8,128)S(1)} %bitcast.198, f32[16,128]{1,0:T(8,128)S(1)} %get-tuple-element.650, f32[16,8,128]{2,1,0:T(8,128)S(1)} %bitcast.197, f32[16,128]{1,0:T(8,128)S(1)} %get-tuple-element.652, f32[16,8,128]{2,1,0:T(8,128)S(1)} %bitcast.196, ...), kind=kOutput, calls=%fused_computation.100.clone.1 | convolution fusion | flops 109051904 | bytes 442368 | tf_op jit(solution)/shard_map/while/body/eval_jaxpr/khij,khcj->kci/dot_general | solution.py:79
  632.2 13.3 %fusion.205 = f32[16,3,128]{2,1,0:T(4,128)S(1)} fusion(f32[16,8,3,128]{3,2,1,0:T(4,128)S(1)} %bitcast.185, f32[16,8,128]{2,1,0:T(8,128)S(1)} %bitcast.198, f32[16,128]{1,0:T(8,128)S(1)} %get-tuple-element.650, f32[16,8,128]{2,1,0:T(8,128)S(1)} %bitcast.197, f32[16,128]{1,0:T(8,128)S(1)} %get-tuple-element.652, f32[16,8,128]{2,1,0:T(8,128)S(1)} %bitcast.196, ...), kind=kOutput, calls=%fused_computation.100.clone.1 | convolution fusion | flops 109051904 | bytes 442368 | tf_op jit(solution)/shard_map/while/body/eval_jaxpr/khij,khcj->kci/dot_general | solution.py:79
  654.4 13.3 %fusion.205 = f32[16,3,128]{2,1,0:T(4,128)S(1)} fusion(f32[16,8,3,128]{3,2,1,0:T(4,128)S(1)} %bitcast.185, f32[16,8,128]{2,1,0:T(8,128)S(1)} %bitcast.198, f32[16,128]{1,0:T(8,128)S(1)} %get-tuple-element.650, f32[16,8,128]{2,1,0:T(8,128)S(1)} %bitcast.197, f32[16,128]{1,0:T(8,128)S(1)} %get-tuple-element.652, f32[16,8,128]{2,1,0:T(8,128)S(1)} %bitcast.196, ...), kind=kOutput, calls=%fused_computation.100.clone.1 | convolution fusion | flops 109051904 | bytes 442368 | tf_op jit(solution)/shard_map/while/body/eval_jaxpr/khij,khcj->kci/dot_general | solution.py:79
  676.6 13.3 %fusion.205 = f32[16,3,128]{2,1,0:T(4,128)S(1)} fusion(f32[16,8,3,128]{3,2,1,0:T(4,128)S(1)} %bitcast.185, f32[16,8,128]{2,1,0:T(8,128)S(1)} %bitcast.198, f32[16,128]{1,0:T(8,128)S(1)} %get-tuple-element.650, f32[16,8,128]{2,1,0:T(8,128)S(1)} %bitcast.197, f32[16,128]{1,0:T(8,128)S(1)} %get-tuple-element.652, f32[16,8,128]{2,1,0:T(8,128)S(1)} %bitcast.196, ...), kind=kOutput, calls=%fused_computation.100.clone.1 | convolution fusion | flops 109051904 | bytes 442368 | tf_op jit(solution)/shard_map/while/body/eval_jaxpr/khij,khcj->kci/dot_general | solution.py:79
  698.8 13.3 %fusion.205 = f32[16,3,128]{2,1,0:T(4,128)S(1)} fusion(f32[16,8,3,128]{3,2,1,0:T(4,128)S(1)} %bitcast.185, f32[16,8,128]{2,1,0:T(8,128)S(1)} %bitcast.198, f32[16,128]{1,0:T(8,128)S(1)} %get-tuple-element.650, f32[16,8,128]{2,1,0:T(8,128)S(1)} %bitcast.197, f32[16,128]{1,0:T(8,128)S(1)} %get-tuple-element.652, f32[16,8,128]{2,1,0:T(8,128)S(1)} %bitcast.196, ...), kind=kOutput, calls=%fused_computation.100.clone.1 | convolution fusion | flops 109051904 | bytes 442368 | tf_op jit(solution)/shard_map/while/body/eval_jaxpr/khij,khcj->kci/dot_general | solution.py:79
  720.9 13.3 %fusion.205 = f32[16,3,128]{2,1,0:T(4,128)S(1)} fusion(f32[16,8,3,128]{3,2,1,0:T(4,128)S(1)} %bitcast.185, f32[16,8,128]{2,1,0:T(8,128)S(1)} %bitcast.198, f32[16,128]{1,0:T(8,128)S(1)} %get-tuple-element.650, f32[16,8,128]{2,1,0:T(8,128)S(1)} %bitcast.197, f32[16,128]{1,0:T(8,128)S(1)} %get-tuple-element.652, f32[16,8,128]{2,1,0:T(8,128)S(1)} %bitcast.196, ...), kind=kOutput, calls=%fused_computation.100.clone.1 | convolution fusion | flops 109051904 | bytes 442368 | tf_op jit(solution)/shard_map/while/body/eval_jaxpr/khij,khcj->kci/dot_general | solution.py:79
  743.1 13.3 %fusion.205 = f32[16,3,128]{2,1,0:T(4,128)S(1)} fusion(f32[16,8,3,128]{3,2,1,0:T(4,128)S(1)} %bitcast.185, f32[16,8,128]{2,1,0:T(8,128)S(1)} %bitcast.198, f32[16,128]{1,0:T(8,128)S(1)} %get-tuple-element.650, f32[16,8,128]{2,1,0:T(8,128)S(1)} %bitcast.197, f32[16,128]{1,0:T(8,128)S(1)} %get-tuple-element.652, f32[16,8,128]{2,1,0:T(8,128)S(1)} %bitcast.196, ...), kind=kOutput, calls=%fused_computation.100.clone.1 | convolution fusion | flops 109051904 | bytes 442368 | tf_op jit(solution)/shard_map/while/body/eval_jaxpr/khij,khcj->kci/dot_general | solution.py:79
  765.3 13.3 %fusion.205 = f32[16,3,128]{2,1,0:T(4,128)S(1)} fusion(f32[16,8,3,128]{3,2,1,0:T(4,128)S(1)} %bitcast.185, f32[16,8,128]{2,1,0:T(8,128)S(1)} %bitcast.198, f32[16,128]{1,0:T(8,128)S(1)} %get-tuple-element.650, f32[16,8,128]{2,1,0:T(8,128)S(1)} %bitcast.197, f32[16,128]{1,0:T(8,128)S(1)} %get-tuple-element.652, f32[16,8,128]{2,1,0:T(8,128)S(1)} %bitcast.196, ...), kind=kOutput, calls=%fused_computation.100.clone.1 | convolution fusion | flops 109051904 | bytes 442368 | tf_op jit(solution)/shard_map/while/body/eval_jaxpr/khij,khcj->kci/dot_general | solution.py:79
  781.4 30.9 %psum.39 = f32[3]{0:T(128)S(1)} all-reduce(f32[3]{0:T(128)S(1)} %multiply_reduce_fusion), channel_id=1, replica_groups=mesh['vol'=8,'ctl'=16] {'ctl'}, use_global_device_ids=true, to_apply=%region_13.0 | all-reduce | flops 3 | bytes 24 | tf_op jit(solution)/shard_map/psum | solution.py:93
  814.2 55.3 %all-gather.11.cloned.1.call-done = f32[2048,384]{0,1:T(8,128)} async-done(((f32[128,384]{0,1:T(8,128)}), f32[2048,384]{0,1:T(8,128)}) %all-gather.11.cloned.1.call-update) | async-done | bytes 3145744 | tf_op jit(solution)/shard_map/all_gather | solution.py:99
  874.5 108.2 %while.41 = (s32[]{:T(128)}, f32[3,64,128]{2,0,1:T(4,128)S(1)}, s32[64,9]{1,0:T(8,128)S(1)}, f32[2048,3,128]{2,1,0:T(4,128)}, f32[3,64,128]{2,1,0:T(8,128)S(1)},...) while((s32[]{:T(128)}, f32[3,64,128]{2,0,1:T(4,128)S(1)}, ...), condition=%wide.region_15.0_spmd, body=%wide.region_14.0_spmd.sunk | while | flops 61346016 | bytes 1288367 | solution.py:123
  880.5 7.5 fusion.210
  948.1 7.5 fusion.210
  961.6 7.5 fusion.210
  (289 shorter events, 252.5 us)
Async XLA Ops:
  7.2 119.0 %all-reduce.7.cloned.1.call-start = ((), (), s32[]{:S(2)}) async-start(), calls=%async_computation.5 | async-start | bytes 8388608
  9.6 10.1 %copy-start.6 = (u32[128]{0:T(128)S(1)}, u32[128]{0:T(128)}, u32[]{:S(2)}) copy-start(u32[128]{0:T(128)} %constant.205) | copy-start | bytes 1540
  19.6 169.7 %copy-start.1 = (f32[3,16384]{1,0:T(4,128)S(1)}, f32[3,16384]{1,0:T(4,128)}, u32[]{:S(2)}) copy-start(f32[3,16384]{1,0:T(4,128)} %param.14) | copy-start | bytes 589828
  19.6 169.8 %copy-start.5 = (s32[128,8]{0,1:T(8,128)S(1)}, s32[128,8]{0,1:T(8,128)}, u32[]{:S(2)}) copy-start(s32[128,8]{0,1:T(8,128)} %param.15) | copy-start | bytes 12292
  19.6 167.3 %all-reduce.5.cloned.1.call-start = ((), (), s32[]{:S(2)}) async-start(), calls=%async_computation.4 | async-start | bytes 524288 | tf_op jit(solution)/shard_map/psum | solution.py:51
  127.8 114.6 %all-gather.5.cloned.1.call-start = ((), (), s32[]{:S(2)}) async-start(), calls=%async_computation | async-start | bytes 3342336 | tf_op jit(solution)/shard_map/all_gather | solution.py:60
  188.7 107.7 %all-gather.7.cloned.1.call-start = ((), (), s32[]{:S(2)}) async-start(), calls=%async_computation.1 | async-start | bytes 4456448 | tf_op jit(solution)/shard_map/all_gather | solution.py:55
  189.3 409.5 %all-gather.9.cloned.1.call-start = ((), (), s32[]{:S(2)}) async-start(), calls=%async_computation.2 | async-start | bytes 3342336 | tf_op jit(solution)/shard_map/all_gather | solution.py:60
  296.4 177.5 %copy-start = (f32[3,16384]{1,0:T(4,128)S(1)}, f32[3,16384]{1,0:T(4,128)}, u32[]{:S(2)}) copy-start(f32[3,16384]{1,0:T(4,128)} %all-reduce.5.cloned.1.call-done) | copy-start | bytes 589828
  535.0 334.4 %all-gather.11.cloned.1.call-start = ((), (), s32[]{:S(2)}) async-start(), calls=%async_computation.3 | async-start | bytes 3342336 | tf_op jit(solution)/shard_map/all_gather | solution.py:99
  603.8 209.4 %copy-start.2 = (f32[3,8192]{1,0:T(4,128)S(1)}, f32[3,8192]{1,0:T(4,128)}, u32[]{:S(2)}) copy-start(f32[3,8192]{1,0:T(4,128)} %param.16) | copy-start | bytes 294916
  603.8 209.5 %copy-start.4 = (s32[64,9]{0,1:T(8,128)S(1)}, s32[64,9]{0,1:T(8,128)}, u32[]{:S(2)}) copy-start(s32[64,9]{0,1:T(8,128)} %param.17) | copy-start | bytes 6916
  982.7 0.7 copy-start.3
Sparse Core Ops, SparseCore 0:
  19.7 106.3 all-reduce.6
  129.0 57.8 all-reduce.4
  189.8 52.5 all-gather.4
  244.7 51.6 all-gather.6
  535.1 63.5 all-gather.8
  813.4 56.0 all-gather.10
where the time goes:
time: 993 us; the launch traced here: 990 us
  waiting for transfers between devices  386 us (39%)
  matrix products  318 us (32%)
  local copies, waits for them, and re-layouts  178 us (18%)
  blocking collectives  90.7 us (9%)
  between operations  14.9 us (2%)
    dot_general x16, matrix products, one_group(): jnp.einsum('khij,khcj->kci', wendland(mate_sq), mate_vec, precision=highest)  213 us
    all_gather x2, waiting for transfers between devices, apply_op(): lax.all_gather(local_vec.reshape(blocks_local, 3 * BS), 'ctl', axis=0, ti...  117 us
    unnamed x7, waiting for transfers between devices  106 us
    dot_general x8, matrix products, shift_group(): jnp.einsum('gtij,gtcj->cgi', wendland(dist_sq), near_w, precision=highest)  60.3 us
    psum x2, blocking collectives, residual_norm(): return lax.psum(local_dot(vec, vec), 'ctl')  59.9 us
    psum x1, waiting for transfers between devices, body(): summed = lax.psum(spread, 'vol')  59 us
    all_gather x1, waiting for transfers between devices, body(): lax.all_gather(weights.reshape(blocks_local, 3 * BS), 'ctl', axis=0, tile...  55.3 us
    all_gather x1, waiting for transfers between devices, body(): lax.all_gather(ctl_coords, 'ctl', axis=1, tiled=True)  48.9 us
  transfers between devices with their start and end apart: 6, of which 6 were waited for; matrix products, arithmetic and copies ran while one was open for 1% of the time, Pallas kernels for 0%

commit v1 on v0

v1 whole, which is shorter than its diff:
```python
import functools

import jax
import jax.numpy as jnp
from jax import lax
from jax.experimental import pallas as pl
from jax.experimental.pallas import tpu as pltpu
from jax.sharding import PartitionSpec as P

BS = 128
COUPLING = 0.0625
NODE_SCALE = 0.25
VMEM = 56 * 1024 * 1024
CHUNK = 32


def whole(shape):
    return pl.BlockSpec(shape, lambda *a: (0,) * len(shape))


def lane_sums(acc):
    ones = jnp.ones((8, BS), jnp.bfloat16)
    dims = (((1,), (1,)), ((), ()))
    rows = lax.broadcasted_iota(jnp.int32, (8, BS), 0)
    out = jnp.zeros((8, BS), jnp.float32)
    for k, part in enumerate(acc):
        high = part.astype(jnp.bfloat16)
        rest = part - high.astype(jnp.float32)
        mid = rest.astype(jnp.bfloat16)
        total = lax.dot_general(ones, high, dims, preferred_element_type=jnp.float32)
        total = total + lax.dot_general(ones, mid, dims, preferred_element_type=jnp.float32)
        out = jnp.where(rows == k, total, out)
    return out


def tiles_kernel(reach, group, with_vec, idx_ref, pts_ref, ctl_ref, *refs):
    if with_vec:
        vec_ref, tile_ref, sum_ref, acc_ref = refs
    else:
        (tile_ref,) = refs
    step = pl.program_id(0)

    def one(g, carry):
        cols = jnp.transpose(pts_ref[g])
        base = (step * group + g) * reach
        for lo in range(0, BS, CHUNK):
            own = [jnp.broadcast_to(cols[lo : lo + CHUNK, k : k + 1], (CHUNK, BS)) for k in range(3)]
            acc = [jnp.zeros((CHUNK, BS), jnp.float32) for _ in range(3)]
            for t in range(reach):
                at = idx_ref[base + t]
                dist = None
                for k in range(3):
                    gap = own[k] - ctl_ref[pl.ds(at + 16 * k, 1), :]
                    dist = gap * gap if dist is None else dist + gap * gap
                ratio = dist * lax.rsqrt(jnp.maximum(dist, 1e-30))
                inner = jnp.maximum(1.0 - ratio, 0.0)
                sq = inner * inner
                tile = (sq * sq) * (4.0 * ratio + 1.0)
                tile_ref[g * reach + t, lo : lo + CHUNK, :] = tile
                if with_vec:
                    for k in range(3):
                        acc[k] = acc[k] + tile * vec_ref[pl.ds(at + 16 * k, 1), :]
            if with_vec:
                for k in range(3):
                    acc_ref[k, lo : lo + CHUNK, :] = acc[k]
        if with_vec:
            sum_ref[g] = lane_sums([acc_ref[k] for k in range(3)])
        return carry

    lax.fori_loop(0, group, one, 0)


def make_tiles(idx, pts, ctl, vec, reach, group):
    count = pts.shape[0]
    with_vec = vec is not None
    out_shape = [jax.ShapeDtypeStruct((count * reach, BS, BS), jnp.float32)]
    out_specs = [pl.BlockSpec((group * reach, BS, BS), lambda m, *_: (m, 0, 0))]
    scratch = []
    operands = [pts, ctl]
    in_specs = [pl.BlockSpec((group, 8, BS), lambda m, *_: (m, 0, 0)), whole(ctl.shape)]
    if with_vec:
        out_shape.append(jax.ShapeDtypeStruct((count, 8, BS), jnp.float32))
        out_specs.append(pl.BlockSpec((group, 8, BS), lambda m, *_: (m, 0, 0)))
        scratch = [pltpu.VMEM((3, BS, BS), jnp.float32)]
        operands.append(vec)
        in_specs.append(whole(vec.shape))
    elements = count * reach * BS * BS
    return pl.pallas_call(
        functools.partial(tiles_kernel, reach, group, with_vec),
        out_shape=out_shape,
        grid_spec=pltpu.PrefetchScalarGridSpec(
            num_scalar_prefetch=1,
            grid=(count // group,),
            in_specs=in_specs,
            out_specs=out_specs,
            scratch_shapes=scratch,
        ),
        compiler_params=pltpu.CompilerParams(vmem_limit_bytes=VMEM),
        cost_estimate=pl.CostEstimate(
            flops=elements * 24, bytes_accessed=elements * 4, transcendentals=elements
        ),
    )(idx, *operands)


def apply_kernel(reach, group, stride, first_scale, idx_ref, tile_ref, vec_ref, sum_ref, acc_ref):
    step = pl.program_id(0)

    def one(g, carry):
        base = (step * group + g) * reach
        for lo in range(0, BS, CHUNK):
            acc = [jnp.zeros((CHUNK, BS), jnp.float32) for _ in range(3)]
            for t in range(reach):
                at = idx_ref[base + t]
                tile = tile_ref[g * reach + t, lo : lo + CHUNK, :]
                for k in range(3):
                    row = vec_ref[pl.ds(at + stride * k, 1), :]
                    if t == 0 and first_scale != 1.0:
                        row = row * first_scale
                    acc[k] = acc[k] + tile * row
            for k in range(3):
                acc_ref[k, lo : lo + CHUNK, :] = acc[k]
        sum_ref[g] = lane_sums([acc_ref[k] for k in range(3)])
        return carry

    lax.fori_loop(0, group, one, 0)


def apply_tiles(idx, tiles, vec, reach, group, stride, first_scale):
    count = tiles.shape[0] // reach
    elements = tiles.size
    return pl.pallas_call(
        functools.partial(apply_kernel, reach, group, stride, first_scale),
        out_shape=jax.ShapeDtypeStruct((count, 8, BS), jnp.float32),
        grid_spec=pltpu.PrefetchScalarGridSpec(
            num_scalar_prefetch=1,
            grid=(count // group,),
            in_specs=[
                pl.BlockSpec((group * reach, BS, BS), lambda m, *_: (m, 0, 0)),
                whole(vec.shape),
            ],
            out_specs=pl.BlockSpec((group, 8, BS), lambda m, *_: (m, 0, 0)),
            scratch_shapes=[pltpu.VMEM((3, BS, BS), jnp.float32)],
        ),
        compiler_params=pltpu.CompilerParams(vmem_limit_bytes=VMEM),
        cost_estimate=pl.CostEstimate(
            flops=elements * 6, bytes_accessed=elements * 4, transcendentals=0
        ),
    )(idx, tiles, vec)


def spread_kernel(rows, want_ref, sens_ref, out_ref):
    ids = jnp.sum(sens_ref[:, 48, :].reshape(16, 8, BS), axis=1)
    want = want_ref[...]
    acc = [jnp.zeros((rows, BS), jnp.float32) for _ in range(3)]
    for g in range(16):
        hot = (want == ids[g : g + 1, :]).astype(jnp.bfloat16)
        for k in range(3):
            part = sens_ref[8 * g : 8 * g + 8, 16 * k : 16 * k + 16, :].reshape(BS, BS)
            for piece in range(3):
                cut = part.astype(jnp.bfloat16)
                acc[k] = acc[k] + jnp.dot(hot, cut, preferred_element_type=jnp.float32)
                if piece < 2:
                    part = part - cut.astype(jnp.float32)
    for k in range(3):
        out_ref[k] = acc[k]


def spread(want, sens):
    rows = want.shape[0]
    return pl.pallas_call(
        functools.partial(spread_kernel, rows),
        out_shape=jax.ShapeDtypeStruct((3, rows, BS), jnp.float32),
        compiler_params=pltpu.CompilerParams(vmem_limit_bytes=VMEM),
        cost_estimate=pl.CostEstimate(
            flops=rows * 2048 * 384 * 6, bytes_accessed=sens.size * 4, transcendentals=0
        ),
    )(want, sens)


def spread_all_kernel(sens_ref, out_ref, cut_ref, ids_ref):
    step = pl.program_id(0)

    @pl.when(step == 0)
    def _():
        ids_ref[...] = jnp.sum(sens_ref[:, 48, :].reshape(16, 8, BS), axis=1)
        for k in range(3):
            part = sens_ref[:, 16 * k : 16 * k + 16, :].reshape(2048, BS)
            high = part.astype(jnp.bfloat16)
            cut_ref[0, :, k * BS : (k + 1) * BS] = high
            cut_ref[1, :, k * BS : (k + 1) * BS] = (part - high.astype(jnp.float32)).astype(jnp.bfloat16)

    want = (lax.broadcasted_iota(jnp.int32, (256, BS), 0) + step * 256).astype(jnp.float32)
    hot = jnp.concatenate(
        [(want == ids_ref[g : g + 1, :]).astype(jnp.bfloat16) for g in range(16)], axis=1
    )
    acc = jnp.dot(hot, cut_ref[0], preferred_element_type=jnp.float32)
    acc = acc + jnp.dot(hot, cut_ref[1], preferred_element_type=jnp.float32)
    for k in range(3):
        out_ref[:, 16 * k : 16 * k + 16, :] = acc[:, k * BS : (k + 1) * BS].reshape(16, 16, BS)


def spread_all(sens):
    return pl.pallas_call(
        spread_all_kernel,
        out_shape=jax.ShapeDtypeStruct((128, 48, BS), jnp.float32),
        grid=(8,),
        in_specs=[whole(sens.shape)],
        out_specs=pl.BlockSpec((16, 48, BS), lambda m: (m, 0, 0)),
        scratch_shapes=[
            pltpu.VMEM((2, 2048, 3 * BS), jnp.bfloat16),
            pltpu.VMEM((16, BS), jnp.float32),
        ],
        compiler_params=pltpu.CompilerParams(vmem_limit_bytes=VMEM),
        cost_estimate=pl.CostEstimate(
            flops=2048 * 2048 * 384 * 4, bytes_accessed=sens.size * 8, transcendentals=0
        ),
    )(sens)


def total_of(part):
    return jnp.sum(jnp.sum(part, axis=0, keepdims=True), axis=1, keepdims=True)


def step_kernel(f_ref, q_ref, p_ref, coef_ref):
    zeros = tuple(jnp.zeros((16, BS), jnp.float32) for _ in range(6))

    def first(d, carry):
        out = []
        for k in range(3):
            f, q = f_ref[d, 16 * k : 16 * k + 16, :], q_ref[d, 16 * k : 16 * k + 16, :]
            out += [carry[2 * k] + f * f, carry[2 * k + 1] + f * q]
        return tuple(out)

    sums = lax.fori_loop(0, 128, first, zeros, unroll=4)
    now = [total_of(sums[2 * k]) for k in range(3)]
    alpha = [now[k] / total_of(sums[2 * k + 1]) for k in range(3)]

    def second(d, carry):
        out = []
        for k in range(3):
            f, q = f_ref[d, 16 * k : 16 * k + 16, :], q_ref[d, 16 * k : 16 * k + 16, :]
            r = f - alpha[k] * q
            p_ref[d, 16 * k : 16 * k + 16, :] = r
            out.append(carry[k] + r * r)
        return tuple(out)

    sums = lax.fori_loop(0, 128, second, zeros[:3], unroll=4)
    later = [total_of(sums[k]) for k in range(3)]
    beta = [later[k] / now[k] for k in range(3)]

    def third(d, carry):
        for k in range(3):
            at = slice(16 * k, 16 * k + 16)
            p_ref[d, at, :] = p_ref[d, at, :] + beta[k] * f_ref[d, at, :]
        return carry

    lax.fori_loop(0, 128, third, 0, unroll=4)
    rows = lax.broadcasted_iota(jnp.int32, (8, BS), 0)
    out = jnp.zeros((8, BS), jnp.float32)
    for k in range(3):
        out = jnp.where(rows == k, alpha[k], out)
        out = jnp.where(rows == 4 + k, later[k], out)
    coef_ref[...] = out


def cg_step(f, q):
    return pl.pallas_call(
        step_kernel,
        out_shape=[
            jax.ShapeDtypeStruct(f.shape, jnp.float32),
            jax.ShapeDtypeStruct((8, BS), jnp.float32),
        ],
        input_output_aliases={1: 0},
        compiler_params=pltpu.CompilerParams(vmem_limit_bytes=VMEM),
        cost_estimate=pl.CostEstimate(
            flops=f.size * 10, bytes_accessed=f.size * 12, transcendentals=0
        ),
    )(f, q)


def over_ctl(x):
    size = lax.axis_size("ctl")
    return lax.all_to_all(jnp.broadcast_to(x[None], (size,) + x.shape), "ctl", 0, 0, tiled=True)


def over_vol(x):
    return lax.all_gather(x, "vol", axis=0, tiled=True)


def place(block):
    return (((block >> 4) & 7) * 16 + (block >> 7)) * 48 + (block & 15)


def slot(block):
    return (((block >> 4) & 7) * 16 + (block >> 7)) * 16 + (block & 15)


def padded(rows):
    return jnp.pad(rows.transpose(1, 0, 2), ((0, 0), (0, 5), (0, 0)))


def body(sensitivity, sens_ids, ctl_coords, partners, node_coords, node_tiles):
    vol, ctl = lax.axis_index("vol"), lax.axis_index("ctl")
    device = vol * 16 + ctl
    own_coords = lax.dynamic_slice_in_dim(ctl_coords.reshape(3, 128, BS), vol * 16, 16, 1)
    ids = slot(sens_ids).astype(jnp.float32)
    lanes = jnp.arange(BS) // 16 == device % 8
    id_row = jnp.where(lanes, jnp.tile(ids, 8), 0.0)[None]
    payload = jnp.concatenate(
        [
            own_coords.reshape(48, BS),
            sensitivity.reshape(48, BS),
            jnp.pad(id_row, ((0, 7), (0, 0))),
        ],
        axis=0,
    )
    near = over_ctl(payload)
    coords = over_vol(near[:, :48])
    sens = over_vol(near[:, 48:])
    coords_rows = coords.reshape(128 * 48, BS)

    own = ctl * 128 + vol * 16 + jnp.arange(16, dtype=jnp.int32)
    mates = lax.dynamic_slice_in_dim(partners, vol * 16, 16, 0)
    lists = jnp.concatenate([own[:, None], mates], axis=1).reshape(-1)
    op_at = place(lists)
    node_at = place(node_tiles.reshape(-1))

    (op_tiles,) = make_tiles(op_at, padded(own_coords), coords_rows, None, 9, 2)
    want = jnp.broadcast_to(slot(lists).astype(jnp.float32)[:, None], (144, BS))
    f_near = spread(want, sens)
    sums = apply_tiles(
        jnp.arange(144, dtype=jnp.int32), op_tiles, f_near.reshape(3 * 144, BS), 9, 2, 144, 8.0
    )

    def back(total):
        return total[:, :3].transpose(1, 0, 2)

    f_own = f_near.reshape(3, 16, 9, BS)[:, :, 0]
    image = f_own + back(sums) * COUPLING
    near_image = over_ctl(image.reshape(48, BS))
    image_all = over_vol(near_image)
    f_all = spread_all(sens)
    node_rows = node_coords.reshape(3, 64, BS)
    node_tile, node_f = make_tiles(
        node_at, padded(node_rows), coords_rows, f_all.reshape(128 * 48, BS), 9, 4
    )
    p_all, coef = cg_step(f_all, image_all)
    p_rows = p_all.reshape(128 * 48, BS)
    sums = apply_tiles(op_at, op_tiles, p_rows, 9, 2, 16, 8.0)
    p_own = lax.dynamic_slice_in_dim(p_all, device, 1, 0).reshape(3, 16, BS)
    image = p_own + back(sums) * COUPLING
    dots = jnp.sum(p_own * image, axis=(1, 2))
    dot_row = jnp.broadcast_to(jnp.pad(dots, (0, BS - 3))[None], (128, BS))
    dots = jnp.sum(lax.all_to_all(dot_row, ("vol", "ctl"), 0, 0, tiled=True), axis=0)[:3]
    node_p = apply_tiles(node_at, node_tile, p_rows, 9, 4, 16, 1.0)

    alpha0 = coef[0:3, 0]
    alpha1 = coef[4:7, 0] / dots

    def mine(full):
        part = lax.dynamic_slice_in_dim(full.reshape(8, 16, 3, 16, BS), ctl, 1, 1)
        return part.reshape(8, 3, 16, BS).transpose(1, 0, 2, 3).reshape(3, 128, BS)

    weights = alpha0[:, None, None] * mine(f_all) + alpha1[:, None, None] * mine(p_all)
    shift = NODE_SCALE * (
        alpha0[:, None, None] * back(node_f) + alpha1[:, None, None] * back(node_p)
    )
    return weights.reshape(3, -1), shift.reshape(3, -1)


def solution(mesh):
    placed = (
        P(None, ("vol", "ctl")),
        P(("vol", "ctl")),
        P(None, "ctl"),
        P("ctl", None),
        P(None, ("vol", "ctl")),
        P(("vol", "ctl"), None),
    )
    return jax.shard_map(
        body,
        mesh=mesh,
        in_specs=placed,
        out_specs=(P(None, "ctl"), P(None, ("vol", "ctl"))),
        check_vma=False,
    )
```

time: 993 us -> 260 us (0.26)
  waiting for transfers between devices: 386 us -> 45.5 us
  matrix products: 318 us -> 0 us
  local copies, waits for them, and re-layouts: 178 us -> 10.7 us
  Pallas kernels: 0 us -> 141 us
  blocking collectives: 90.7 us -> 37.5 us
    dot_general x41 -> x0, matrix products: 318 us -> none  [the longest x16 213 us: one_group(): jnp.einsum('khij,khcj->kci', wendland(mate_sq), mate_vec, precision=highest)]
    all_gather x4 -> x3, waiting for transfers between devices: 221 us -> 45.5 us  [over_vol(): return lax.all_gather(x, 'vol', axis=0, tiled=True)]
    pallas_call x0 -> x8, Pallas kernels: none -> 141 us  [the longest x2 66.9 us: make_tiles(): pl.pallas_call(functools.partial(tiles_kernel, reach, group, with_vec), o...]
    gather x48 -> x0, local copies, waits for them, and re-layouts: 140 us -> none  [the longest x16 47.2 us: one_group(): mate_pts = all_rows[lists]]
    unnamed x7 -> x3, waiting for transfers between devices: 106 us -> 0.05 us
    psum x3 -> x0, blocking collectives: 90.7 us -> none  [the longest x2 59.9 us: residual_norm(): return lax.psum(local_dot(vec, vec), 'ctl')]
    psum x1 -> x0, waiting for transfers between devices: 59 us -> none  [body(): summed = lax.psum(spread, 'vol')]
    all_to_all x0 -> x2, blocking collectives: none -> 37.5 us  [over_ctl(): lax.all_to_all(jnp.broadcast_to(x[None], (size,) + x.shape), 'ctl', 0, 0,...]
  transfers between devices with their start and end apart: 6 -> 4, of which waited for: 6 -> 2; matrix products, arithmetic and copies ran while one was open for 1% -> 2% of each run, Pallas kernels for 0% -> 42%
where the time goes in v1:
time: 260 us; the launch traced here: 259 us
  Pallas kernels  141 us (54%)
  waiting for transfers between devices  45.5 us (18%)
  blocking collectives  37.5 us (14%)
  between operations  14 us (5%)
  local copies, waits for them, and re-layouts  10.7 us (4%)
  starting transfers between devices  5.26 us (2%)
  other arithmetic  5.26 us (2%)
    pallas_call x2, Pallas kernels, make_tiles(): pl.pallas_call(functools.partial(tiles_kernel, reach, group, with_vec), o...  66.9 us
    pallas_call x3, Pallas kernels, apply_tiles(): pl.pallas_call(functools.partial(apply_kernel, reach, group, stride, firs...  48.2 us
    all_gather x3, waiting for transfers between devices, over_vol(): return lax.all_gather(x, 'vol', axis=0, tiled=True)  45.5 us
    all_to_all x2, blocking collectives, over_ctl(): lax.all_to_all(jnp.broadcast_to(x[None], (size,) + x.shape), 'ctl', 0, 0,...  37.5 us
    pallas_call x1, Pallas kernels, spread_all(): pl.pallas_call(spread_all_kernel, out_shape=jax.ShapeDtypeStruct((128, 48...  13.5 us
    pallas_call x1, Pallas kernels, cg_step(): pl.pallas_call(step_kernel, out_shape=[jax.ShapeDtypeStruct(f.shape, jnp....  6.25 us
    pallas_call x1, Pallas kernels, spread(): pl.pallas_call(functools.partial(spread_kernel, rows), out_shape=jax.Shap...  5.67 us
  transfers between devices with their start and end apart: 4, of which 2 were waited for; matrix products, arithmetic and copies ran while one was open for 2% of the time, Pallas kernels for 42%

profile of v1, /device:TPU:1, one launch (start us, length us, event | category | flops | bytes accessed | tf_op | source)
XLA Modules:
  0.0 258.8 jit_solution(13616280606452276820)
XLA Ops:
  7.3 0.7 add_convert_fusion.1
  8.0 0.8 reshape.168
  8.9 21.6 %all_to_all.16 = f32[16,104,128]{2,1,0:T(8,128)S(1)} all-to-all(f32[16,104,128]{2,1,0:T(8,128)S(1)} %broadcast_in_dim.15), channel_id=1, replica_groups=mesh['vol'=8,'ctl'=16] {'ctl'}, dimensions={0} | all-to-all | bytes 1703936 | tf_op jit(solution)/shard_map/all_to_all | solution.py:283
  30.5 0.8 slice.42
  31.4 0.8 slice.40
  32.6 0.7 reshape.190.idx_ref
  33.3 0.6 pad.17.pts_ref
  33.9 25.4 %all-gather.6.cloned.1.call-done = f32[128,48,128]{2,1,0:T(8,128)} async-done(((f32[16,48,128]{2,1,0:T(8,128)}), f32[128,48,128]{2,1,0:T(8,128)}) %all-gather.6.cloned.1.call-update) | async-done | bytes 3145744 | tf_op jit(solution)/shard_map/all_gather | solution.py:287
  59.4 11.8 %shard_map.79.tile_ref = f32[144,128,128]{2,1,0:T(8,128)} custom-call(s32[144]{0:T(256)} %reshape.190.idx_ref, f32[16,8,128]{2,1,0:T(8,128)} %pad.17.pts_ref, f32[6144,128]{1,0:T(8,128)} %bitcast.66), custom_call_target="tpu_custom_call" | custom-call | flops 56623104 | bytes 9437184 | tf_op jit(solution)/shard_map/pallas_call | solution.py:88
  71.1 20.0 %all-gather.4.cloned.1.call-done.sens_ref = f32[128,56,128]{2,1,0:T(8,128)} async-done(((f32[16,56,128]{2,1,0:T(8,128)}), f32[128,56,128]{2,1,0:T(8,128)}) %all-gather.4.cloned.1.call-update) | async-done | bytes 3670032 | tf_op jit(solution)/shard_map/all_gather | solution.py:287
  91.2 0.7 broadcast_in_dim.16.want_ref
  91.9 5.7 %shard_map.78 = f32[3,144,128]{2,1,0:T(8,128)} custom-call(f32[144,128]{1,0:T(8,128)} %broadcast_in_dim.16.want_ref, f32[128,56,128]{2,1,0:T(8,128)} %all-gather.4.cloned.1.call-done.sens_ref), custom_call_target="tpu_custom_call" | custom-call | flops 679477248 | bytes 3670016 | tf_op jit(solution)/shard_map/pallas_call | solution.py:170
  97.6 1.1 copy.75
  98.6 0.5 iota.13.idx_ref
  99.1 9.9 %shard_map.80 = f32[16,8,128]{2,1,0:T(8,128)} custom-call(s32[144]{0:T(256)} %iota.13.idx_ref, f32[144,128,128]{2,1,0:T(8,128)} %shard_map.79.tile_ref, f32[432,128]{1,0:T(8,128)} %bitcast.68), custom_call_target="tpu_custom_call" | custom-call | flops 14155776 | bytes 9437184 | tf_op jit(solution)/shard_map/pallas_call | solution.py:131
  109.1 0.8 fusion.7
  110.0 15.9 %all_to_all.17 = f32[16,48,128]{2,1,0:T(8,128)} all-to-all(f32[16,48,128]{2,1,0:T(8,128)S(1)} %broadcast_in_dim.18), channel_id=1, replica_groups=mesh['vol'=8,'ctl'=16] {'ctl'}, dimensions={0} | all-to-all | bytes 786432 | tf_op jit(solution)/shard_map/all_to_all | solution.py:283
  126.0 0.7 reshape.191.idx_ref
  126.8 0.7 pad.19.pts_ref
  127.5 13.5 %shard_map.77.f_ref = f32[128,48,128]{2,1,0:T(8,128)} custom-call(f32[128,56,128]{2,1,0:T(8,128)} %all-gather.4.cloned.1.call-done.sens_ref), custom_call_target="tpu_custom_call" | custom-call | flops 6442450944 | bytes 7340032 | tf_op jit(solution)/shard_map/pallas_call | solution.py:203
  141.0 55.1 %shard_map.83 = (f32[576,128,128]{2,1,0:T(8,128)}, f32[64,8,128]{2,1,0:T(8,128)}) custom-call(s32[576]{0:T(1024)} %reshape.191.idx_ref, f32[64,8,128]{2,1,0:T(8,128)} %pad.19.pts_ref, f32[6144,128]{1,0:T(8,128)} %bitcast.67, f32[6144,128]{1,0:T(8,128)} %bitcast.64), custom_call_target="tpu_custom_call" | custom-call | flops 226492416 | bytes 37748736 | tf_op jit(solution)/shard_map/pallas_call | solution.py:88
  196.1 6.2 %shard_map.81 = (f32[128,48,128]{2,1,0:T(8,128)}, f32[8,128]{1,0:T(8,128)}) custom-call(f32[128,48,128]{2,1,0:T(8,128)} %shard_map.77.f_ref, f32[128,48,128]{2,1,0:T(8,128)} %all-gather.8.cloned.1.call-done.q_ref), custom_call_target="tpu_custom_call", output_to_operand_aliasing={{0}: (1, {})} | custom-call | flops 7864320 | bytes 9437184 | tf_op jit(solution)/shard_map/pallas_call | solution.py:267
  202.4 10.8 %shard_map.82 = f32[16,8,128]{2,1,0:T(8,128)} custom-call(s32[144]{0:T(256)} %reshape.190.idx_ref, f32[144,128,128]{2,1,0:T(8,128)} %shard_map.79.tile_ref, f32[6144,128]{1,0:T(8,128)} %bitcast.61), custom_call_target="tpu_custom_call" | custom-call | flops 14155776 | bytes 9437184 | tf_op jit(solution)/shard_map/pallas_call | solution.py:131
  213.2 0.7 constant_dynamic-slice_fusion
  213.9 1.0 fusion.4
  214.9 0.7 broadcast_in_dim.19
  215.5 5.1 %all-to-all-start.2 = ((f32[128,1,128]{2,1,0:T(1,128)}), f32[128,1,128]{2,1,0:T(1,128)S(1)}, u32[]{:S(2)}, u32[]{:S(2)}) async-start(f32[128,1,128]{2,1,0:T(1,128)} %broadcast_in_dim.19), calls=%async_computation.2 | async-start | bytes 131072 | tf_op jit(solution)/shard_map/all_to_all | solution.py:354
  220.7 1.1 dynamic-slice_bitcast_fusion
  221.8 27.5 %shard_map.84 = f32[64,8,128]{2,1,0:T(8,128)} custom-call(s32[576]{0:T(1024)} %reshape.191.idx_ref, f32[576,128,128]{2,1,0:T(8,128)} %get-tuple-element.9.tile_ref, f32[6144,128]{1,0:T(8,128)} %bitcast.63), custom_call_target="tpu_custom_call" | custom-call | flops 56623104 | bytes 37748736 | tf_op jit(solution)/shard_map/pallas_call | solution.py:131
  249.4 0.1 slice_reduce_fusion.1
  249.5 1.0 fusion
  250.5 1.7 fusion.3
  (45 shorter events, 1.0 us)
Async XLA Ops:
  7.2 1.6 copy-start
  7.2 25.1 %copy-start.6 = (s32[128,8]{0,1:T(8,128)S(1)}, s32[128,8]{0,1:T(8,128)}, u32[]{:S(2)}) copy-start(s32[128,8]{0,1:T(8,128)} %param.9) | copy-start | bytes 12292
  7.2 52.2 %all-gather.6.cloned.1.call-start = ((), (), s32[]{:S(2)}) async-start(), calls=%async_computation.4 | async-start | bytes 3538944 | tf_op jit(solution)/shard_map/all_gather | solution.py:287
  31.3 59.9 %all-gather.4.cloned.1.call-start = ((), (), s32[]{:S(2)}) async-start(), calls=%async_computation.3 | async-start | bytes 4128768 | tf_op jit(solution)/shard_map/all_gather | solution.py:287
  32.2 164.0 %all-gather.8.cloned.1.call-start = ((), (), s32[]{:S(2)}) async-start(), calls=%async_computation.5 | async-start | bytes 3538944 | tf_op jit(solution)/shard_map/all_gather | solution.py:287
  99.1 26.8 %copy-start.4 = (s32[64,9]{0,1:T(8,128)S(1)}, s32[64,9]{0,1:T(8,128)}, u32[]{:S(2)}) copy-start(s32[64,9]{0,1:T(8,128)} %param.11) | copy-start | bytes 6916
  99.1 27.6 %copy-start.2 = (f32[3,8192]{1,0:T(4,128)S(1)}, f32[3,8192]{1,0:T(4,128)}, u32[]{:S(2)}) copy-start(f32[3,8192]{1,0:T(4,128)} %param.10) | copy-start | bytes 294916
  215.5 33.9 %all-to-all-start.2 = ((f32[128,1,128]{2,1,0:T(1,128)}), f32[128,1,128]{2,1,0:T(1,128)S(1)}, u32[]{:S(2)}, u32[]{:S(2)}) async-start(f32[128,1,128]{2,1,0:T(1,128)} %broadcast_in_dim.19), calls=%async_computation.2 | async-start | bytes 131072 | tf_op jit(solution)/shard_map/all_to_all | solution.py:354
  221.8 27.5 %copy-start.5 = (f32[8,128]{1,0:T(8,128)S(1)}, f32[8,128]{1,0:T(8,128)}, u32[]{:S(2)}) copy-start(f32[8,128]{1,0:T(8,128)} %get-tuple-element.6) | copy-start | bytes 12292
  221.8 28.7 %copy-start.3 = (f32[64,8,128]{2,1,0:T(8,128)S(1)}, f32[64,8,128]{2,1,0:T(8,128)}, u32[]{:S(2)}) copy-start(f32[64,8,128]{2,1,0:T(8,128)} %get-tuple-element.8) | copy-start | bytes 786436
  221.8 30.4 %copy-start.1 = (f32[3,16384]{1,0:T(4,128)S(1)}, f32[3,16384]{1,0:T(4,128)}, u32[]{:S(2)}) copy-start(f32[3,16384]{1,0:T(4,128)} %param.8) | copy-start | bytes 589828
Sparse Core Ops, SparseCore 0:
  31.4 27.8 all-gather.5
  61.1 30.0 all-gather.3
  126.0 25.2 all-gather.7

commit v2 on v1

v2 whole, which is shorter than its diff:
```python
import functools

import jax
import jax.numpy as jnp
from jax import lax
from jax.experimental import pallas as pl
from jax.experimental.pallas import tpu as pltpu
from jax.sharding import PartitionSpec as P

BS = 128
COUPLING = 0.0625
NODE_SCALE = 0.25
VMEM = 56 * 1024 * 1024
CHUNK = 32
HEAD = 32


def whole(shape):
    return pl.BlockSpec(shape, lambda *a: (0,) * len(shape))


def lane_sums(group, acc_ref):
    ones = jnp.ones((BS, BS), jnp.bfloat16)
    eye = lax.broadcasted_iota(jnp.int32, (BS, BS), 0) == lax.broadcasted_iota(jnp.int32, (BS, BS), 1)
    out = []
    for k in range(3):
        part = acc_ref[k]
        high = part.astype(jnp.bfloat16)
        rest = (part - high.astype(jnp.float32)).astype(jnp.bfloat16)
        total = jnp.dot(high, ones, preferred_element_type=jnp.float32)
        total = total + jnp.dot(rest, ones, preferred_element_type=jnp.float32)
        out.append(
            [
                jnp.sum(jnp.where(eye, total[g * BS : (g + 1) * BS], 0.0), axis=0, keepdims=True)
                for g in range(group)
            ]
        )
    return out


def store_sums(group, acc_ref, sum_ref):
    rows = lax.broadcasted_iota(jnp.int32, (8, BS), 0)
    found = lane_sums(group, acc_ref)
    for g in range(group):
        out = jnp.zeros((8, BS), jnp.float32)
        for k in range(3):
            out = jnp.where(rows == k, found[k][g], out)
        sum_ref[g] = out


def tiles_kernel(reach, group, with_vec, idx_ref, pts_ref, ctl_ref, *refs):
    if with_vec:
        vec_ref, tile_ref, sum_ref, cols_ref, acc_ref = refs
    else:
        tile_ref, cols_ref = refs
    step = pl.program_id(0)
    for g in range(group):
        cols_ref[g] = jnp.transpose(pts_ref[g])

    def one(g, carry):
        base = (step * group + g) * reach
        for lo in range(0, BS, CHUNK):
            own = [jnp.broadcast_to(cols_ref[g, lo : lo + CHUNK, k : k + 1], (CHUNK, BS)) for k in range(3)]
            acc = [jnp.zeros((CHUNK, BS), jnp.float32) for _ in range(3)]
            for t in range(reach):
                at = idx_ref[base + t]
                dist = None
                for k in range(3):
                    gap = own[k] - ctl_ref[pl.ds(at + 16 * k, 1), :]
                    dist = gap * gap if dist is None else dist + gap * gap
                ratio = dist * lax.rsqrt(jnp.maximum(dist, 1e-30))
                inner = jnp.maximum(1.0 - ratio, 0.0)
                sq = inner * inner
                tile = (sq * sq) * (4.0 * ratio + 1.0)
                tile_ref[g * reach + t, lo : lo + CHUNK, :] = tile
                if with_vec:
                    for k in range(3):
                        acc[k] = acc[k] + tile * vec_ref[pl.ds(at + 16 * k, 1), :]
            if with_vec:
                for k in range(3):
                    acc_ref[k, pl.ds(pl.multiple_of(g * BS, BS) + lo, CHUNK), :] = acc[k]
        return carry

    lax.fori_loop(0, group, one, 0)
    if with_vec:
        store_sums(group, acc_ref, sum_ref)


def make_tiles(idx, pts, ctl, vec, reach, group):
    count = pts.shape[0]
    with_vec = vec is not None
    out_shape = [jax.ShapeDtypeStruct((count * reach, BS, BS), jnp.float32)]
    out_specs = [pl.BlockSpec((group * reach, BS, BS), lambda m, *_: (m, 0, 0))]
    scratch = [pltpu.VMEM((group, BS, 8), jnp.float32)]
    operands = [pts, ctl]
    in_specs = [pl.BlockSpec((group, 8, BS), lambda m, *_: (m, 0, 0)), whole(ctl.shape)]
    if with_vec:
        out_shape.append(jax.ShapeDtypeStruct((count, 8, BS), jnp.float32))
        out_specs.append(pl.BlockSpec((group, 8, BS), lambda m, *_: (m, 0, 0)))
        scratch.append(pltpu.VMEM((3, group * BS, BS), jnp.float32))
        operands.append(vec)
        in_specs.append(whole(vec.shape))
    elements = count * reach * BS * BS
    return pl.pallas_call(
        functools.partial(tiles_kernel, reach, group, with_vec),
        out_shape=out_shape,
        grid_spec=pltpu.PrefetchScalarGridSpec(
            num_scalar_prefetch=1,
            grid=(count // group,),
            in_specs=in_specs,
            out_specs=out_specs,
            scratch_shapes=scratch,
        ),
        compiler_params=pltpu.CompilerParams(vmem_limit_bytes=VMEM),
        cost_estimate=pl.CostEstimate(
            flops=elements * 24, bytes_accessed=elements * 4, transcendentals=elements
        ),
    )(idx, *operands)


def apply_kernel(reach, group, count, idx_ref, tile_ref, *refs):
    vec_refs, sum_refs, acc_refs = refs[:count], refs[count : 2 * count], refs[2 * count :]
    step = pl.program_id(0)

    def one(g, carry):
        base = (step * group + g) * reach
        start = pl.multiple_of(g * BS, BS)
        for lo in range(0, BS, CHUNK):
            acc = [[jnp.zeros((CHUNK, BS), jnp.float32) for _ in range(3)] for _ in vec_refs]
            for t in range(reach):
                at = idx_ref[base + t]
                tile = tile_ref[g * reach + t, lo : lo + CHUNK, :]
                for n, vec_ref in enumerate(vec_refs):
                    for k in range(3):
                        acc[n][k] = acc[n][k] + tile * vec_ref[pl.ds(at + 16 * k, 1), :]
            for n, acc_ref in enumerate(acc_refs):
                for k in range(3):
                    acc_ref[k, pl.ds(start + lo, CHUNK), :] = acc[n][k]
        return carry

    lax.fori_loop(0, group, one, 0)
    for acc_ref, sum_ref in zip(acc_refs, sum_refs):
        store_sums(group, acc_ref, sum_ref)


def apply_tiles(idx, tiles, vecs, reach, group):
    count = tiles.shape[0] // reach
    elements = tiles.size
    return pl.pallas_call(
        functools.partial(apply_kernel, reach, group, len(vecs)),
        out_shape=[jax.ShapeDtypeStruct((count, 8, BS), jnp.float32) for _ in vecs],
        grid_spec=pltpu.PrefetchScalarGridSpec(
            num_scalar_prefetch=1,
            grid=(count // group,),
            in_specs=[pl.BlockSpec((group * reach, BS, BS), lambda m, *_: (m, 0, 0))]
            + [whole(vec.shape) for vec in vecs],
            out_specs=[pl.BlockSpec((group, 8, BS), lambda m, *_: (m, 0, 0)) for _ in vecs],
            scratch_shapes=[pltpu.VMEM((3, group * BS, BS), jnp.float32) for _ in vecs],
        ),
        compiler_params=pltpu.CompilerParams(vmem_limit_bytes=VMEM),
        cost_estimate=pl.CostEstimate(
            flops=elements * 6 * len(vecs), bytes_accessed=elements * 4, transcendentals=0
        ),
    )(idx, tiles, *vecs)


def operator_sums(tile_ref, acc_ref, row):
    def one(g, carry):
        start = pl.multiple_of(g * BS, BS)
        for lo in range(0, BS, CHUNK):
            acc = [jnp.zeros((CHUNK, BS), jnp.float32) for _ in range(3)]
            for t in range(9):
                tile = tile_ref[g * 9 + t, lo : lo + CHUNK, :]
                for k in range(3):
                    part = row(g * 9 + t, k)
                    acc[k] = acc[k] + tile * (part * 8.0 if t == 0 else part)
            for k in range(3):
                acc_ref[k, pl.ds(start + lo, CHUNK), :] = acc[k]
        return carry

    lax.fori_loop(0, 16, one, 0)
    return lane_sums(16, acc_ref)


OPERATOR_SCRATCH = [
    pltpu.VMEM((144, BS, BS), jnp.float32),
    pltpu.VMEM((3, 16 * BS, BS), jnp.float32),
    pltpu.SemaphoreType.DMA,
]


def spread_kernel(want_ref, sens_ref, tile_hbm, own_ref, image_ref, near_ref, tile_ref, acc_ref, sem):
    copy = pltpu.make_async_copy(tile_hbm, tile_ref, sem)
    copy.start()
    ids = jnp.sum(sens_ref[:, 48, :].reshape(16, 8, BS), axis=1)
    want = want_ref[...]
    acc = [jnp.zeros((144, BS), jnp.float32) for _ in range(3)]
    for g in range(16):
        hot = (want == ids[g : g + 1, :]).astype(jnp.bfloat16)
        for k in range(3):
            part = sens_ref[8 * g : 8 * g + 8, 16 * k : 16 * k + 16, :].reshape(BS, BS)
            high = part.astype(jnp.bfloat16)
            rest = (part - high.astype(jnp.float32)).astype(jnp.bfloat16)
            acc[k] = acc[k] + jnp.dot(hot, high, preferred_element_type=jnp.float32)
            acc[k] = acc[k] + jnp.dot(hot, rest, preferred_element_type=jnp.float32)
    for k in range(3):
        near_ref[144 * k : 144 * k + 144] = acc[k]
    copy.wait()
    sums = operator_sums(tile_ref, acc_ref, lambda n, k: near_ref[pl.ds(n + 144 * k, 1), :])
    for k in range(3):
        for g in range(16):
            own = near_ref[144 * k + 9 * g : 144 * k + 9 * g + 1, :]
            own_ref[16 * k + g : 16 * k + g + 1, :] = own
            image_ref[16 * k + g : 16 * k + g + 1, :] = own + sums[k][g] * COUPLING


def spread_and_apply(want, sens, tiles):
    return pl.pallas_call(
        spread_kernel,
        out_shape=[jax.ShapeDtypeStruct((48, BS), jnp.float32)] * 2,
        in_specs=[
            pl.BlockSpec(memory_space=pltpu.VMEM),
            pl.BlockSpec(memory_space=pltpu.VMEM),
            pl.BlockSpec(memory_space=pl.ANY),
        ],
        scratch_shapes=[pltpu.VMEM((3 * 144, BS), jnp.float32)] + OPERATOR_SCRATCH,
        compiler_params=pltpu.CompilerParams(vmem_limit_bytes=VMEM),
        cost_estimate=pl.CostEstimate(
            flops=144 * 2048 * 384 * 4, bytes_accessed=tiles.size * 4, transcendentals=0
        ),
    )(want, sens, tiles)


def spread_all_kernel(sens_ref, out_ref, cut_ref, ids_ref):
    step = pl.program_id(0)

    @pl.when(step == 0)
    def _():
        ids_ref[...] = jnp.sum(sens_ref[:, 48, :].reshape(16, 8, BS), axis=1)
        for k in range(3):
            part = sens_ref[:, 16 * k : 16 * k + 16, :].reshape(2048, BS)
            high = part.astype(jnp.bfloat16)
            cut_ref[0, :, k * BS : (k + 1) * BS] = high
            cut_ref[1, :, k * BS : (k + 1) * BS] = (part - high.astype(jnp.float32)).astype(jnp.bfloat16)

    want = (lax.broadcasted_iota(jnp.int32, (256, BS), 0) + step * 256).astype(jnp.float32)
    hot = jnp.concatenate(
        [(want == ids_ref[g : g + 1, :]).astype(jnp.bfloat16) for g in range(16)], axis=1
    )
    acc = jnp.dot(hot, cut_ref[0], preferred_element_type=jnp.float32)
    acc = acc + jnp.dot(hot, cut_ref[1], preferred_element_type=jnp.float32)
    for k in range(3):
        out_ref[:, 16 * k : 16 * k + 16, :] = acc[:, k * BS : (k + 1) * BS].reshape(16, 16, BS)


def spread_all(sens):
    return pl.pallas_call(
        spread_all_kernel,
        out_shape=jax.ShapeDtypeStruct((128, 48, BS), jnp.float32),
        grid=(8,),
        in_specs=[whole(sens.shape)],
        out_specs=pl.BlockSpec((16, 48, BS), lambda m: (m, 0, 0)),
        scratch_shapes=[
            pltpu.VMEM((2, 2048, 3 * BS), jnp.bfloat16),
            pltpu.VMEM((16, BS), jnp.float32),
        ],
        compiler_params=pltpu.CompilerParams(vmem_limit_bytes=VMEM),
        cost_estimate=pl.CostEstimate(
            flops=2048 * 2048 * 384 * 4, bytes_accessed=sens.size * 8, transcendentals=0
        ),
    )(sens)


def total_of(part):
    return jnp.sum(jnp.sum(part, axis=0, keepdims=True), axis=1, keepdims=True)


def step_kernel(idx_ref, f_ref, q_ref, tile_hbm, p_ref, coef_ref, dot_ref, tile_ref, acc_ref, sem):
    copy = pltpu.make_async_copy(tile_hbm, tile_ref, sem)
    copy.start()
    zeros = tuple(jnp.zeros((16, BS), jnp.float32) for _ in range(6))

    def at(d, k):
        return pl.ds(pl.multiple_of(d * 48 + 16 * k, 16), 16)

    def first(d, carry):
        out = []
        for k in range(3):
            f, q = f_ref[at(d, k), :], q_ref[at(d, k), :]
            out += [carry[2 * k] + f * f, carry[2 * k + 1] + f * q]
        return tuple(out)

    sums = lax.fori_loop(0, 128, first, zeros, unroll=4)
    now = [total_of(sums[2 * k]) for k in range(3)]
    alpha = [now[k] / total_of(sums[2 * k + 1]) for k in range(3)]

    def second(d, carry):
        out = []
        for k in range(3):
            r = f_ref[at(d, k), :] - alpha[k] * q_ref[at(d, k), :]
            p_ref[at(d, k), :] = r
            out.append(carry[k] + r * r)
        return tuple(out)

    sums = lax.fori_loop(0, 128, second, zeros[:3], unroll=4)
    later = [total_of(sums[k]) for k in range(3)]
    beta = [later[k] / now[k] for k in range(3)]

    def third(d, carry):
        for k in range(3):
            p_ref[at(d, k), :] = p_ref[at(d, k), :] + beta[k] * f_ref[at(d, k), :]
        return carry

    lax.fori_loop(0, 128, third, 0, unroll=4)
    rows = lax.broadcasted_iota(jnp.int32, (8, BS), 0)
    out = jnp.zeros((8, BS), jnp.float32)
    for k in range(3):
        out = jnp.where(rows == k, alpha[k], out)
        out = jnp.where(rows == 4 + k, later[k], out)
    coef_ref[...] = out
    copy.wait()
    sums = operator_sums(tile_ref, acc_ref, lambda n, k: p_ref[pl.ds(idx_ref[n] + 16 * k, 1), :])
    lanes = lax.broadcasted_iota(jnp.int32, (1, BS), 1)
    out = jnp.zeros((1, BS), jnp.float32)
    for k in range(3):
        total = jnp.zeros((1, BS), jnp.float32)
        for g in range(16):
            own = p_ref[pl.ds(idx_ref[9 * g] + 16 * k, 1), :]
            total = total + own * (own + sums[k][g] * COUPLING)
        out = jnp.where(lanes == k, jnp.sum(total, axis=1, keepdims=True), out)
    dot_ref[...] = out


def step_and_apply(idx, f, q, tiles):
    vmem = pl.BlockSpec(memory_space=pltpu.VMEM)
    return pl.pallas_call(
        step_kernel,
        out_shape=[
            jax.ShapeDtypeStruct(f.shape, jnp.float32),
            jax.ShapeDtypeStruct((8, BS), jnp.float32),
            jax.ShapeDtypeStruct((1, BS), jnp.float32),
        ],
        in_specs=[pl.BlockSpec(memory_space=pltpu.SMEM), vmem, vmem, pl.BlockSpec(memory_space=pl.ANY)],
        scratch_shapes=OPERATOR_SCRATCH,
        input_output_aliases={2: 0},
        compiler_params=pltpu.CompilerParams(vmem_limit_bytes=VMEM),
        cost_estimate=pl.CostEstimate(
            flops=f.size * 10 + tiles.size * 6, bytes_accessed=tiles.size * 8, transcendentals=0
        ),
    )(idx, f, q, tiles)


def over_ctl(x):
    size = lax.axis_size("ctl")
    return lax.all_to_all(jnp.broadcast_to(x[None], (size,) + x.shape), "ctl", 0, 0, tiled=True)


def over_vol(x):
    return lax.all_gather(x, "vol", axis=0, tiled=True)


def place(block):
    return (((block >> 4) & 7) * 16 + (block >> 7)) * 48 + (block & 15)


def slot(block):
    return (((block >> 4) & 7) * 16 + (block >> 7)) * 16 + (block & 15)


def padded(rows):
    return jnp.pad(rows.transpose(1, 0, 2), ((0, 0), (0, 5), (0, 0)))


def body(sensitivity, sens_ids, ctl_coords, partners, node_coords, node_tiles):
    vol, ctl = lax.axis_index("vol"), lax.axis_index("ctl")
    device = vol * 16 + ctl
    own_coords = lax.dynamic_slice_in_dim(ctl_coords.reshape(3, 128, BS), vol * 16, 16, 1)
    ids = slot(sens_ids).astype(jnp.float32)
    lanes = jnp.arange(BS) // 16 == device % 8
    id_row = jnp.where(lanes, jnp.tile(ids, 8), 0.0)[None]
    payload = jnp.concatenate(
        [
            own_coords.reshape(48, BS),
            sensitivity.reshape(48, BS),
            jnp.pad(id_row, ((0, 7), (0, 0))),
        ],
        axis=0,
    )
    near = over_ctl(payload)
    coords = over_vol(near[:, :48])
    sens = over_vol(near[:, 48:])
    coords_rows = coords.reshape(128 * 48, BS)

    own = ctl * 128 + vol * 16 + jnp.arange(16, dtype=jnp.int32)
    mates = lax.dynamic_slice_in_dim(partners, vol * 16, 16, 0)
    lists = jnp.concatenate([own[:, None], mates], axis=1).reshape(-1)
    op_at = place(lists)
    node_at = place(node_tiles.reshape(-1))

    (op_tiles,) = make_tiles(op_at, padded(own_coords), coords_rows, None, 9, 4)
    points = padded(node_coords.reshape(3, 64, BS))
    head_at, tail_at = node_at[: HEAD * 9], node_at[HEAD * 9 :]
    (head_tiles,) = make_tiles(head_at, points[:HEAD], coords_rows, None, 9, 8)
    sens, head_tiles = lax.optimization_barrier((sens, head_tiles))
    want = jnp.broadcast_to(slot(lists).astype(jnp.float32)[:, None], (144, BS))
    f_own, image = spread_and_apply(want, sens, op_tiles)
    sens, image = lax.optimization_barrier((sens, image))
    near_image = over_ctl(image)
    f_all = spread_all(sens)
    image_all = over_vol(near_image).reshape(128 * 48, BS)
    f_rows = f_all.reshape(128 * 48, BS)
    tail_tiles, tail_f = make_tiles(tail_at, points[HEAD:], coords_rows, f_rows, 9, 8)
    image_all, tail_f = lax.optimization_barrier((image_all, tail_f))
    p_rows, coef, dot_row = step_and_apply(op_at, f_rows, image_all, op_tiles)
    dot_rows = lax.all_to_all(
        jnp.broadcast_to(dot_row, (128, BS)), ("vol", "ctl"), 0, 0, tiled=True
    )
    (tail_p,) = apply_tiles(tail_at, tail_tiles, [p_rows], 9, 8)
    head_f, head_p = apply_tiles(head_at, head_tiles, [f_rows, p_rows], 9, 8)
    dots = jnp.sum(dot_rows, axis=0)[:3]

    alpha0 = coef[0:3, 0]
    alpha1 = coef[4:7, 0] / dots

    def mine(full):
        part = lax.dynamic_slice_in_dim(full.reshape(8, 16, 3, 16, BS), ctl, 1, 1)
        return part.reshape(8, 3, 16, BS).transpose(1, 0, 2, 3).reshape(3, 128, BS)

    def back(head, tail):
        return jnp.concatenate([head[:, :3], tail[:, :3]], axis=0).transpose(1, 0, 2)

    weights = alpha0[:, None, None] * mine(f_rows) + alpha1[:, None, None] * mine(p_rows)
    shift = NODE_SCALE * (
        alpha0[:, None, None] * back(head_f, tail_f) + alpha1[:, None, None] * back(head_p, tail_p)
    )
    return weights.reshape(3, -1), shift.reshape(3, -1)


def solution(mesh):
    placed = (
        P(None, ("vol", "ctl")),
        P(("vol", "ctl")),
        P(None, "ctl"),
        P("ctl", None),
        P(None, ("vol", "ctl")),
        P(("vol", "ctl"), None),
    )
    return jax.shard_map(
        body,
        mesh=mesh,
        in_specs=placed,
        out_specs=(P(None, "ctl"), P(None, ("vol", "ctl"))),
        check_vma=False,
    )
```

time: 260 us -> 226 us (0.87)
  Pallas kernels: 141 us -> 121 us
  waiting for transfers between devices: 45.5 us -> 33 us
  other arithmetic: 5.26 us -> 2.54 us
    all_gather x3, waiting for transfers between devices: 45.5 us -> 24.7 us  [over_vol(): return lax.all_gather(x, 'vol', axis=0, tiled=True)]
    pallas_call x2 -> x3, Pallas kernels: 66.9 us -> 56.8 us  [make_tiles(): pl.pallas_call(functools.partial(tiles_kernel, reach, group, with_vec), o...]
    pallas_call x5 -> x4, Pallas kernels: 60.1 us -> 50.6 us  [the longest x2 29.6 us: apply_tiles(): pl.pallas_call(functools.partial(apply_kernel, reach, group, len(vecs)),...]
    all_to_all x1, waiting for transfers between devices: 0.01 us -> 8.22 us  [body(): lax.all_to_all(jnp.broadcast_to(dot_row, (128, BS)), ('vol', 'ctl'), 0, 0...]
    slice x0 -> x11, local copies, waits for them, and re-layouts: none -> 4.18 us  [the longest x2 1.83 us: back(): head[:, :3]]
  transfers between devices with their start and end apart: 4 -> 4, of which waited for: 2 -> 3; matrix products, arithmetic and copies ran while one was open for 2% -> 3% of each run, Pallas kernels for 42% -> 31%
where the time goes in v2:
time: 226 us; the launch traced here: 225 us
  Pallas kernels  121 us (54%)
  blocking collectives  37.5 us (17%)
  waiting for transfers between devices  33 us (15%)
  between operations  14 us (6%)
  local copies, waits for them, and re-layouts  11.8 us (5%)
  starting transfers between devices  5.28 us (2%)
  other arithmetic  2.54 us (1%)
    pallas_call x3, Pallas kernels, make_tiles(): pl.pallas_call(functools.partial(tiles_kernel, reach, group, with_vec), o...  56.8 us
    all_to_all x2, blocking collectives, over_ctl(): lax.all_to_all(jnp.broadcast_to(x[None], (size,) + x.shape), 'ctl', 0, 0,...  37.5 us
    pallas_call x2, Pallas kernels, apply_tiles(): pl.pallas_call(functools.partial(apply_kernel, reach, group, len(vecs)),...  29.6 us
    all_gather x3, waiting for transfers between devices, over_vol(): return lax.all_gather(x, 'vol', axis=0, tiled=True)  24.7 us
    pallas_call x1, Pallas kernels, spread_all(): pl.pallas_call(spread_all_kernel, out_shape=jax.ShapeDtypeStruct((128, 48...  13.6 us
    pallas_call x1, Pallas kernels, step_and_apply(): pl.pallas_call(step_kernel, out_shape=[jax.ShapeDtypeStruct(f.shape, jnp....  11 us
    pallas_call x1, Pallas kernels, spread_and_apply(): pl.pallas_call(spread_kernel, out_shape=[jax.ShapeDtypeStruct((48, BS), j...  9.98 us
    all_to_all x1, waiting for transfers between devices, body(): lax.all_to_all(jnp.broadcast_to(dot_row, (128, BS)), ('vol', 'ctl'), 0, 0...  8.22 us
  transfers between devices with their start and end apart: 4, of which 3 were waited for; matrix products, arithmetic and copies ran while one was open for 3% of the time, Pallas kernels for 31%

profile of v2, /device:TPU:1, one launch (start us, length us, event | category | flops | bytes accessed | tf_op | source)
XLA Modules:
  0.0 225.1 jit_solution(16354912005767069036)
XLA Ops:
  7.3 0.7 add_convert_fusion.1
  8.1 0.8 reshape.156
  9.0 21.6 %all_to_all.16 = f32[16,104,128]{2,1,0:T(8,128)S(1)} all-to-all(f32[16,104,128]{2,1,0:T(8,128)S(1)} %broadcast_in_dim.13), channel_id=1, replica_groups=mesh['vol'=8,'ctl'=16] {'ctl'}, dimensions={0} | all-to-all | bytes 1703936 | tf_op jit(solution)/shard_map/all_to_all | solution.py:355
  30.6 0.8 slice.56
  31.4 0.8 slice.54
  32.5 0.7 reshape.176.idx_ref
  33.4 0.7 reshape.173.idx_ref
  34.2 0.6 pad.14.pts_ref
  34.9 0.7 pad_slice_fusion
  35.6 23.8 %all-gather.6.cloned.1.call-done = f32[128,48,128]{2,1,0:T(8,128)} async-done(((f32[16,48,128]{2,1,0:T(8,128)}), f32[128,48,128]{2,1,0:T(8,128)}) %all-gather.6.cloned.1.call-update) | async-done | bytes 3145744 | tf_op jit(solution)/shard_map/all_gather | solution.py:359
  59.4 11.5 %shard_map.78.tile_hbm = f32[144,128,128]{2,1,0:T(8,128)} custom-call(s32[144]{0:T(256)} %reshape.173.idx_ref, f32[16,8,128]{2,1,0:T(8,128)} %pad.14.pts_ref, f32[6144,128]{1,0:T(8,128)} %bitcast.50), custom_call_target="tpu_custom_call" | custom-call | flops 56623104 | bytes 9437184 | tf_op jit(solution)/shard_map/pallas_call | solution.py:104
  71.0 19.4 %shard_map.77.tile_ref = f32[288,128,128]{2,1,0:T(8,128)} custom-call(s32[288]{0:T(512)} %reshape.176.idx_ref, f32[32,8,128]{2,1,0:T(8,128)} %get-tuple-element.33.pts_ref, f32[6144,128]{1,0:T(8,128)} %bitcast.51), custom_call_target="tpu_custom_call" | custom-call | flops 113246208 | bytes 18874368 | tf_op jit(solution)/shard_map/pallas_call | solution.py:104
  90.3 0.9 all-gather.4.cloned.1.call-done.sens_ref
  91.2 0.7 broadcast_in_dim.14.want_ref
  91.9 10.0 %shard_map.79 = (f32[48,128]{1,0:T(8,128)}, f32[48,128]{1,0:T(8,128)}) custom-call(f32[144,128]{1,0:T(8,128)} %broadcast_in_dim.14.want_ref, f32[128,56,128]{2,1,0:T(8,128)} %all-gather.4.cloned.1.call-done.sens_ref, f32[144,128,128]{2,1,0:T(8,128)} %shard_map.78.tile_hbm), custom_call_target="tpu_custom_call" | custom-call | flops 452984832 | bytes 9437184 | tf_op jit(solution)/shard_map/pallas_call | solution.py:218
  101.9 0.8 broadcast_in_dim.15
  102.7 15.9 %all_to_all.17 = f32[16,48,128]{2,1,0:T(8,128)} all-to-all(f32[16,48,128]{2,1,0:T(8,128)S(1)} %broadcast_in_dim.15), channel_id=1, replica_groups=mesh['vol'=8,'ctl'=16] {'ctl'}, dimensions={0} | all-to-all | bytes 786432 | tf_op jit(solution)/shard_map/all_to_all | solution.py:355
  118.7 0.7 reshape.177.idx_ref
  119.4 13.6 %shard_map.80 = f32[128,48,128]{2,1,0:T(8,128)} custom-call(f32[128,56,128]{2,1,0:T(8,128)} %all-gather.4.cloned.1.call-done.sens_ref), custom_call_target="tpu_custom_call" | custom-call | flops 6442450944 | bytes 7340032 | tf_op jit(solution)/shard_map/pallas_call | solution.py:257
  133.0 26.0 %shard_map.81 = (f32[288,128,128]{2,1,0:T(8,128)}, f32[32,8,128]{2,1,0:T(8,128)}) custom-call(s32[288]{0:T(512)} %reshape.177.idx_ref, f32[32,8,128]{2,1,0:T(8,128)} %get-tuple-element.32.pts_ref, f32[6144,128]{1,0:T(8,128)} %bitcast.52, f32[6144,128]{1,0:T(8,128)} %bitcast.46), custom_call_target="tpu_custom_call" | custom-call | flops 113246208 | bytes 18874368 | tf_op jit(solution)/shard_map/pallas_call | solution.py:104
  158.9 11.0 %shard_map.82 = (f32[6144,128]{1,0:T(8,128)}, f32[8,128]{1,0:T(8,128)}, f32[1,128]{1,0:T(1,128)}) custom-call(s32[144]{0:T(256)} %reshape.173.idx_ref, f32[6144,128]{1,0:T(8,128)} %bitcast.47, f32[6144,128]{1,0:T(8,128)} %bitcast.44, f32[144,128,128]{2,1,0:T(8,128)} %shard_map.78.tile_hbm), custom_call_target="tpu_custom_call", output_to_operand_aliasing={{0}: (2, {})} | custom-call | flops 22020096 | bytes 18874368 | tf_op jit(solution)/shard_map/pallas_call | solution.py:336
  170.0 12.0 %shard_map.84 = f32[32,8,128]{2,1,0:T(8,128)} custom-call(s32[288]{0:T(512)} %reshape.177.idx_ref, f32[288,128,128]{2,1,0:T(8,128)} %get-tuple-element.29.tile_ref, f32[6144,128]{1,0:T(8,128)} %get-tuple-element.24.refs_1_.refs_0_), custom_call_target="tpu_custom_call" | custom-call | flops 28311552 | bytes 18874368 | tf_op jit(solution)/shard_map/pallas_call | solution.py:149
  182.0 17.6 %shard_map.83 = (f32[32,8,128]{2,1,0:T(8,128)}, f32[32,8,128]{2,1,0:T(8,128)}) custom-call(s32[288]{0:T(512)} %reshape.176.idx_ref, f32[288,128,128]{2,1,0:T(8,128)} %shard_map.77.tile_ref, f32[6144,128]{1,0:T(8,128)} %bitcast.48, f32[6144,128]{1,0:T(8,128)} %get-tuple-element.24.refs_1_.refs_0_), custom_call_target="tpu_custom_call" | custom-call | flops 56623104 | bytes 18874368 | tf_op jit(solution)/shard_map/pallas_call | solution.py:149
  199.6 0.9 slice.48
  200.5 0.9 slice.50
  201.4 0.7 broadcast_in_dim.16
  202.1 5.2 %all-to-all-start.2 = ((f32[128,1,128]{2,1,0:T(1,128)}), f32[128,1,128]{2,1,0:T(1,128)S(1)}, u32[]{:S(2)}, u32[]{:S(2)}) async-start(f32[128,1,128]{2,1,0:T(1,128)} %broadcast_in_dim.16), calls=%async_computation.2 | async-start | bytes 131072 | tf_op jit(solution)/shard_map/all_to_all | solution.py:415
  207.3 1.1 dynamic-slice_bitcast_fusion
  208.4 0.1 slice_reduce_fusion.1
  208.6 8.2 %all-to-all-done.2 = f32[128,1,128]{2,1,0:T(1,128)S(1)} async-done(((f32[128,1,128]{2,1,0:T(1,128)}), f32[128,1,128]{2,1,0:T(1,128)S(1)}, u32[]{:S(2)}, u32[]{:S(2)}) %all-to-all-start.2) | async-done | bytes 65568 | tf_op jit(solution)/shard_map/all_to_all | solution.py:415
  216.8 1.0 fusion
  217.8 0.8 fusion.3
  (46 shorter events, 1.1 us)
Async XLA Ops:
  7.2 1.0 copy-start
  7.2 25.2 %copy-start.3 = (s32[64,9]{0,1:T(8,128)S(1)}, s32[64,9]{0,1:T(8,128)}, u32[]{:S(2)}) copy-start(s32[64,9]{0,1:T(8,128)} %param.11) | copy-start | bytes 6916
  7.2 26.0 %copy-start.5 = (s32[128,8]{0,1:T(8,128)S(1)}, s32[128,8]{0,1:T(8,128)}, u32[]{:S(2)}) copy-start(s32[128,8]{0,1:T(8,128)} %param.9) | copy-start | bytes 12292
  7.2 27.7 %copy-start.1 = (f32[3,8192]{1,0:T(4,128)S(1)}, f32[3,8192]{1,0:T(4,128)}, u32[]{:S(2)}) copy-start(f32[3,8192]{1,0:T(4,128)} %param.10) | copy-start | bytes 294916
  7.2 52.2 %all-gather.6.cloned.1.call-start = ((), (), s32[]{:S(2)}) async-start(), calls=%async_computation.4 | async-start | bytes 3538944 | tf_op jit(solution)/shard_map/all_gather | solution.py:359
  31.4 59.8 %all-gather.4.cloned.1.call-start = ((), (), s32[]{:S(2)}) async-start(), calls=%async_computation.3 | async-start | bytes 4128768 | tf_op jit(solution)/shard_map/all_gather | solution.py:359
  32.3 126.7 %all-gather.8.cloned.1.call-start = ((), (), s32[]{:S(2)}) async-start(), calls=%async_computation.5 | async-start | bytes 3538944 | tf_op jit(solution)/shard_map/all_gather | solution.py:359
  182.0 19.4 %copy-start.6 = (f32[1,128]{1,0:T(1,128)S(1)}, f32[1,128]{1,0:T(1,128)}, u32[]{:S(2)}) copy-start(f32[1,128]{1,0:T(1,128)} %get-tuple-element.23) | copy-start | bytes 1540
  182.0 25.3 %copy-start.2 = (f32[32,8,128]{2,1,0:T(8,128)S(1)}, f32[32,8,128]{2,1,0:T(8,128)}, u32[]{:S(2)}) copy-start(f32[32,8,128]{2,1,0:T(8,128)} %get-tuple-element.27) | copy-start | bytes 393220
  182.0 26.4 %copy-start.4 = (f32[8,128]{1,0:T(8,128)S(1)}, f32[8,128]{1,0:T(8,128)}, u32[]{:S(2)}) copy-start(f32[8,128]{1,0:T(8,128)} %get-tuple-element.22) | copy-start | bytes 12292
  182.0 35.8 %slice-start = ((f32[32,8,128]{2,1,0:T(8,128)}), f32[32,3,128]{2,1,0:T(4,128)S(1)}, s32[]{:S(2)}) async-start(f32[32,8,128]{2,1,0:T(8,128)} %shard_map.84), calls=%async_computation.6 | async-start | bytes 131072 | tf_op jit(solution)/shard_map/slice | solution.py:430
  202.1 14.7 %all-to-all-start.2 = ((f32[128,1,128]{2,1,0:T(1,128)}), f32[128,1,128]{2,1,0:T(1,128)S(1)}, u32[]{:S(2)}, u32[]{:S(2)}) async-start(f32[128,1,128]{2,1,0:T(1,128)} %broadcast_in_dim.16), calls=%async_computation.2 | async-start | bytes 131072 | tf_op jit(solution)/shard_map/all_to_all | solution.py:415
Sparse Core Ops, SparseCore 0:
  31.5 27.8 all-gather.5
  61.1 30.0 all-gather.3
  118.7 25.2 all-gather.7

commit v3 on v2

--- a/solution.py
+++ b/solution.py
@@ -48,11 +48,8 @@
         sum_ref[g] = out
 
 
-def tiles_kernel(reach, group, with_vec, idx_ref, pts_ref, ctl_ref, *refs):
-    if with_vec:
-        vec_ref, tile_ref, sum_ref, cols_ref, acc_ref = refs
-    else:
-        tile_ref, cols_ref = refs
+def tiles_kernel(reach, group, idx_ref, pts_ref, ctl_ref, *refs):
+    tile_ref, cols_ref = refs[-2:]
     step = pl.program_id(0)
     for g in range(group):
         cols_ref[g] = jnp.transpose(pts_ref[g])
@@ -60,8 +57,10 @@
     def one(g, carry):
         base = (step * group + g) * reach
         for lo in range(0, BS, CHUNK):
-            own = [jnp.broadcast_to(cols_ref[g, lo : lo + CHUNK, k : k + 1], (CHUNK, BS)) for k in range(3)]
-            acc = [jnp.zeros((CHUNK, BS), jnp.float32) for _ in range(3)]
+            own = [
+                jnp.broadcast_to(cols_ref[g, lo : lo + CHUNK, k : k + 1], (CHUNK, BS))
+                for k in range(3)
+            ]
             for t in range(reach):
                 at = idx_ref[base + t]
                 dist = None
@@ -73,44 +72,34 @@
                 sq = inner * inner
                 tile = (sq * sq) * (4.0 * ratio + 1.0)
                 tile_ref[g * reach + t, lo : lo + CHUNK, :] = tile
-                if with_vec:
-                    for k in range(3):
-                        acc[k] = acc[k] + tile * vec_ref[pl.ds(at + 16 * k, 1), :]
-            if with_vec:
-                for k in range(3):
-                    acc_ref[k, pl.ds(pl.multiple_of(g * BS, BS) + lo, CHUNK), :] = acc[k]
         return carry
 
     lax.fori_loop(0, group, one, 0)
-    if with_vec:
-        store_sums(group, acc_ref, sum_ref)
-
-
-def make_tiles(idx, pts, ctl, vec, reach, group):
-    count = pts.shape[0]
-    with_vec = vec is not None
-    out_shape = [jax.ShapeDtypeStruct((count * reach, BS, BS), jnp.float32)]
-    out_specs = [pl.BlockSpec((group * reach, BS, BS), lambda m, *_: (m, 0, 0))]
-    scratch = [pltpu.VMEM((group, BS, 8), jnp.float32)]
+
+
+def make_tiles(idx, pts, ctl, reach, group, count=None, skip=0, into=None):
+    here = pts.shape[0]
+    count = count or here
+    first = skip // group
     operands = [pts, ctl]
     in_specs = [pl.BlockSpec((group, 8, BS), lambda m, *_: (m, 0, 0)), whole(ctl.shape)]
-    if with_vec:
-        out_shape.append(jax.ShapeDtypeStruct((count, 8, BS), jnp.float32))
-        out_specs.append(pl.BlockSpec((group, 8, BS), lambda m, *_: (m, 0, 0)))
-        scratch.append(pltpu.VMEM((3, group * BS, BS), jnp.float32))
-        operands.append(vec)
-        in_specs.append(whole(vec.shape))
-    elements = count * reach * BS * BS
+    alias = {}
+    if into is not None:
+        operands.append(into)
+        in_specs.append(pl.BlockSpec(memory_space=pl.ANY))
+        alias = {3: 0}
+    elements = here * reach * BS * BS
     return pl.pallas_call(
-        functools.partial(tiles_kernel, reach, group, with_vec),
-        out_shape=out_shape,
+        functools.partial(tiles_kernel, reach, group),
+        out_shape=jax.ShapeDtypeStruct((count * reach, BS, BS), jnp.float32),
         grid_spec=pltpu.PrefetchScalarGridSpec(
             num_scalar_prefetch=1,
-            grid=(count // group,),
+            grid=(here // group,),
             in_specs=in_specs,
-            out_specs=out_specs,
-            scratch_shapes=scratch,
-        ),
+            out_specs=pl.BlockSpec((group * reach, BS, BS), lambda m, *_: (m + first, 0, 0)),
+            scratch_shapes=[pltpu.VMEM((group, BS, 8), jnp.float32)],
+        ),
+        input_output_aliases=alias,
         compiler_params=pltpu.CompilerParams(vmem_limit_bytes=VMEM),
         cost_estimate=pl.CostEstimate(
             flops=elements * 24, bytes_accessed=elements * 4, transcendentals=elements
@@ -350,9 +339,12 @@
     )(idx, f, q, tiles)
 
 
+def copies(x):
+    return jnp.broadcast_to(x[None], (lax.axis_size("ctl"),) + x.shape)
+
+
 def over_ctl(x):
-    size = lax.axis_size("ctl")
-    return lax.all_to_all(jnp.broadcast_to(x[None], (size,) + x.shape), "ctl", 0, 0, tiled=True)
+    return lax.all_to_all(x, "ctl", 0, 0, tiled=True)
 
 
 def over_vol(x):
@@ -386,7 +378,7 @@
         ],
         axis=0,
     )
-    near = over_ctl(payload)
+    near = over_ctl(copies(payload))
     coords = over_vol(near[:, :48])
     sens = over_vol(near[:, 48:])
     coords_rows = coords.reshape(128 * 48, BS)
@@ -397,41 +389,43 @@
     op_at = place(lists)
     node_at = place(node_tiles.reshape(-1))
 
-    (op_tiles,) = make_tiles(op_at, padded(own_coords), coords_rows, None, 9, 4)
+    op_tiles = make_tiles(op_at, padded(own_coords), coords_rows, 9, 4)
     points = padded(node_coords.reshape(3, 64, BS))
     head_at, tail_at = node_at[: HEAD * 9], node_at[HEAD * 9 :]
-    (head_tiles,) = make_tiles(head_at, points[:HEAD], coords_rows, None, 9, 8)
-    sens, head_tiles = lax.optimization_barrier((sens, head_tiles))
+    tiles = make_tiles(head_at, points[:HEAD], coords_rows, 9, 8, count=64)
+    sens, tiles = lax.optimization_barrier((sens, tiles))
     want = jnp.broadcast_to(slot(lists).astype(jnp.float32)[:, None], (144, BS))
     f_own, image = spread_and_apply(want, sens, op_tiles)
-    sens, image = lax.optimization_barrier((sens, image))
+    image, sens = lax.optimization_barrier((copies(image), sens))
     near_image = over_ctl(image)
     f_all = spread_all(sens)
+    near_image, f_all = lax.optimization_barrier((near_image, f_all))
     image_all = over_vol(near_image).reshape(128 * 48, BS)
     f_rows = f_all.reshape(128 * 48, BS)
-    tail_tiles, tail_f = make_tiles(tail_at, points[HEAD:], coords_rows, f_rows, 9, 8)
-    image_all, tail_f = lax.optimization_barrier((image_all, tail_f))
+    tiles = make_tiles(tail_at, points[HEAD:], coords_rows, 9, 8, 64, HEAD, tiles)
+    image_all, tiles = lax.optimization_barrier((image_all, tiles))
     p_rows, coef, dot_row = step_and_apply(op_at, f_rows, image_all, op_tiles)
-    dot_rows = lax.all_to_all(
-        jnp.broadcast_to(dot_row, (128, BS)), ("vol", "ctl"), 0, 0, tiled=True
-    )
-    (tail_p,) = apply_tiles(tail_at, tail_tiles, [p_rows], 9, 8)
-    head_f, head_p = apply_tiles(head_at, head_tiles, [f_rows, p_rows], 9, 8)
-    dots = jnp.sum(dot_rows, axis=0)[:3]
-
-    alpha0 = coef[0:3, 0]
-    alpha1 = coef[4:7, 0] / dots
 
     def mine(full):
         part = lax.dynamic_slice_in_dim(full.reshape(8, 16, 3, 16, BS), ctl, 1, 1)
         return part.reshape(8, 3, 16, BS).transpose(1, 0, 2, 3).reshape(3, 128, BS)
 
-    def back(head, tail):
-        return jnp.concatenate([head[:, :3], tail[:, :3]], axis=0).transpose(1, 0, 2)
-
-    weights = alpha0[:, None, None] * mine(f_rows) + alpha1[:, None, None] * mine(p_rows)
+    f_mine, p_mine = mine(f_rows), mine(p_rows)
+    alpha0 = coef[0:3, 0]
+    dot_rows, p_rows, f_mine, p_mine = lax.optimization_barrier(
+        (jnp.broadcast_to(dot_row[None], (128, 8, BS)), p_rows, f_mine, p_mine)
+    )
+    dot_rows = lax.all_to_all(dot_rows, ("vol", "ctl"), 0, 0, tiled=True)
+    node_f, node_p = apply_tiles(node_at, tiles, [f_rows, p_rows], 9, 8)
+    dot_rows, node_f, node_p = lax.optimization_barrier((dot_rows, node_f, node_p))
+    alpha1 = coef[4:7, 0] / jnp.sum(dot_rows[:, 0], axis=0)[:3]
+
+    def back(sums):
+        return sums[:, :3].transpose(1, 0, 2)
+
+    weights = alpha0[:, None, None] * f_mine + alpha1[:, None, None] * p_mine
     shift = NODE_SCALE * (
-        alpha0[:, None, None] * back(head_f, tail_f) + alpha1[:, None, None] * back(head_p, tail_p)
+        alpha0[:, None, None] * back(node_f) + alpha1[:, None, None] * back(node_p)
     )
     return weights.reshape(3, -1), shift.reshape(3, -1)
 

time: 226 us -> 215 us (0.951)
  blocking collectives: 37.5 us -> 21.6 us
  starting transfers between devices: 5.28 us -> 14.4 us
  Pallas kernels: 121 us -> 114 us
    all_to_all x2 -> x1, blocking collectives: 37.5 us -> 21.6 us  [over_ctl(): return lax.all_to_all(x, 'ctl', 0, 0, tiled=True)]
    all_to_all x1 -> x2, starting transfers between devices: 5.16 us -> 14.3 us  [the longest x1 7.76 us: body(): dot_rows = lax.all_to_all(dot_rows, ('vol', 'ctl'), 0, 0, tiled=True)]
    all_gather x3, waiting for transfers between devices: 24.7 us -> 33.2 us  [over_vol(): return lax.all_gather(x, 'vol', axis=0, tiled=True)]
    all_to_all x1 -> x2, waiting for transfers between devices: 8.22 us -> 0.01 us  [the longest x1 0.01 us: over_ctl(): return lax.all_to_all(x, 'ctl', 0, 0, tiled=True)]
    pallas_call x3, Pallas kernels: 56.8 us -> 50.3 us  [make_tiles(): pl.pallas_call(functools.partial(tiles_kernel, reach, group), out_shape=j...]
    pallas_call x2 -> x1, Pallas kernels: 29.6 us -> 29.4 us  [apply_tiles(): pl.pallas_call(functools.partial(apply_kernel, reach, group, len(vecs)),...]
  transfers between devices with their start and end apart: 4 -> 5, of which waited for: 3 -> 3; matrix products, arithmetic and copies ran while one was open for 3% -> 3% of each run, Pallas kernels for 31% -> 44%
where the time goes in v3:
time: 215 us; the launch traced here: 214 us
  Pallas kernels  114 us (53%)
  waiting for transfers between devices  33.2 us (15%)
  blocking collectives  21.6 us (10%)
  starting transfers between devices  14.4 us (7%)
  local copies, waits for them, and re-layouts  13.9 us (6%)
  between operations  13.9 us (6%)
  other arithmetic  2.71 us (1%)
    pallas_call x3, Pallas kernels, make_tiles(): pl.pallas_call(functools.partial(tiles_kernel, reach, group), out_shape=j...  50.3 us
    all_gather x3, waiting for transfers between devices, over_vol(): return lax.all_gather(x, 'vol', axis=0, tiled=True)  33.2 us
    pallas_call x1, Pallas kernels, apply_tiles(): pl.pallas_call(functools.partial(apply_kernel, reach, group, len(vecs)),...  29.4 us
    all_to_all x1, blocking collectives, over_ctl(): return lax.all_to_all(x, 'ctl', 0, 0, tiled=True)  21.6 us
    pallas_call x1, Pallas kernels, spread_all(): pl.pallas_call(spread_all_kernel, out_shape=jax.ShapeDtypeStruct((128, 48...  13.6 us
    pallas_call x1, Pallas kernels, step_and_apply(): pl.pallas_call(step_kernel, out_shape=[jax.ShapeDtypeStruct(f.shape, jnp....  11 us
    pallas_call x1, Pallas kernels, spread_and_apply(): pl.pallas_call(spread_kernel, out_shape=[jax.ShapeDtypeStruct((48, BS), j...  9.98 us
    all_to_all x1, starting transfers between devices, body(): dot_rows = lax.all_to_all(dot_rows, ('vol', 'ctl'), 0, 0, tiled=True)  7.76 us
  transfers between devices with their start and end apart: 5, of which 3 were waited for; matrix products, arithmetic and copies ran while one was open for 3% of the time, Pallas kernels for 44%

profile of v3, /device:TPU:1, one launch (start us, length us, event | category | flops | bytes accessed | tf_op | source)
XLA Modules:
  0.0 214.1 jit_solution(5208606935015432108)
XLA Ops:
  7.3 0.7 add_convert_fusion.1
  8.1 0.8 reshape.151
  9.0 21.6 %all_to_all.15 = f32[16,104,128]{2,1,0:T(8,128)S(1)} all-to-all(f32[16,104,128]{2,1,0:T(8,128)S(1)} %broadcast_in_dim.16), channel_id=1, replica_groups=mesh['vol'=8,'ctl'=16] {'ctl'}, dimensions={0} | all-to-all | bytes 1703936 | tf_op jit(solution)/shard_map/all_to_all | solution.py:347
  30.6 0.8 slice.52
  31.4 0.8 slice.50
  32.4 0.6 reshape.172.idx_ref
  33.3 0.7 reshape.169.idx_ref
  34.1 0.6 pad.14.pts_ref
  34.8 0.7 pad_slice_fusion
  35.5 24.0 %all-gather.6.cloned.1.call-done = f32[128,48,128]{2,1,0:T(8,128)} async-done(((f32[16,48,128]{2,1,0:T(8,128)}), f32[128,48,128]{2,1,0:T(8,128)}) %all-gather.6.cloned.1.call-update) | async-done | bytes 3145744 | tf_op jit(solution)/shard_map/all_gather | solution.py:351
  59.4 11.5 %shard_map.78.tile_hbm = f32[144,128,128]{2,1,0:T(8,128)} custom-call(s32[144]{0:T(256)} %reshape.169.idx_ref, f32[16,8,128]{2,1,0:T(8,128)} %pad.14.pts_ref, f32[6144,128]{1,0:T(8,128)} %bitcast.39), custom_call_target="tpu_custom_call" | custom-call | flops 56623104 | bytes 9437184 | tf_op jit(solution)/shard_map/pallas_call | solution.py:92
  71.0 19.4 %shard_map.77.refs_0_ = f32[576,128,128]{2,1,0:T(8,128)} custom-call(s32[288]{0:T(512)} %reshape.172.idx_ref, f32[32,8,128]{2,1,0:T(8,128)} %get-tuple-element.47.pts_ref, f32[6144,128]{1,0:T(8,128)} %bitcast.40), custom_call_target="tpu_custom_call" | custom-call | flops 113246208 | bytes 18874368 | tf_op jit(solution)/shard_map/pallas_call | solution.py:92
  90.3 0.9 all-gather.4.cloned.1.call-done.sens_ref
  91.2 0.7 broadcast_in_dim.14.want_ref
  91.9 10.0 %shard_map.79 = (f32[48,128]{1,0:T(8,128)}, f32[48,128]{1,0:T(8,128)}) custom-call(f32[144,128]{1,0:T(8,128)} %broadcast_in_dim.14.want_ref, f32[128,56,128]{2,1,0:T(8,128)} %all-gather.4.cloned.1.call-done.sens_ref, f32[144,128,128]{2,1,0:T(8,128)} %shard_map.78.tile_hbm), custom_call_target="tpu_custom_call" | custom-call | flops 452984832 | bytes 9437184 | tf_op jit(solution)/shard_map/pallas_call | solution.py:207
  101.9 1.5 broadcast_in_dim.17
  103.4 6.5 %all-to-all-start.1 = ((f32[16,48,128]{2,1,0:T(8,128)}), f32[16,48,128]{2,1,0:T(8,128)S(1)}, u32[]{:S(2)}, u32[]{:S(2)}) async-start(f32[16,48,128]{2,1,0:T(8,128)} %broadcast_in_dim.17), calls=%async_computation.1 | async-start | bytes 786432 | tf_op jit(solution)/shard_map/all_to_all | solution.py:347
  110.0 13.6 %shard_map.80 = f32[128,48,128]{2,1,0:T(8,128)} custom-call(f32[128,56,128]{2,1,0:T(8,128)} %all-gather.4.cloned.1.call-done.sens_ref), custom_call_target="tpu_custom_call" | custom-call | flops 6442450944 | bytes 7340032 | tf_op jit(solution)/shard_map/pallas_call | solution.py:246
  123.6 0.8 copy-done.2
  124.4 0.7 reshape.173.idx_ref
  125.1 19.5 %shard_map.81.tile_ref = f32[576,128,128]{2,1,0:T(8,128)} custom-call(s32[288]{0:T(512)} %reshape.173.idx_ref, f32[32,8,128]{2,1,0:T(8,128)} %get-tuple-element.46.pts_ref, f32[6144,128]{1,0:T(8,128)} %bitcast.41, f32[576,128,128]{2,1,0:T(8,128)} %shard_map.77.refs_0_), custom_call_target="tpu_custom_call", output_to_operand_aliasing={{}: (3, {})} | custom-call | flops 113246208 | bytes 18874368 | tf_op jit(solution)/shard_map/pallas_call | solution.py:92
  144.6 8.3 %all-gather.8.cloned.1.call-done = f32[128,48,128]{2,1,0:T(8,128)} async-done(((f32[16,48,128]{2,1,0:T(8,128)}), f32[128,48,128]{2,1,0:T(8,128)}) %all-gather.8.cloned.1.call-update) | async-done | bytes 3145744 | tf_op jit(solution)/shard_map/all_gather | solution.py:351
  152.9 11.0 %shard_map.82 = (f32[6144,128]{1,0:T(8,128)}, f32[8,128]{1,0:T(8,128)}, f32[1,128]{1,0:T(1,128)}) custom-call(s32[144]{0:T(256)} %reshape.169.idx_ref, f32[6144,128]{1,0:T(8,128)} %bitcast.42, f32[6144,128]{1,0:T(8,128)} %bitcast.45, f32[144,128,128]{2,1,0:T(8,128)} %shard_map.78.tile_hbm), custom_call_target="tpu_custom_call", output_to_operand_aliasing={{0}: (2, {})} | custom-call | flops 22020096 | bytes 18874368 | tf_op jit(solution)/shard_map/pallas_call | solution.py:325
  163.9 1.1 dynamic-slice_bitcast_fusion
  165.1 1.5 broadcast_in_dim.19
  166.5 7.8 %all-to-all-start.2 = ((f32[128,8,128]{2,1,0:T(8,128)}), f32[128,8,128]{2,1,0:T(8,128)S(1)}, u32[]{:S(2)}, u32[]{:S(2)}) async-start(f32[128,8,128]{2,1,0:T(8,128)} %broadcast_in_dim.19), calls=%async_computation.2 | async-start | bytes 1048576 | tf_op jit(solution)/shard_map/all_to_all | solution.py:418
  174.4 0.7 reshape.171.idx_ref
  175.1 29.4 %shard_map.83 = (f32[64,8,128]{2,1,0:T(8,128)}, f32[64,8,128]{2,1,0:T(8,128)}) custom-call(s32[576]{0:T(1024)} %reshape.171.idx_ref, f32[576,128,128]{2,1,0:T(8,128)} %shard_map.81.tile_ref, f32[6144,128]{1,0:T(8,128)} %bitcast.44, f32[6144,128]{1,0:T(8,128)} %get-tuple-element.37.refs_1_), custom_call_target="tpu_custom_call" | custom-call | flops 113246208 | bytes 37748736 | tf_op jit(solution)/shard_map/pallas_call | solution.py:138
  204.6 0.1 slice_reduce_fusion.1
  204.8 0.1 add_bitcast_fusion
  204.9 0.8 copy.63
  205.8 1.8 multiply_bitcast_fusion
  (45 shorter events, 1.2 us)
Async XLA Ops:
  7.2 1.0 copy-start
  7.2 25.1 %copy-start.4 = (s32[64,9]{0,1:T(8,128)S(1)}, s32[64,9]{0,1:T(8,128)}, u32[]{:S(2)}) copy-start(s32[64,9]{0,1:T(8,128)} %param.11) | copy-start | bytes 6916
  7.2 25.9 %copy-start.6 = (s32[128,8]{0,1:T(8,128)S(1)}, s32[128,8]{0,1:T(8,128)}, u32[]{:S(2)}) copy-start(s32[128,8]{0,1:T(8,128)} %param.9) | copy-start | bytes 12292
  7.2 27.6 %copy-start.3 = (f32[3,8192]{1,0:T(4,128)S(1)}, f32[3,8192]{1,0:T(4,128)}, u32[]{:S(2)}) copy-start(f32[3,8192]{1,0:T(4,128)} %param.10) | copy-start | bytes 294916
  7.2 52.2 %all-gather.6.cloned.1.call-start = ((), (), s32[]{:S(2)}) async-start(), calls=%async_computation.4 | async-start | bytes 3538944 | tf_op jit(solution)/shard_map/all_gather | solution.py:351
  31.4 59.8 %all-gather.4.cloned.1.call-start = ((), (), s32[]{:S(2)}) async-start(), calls=%async_computation.3 | async-start | bytes 4128768 | tf_op jit(solution)/shard_map/all_gather | solution.py:351
  103.4 20.2 %all-to-all-start.1 = ((f32[16,48,128]{2,1,0:T(8,128)}), f32[16,48,128]{2,1,0:T(8,128)S(1)}, u32[]{:S(2)}, u32[]{:S(2)}) async-start(f32[16,48,128]{2,1,0:T(8,128)} %broadcast_in_dim.17), calls=%async_computation.1 | async-start | bytes 786432 | tf_op jit(solution)/shard_map/all_to_all | solution.py:347
  109.9 43.0 %all-gather.8.cloned.1.call-start = ((), (), s32[]{:S(2)}) async-start(), calls=%async_computation.5 | async-start | bytes 3538944 | tf_op jit(solution)/shard_map/all_gather | solution.py:351
  123.6 0.8 copy-start.2
  166.5 38.2 %all-to-all-start.2 = ((f32[128,8,128]{2,1,0:T(8,128)}), f32[128,8,128]{2,1,0:T(8,128)S(1)}, u32[]{:S(2)}, u32[]{:S(2)}) async-start(f32[128,8,128]{2,1,0:T(8,128)} %broadcast_in_dim.19), calls=%async_computation.2 | async-start | bytes 1048576 | tf_op jit(solution)/shard_map/all_to_all | solution.py:418
  175.1 29.5 %copy-start.5 = (f32[8,128]{1,0:T(8,128)S(1)}, f32[8,128]{1,0:T(8,128)}, u32[]{:S(2)}) copy-start(f32[8,128]{1,0:T(8,128)} %get-tuple-element.31) | copy-start | bytes 12292
  175.1 32.4 %copy-start.1 = (f32[3,16384]{1,0:T(4,128)S(1)}, f32[3,16384]{1,0:T(4,128)}, u32[]{:S(2)}) copy-start(f32[3,16384]{1,0:T(4,128)} %param.8) | copy-start | bytes 589828
Sparse Core Ops, SparseCore 0:
  31.5 27.8 all-gather.5
  61.1 30.0 all-gather.3
  124.5 28.4 all-gather.7

commit v4 on v3

--- a/solution.py
+++ b/solution.py
@@ -12,7 +12,6 @@
 NODE_SCALE = 0.25
 VMEM = 56 * 1024 * 1024
 CHUNK = 32
-HEAD = 32
 
 
 def whole(shape):
@@ -48,8 +47,7 @@
         sum_ref[g] = out
 
 
-def tiles_kernel(reach, group, idx_ref, pts_ref, ctl_ref, *refs):
-    tile_ref, cols_ref = refs[-2:]
+def tiles_kernel(reach, group, idx_ref, pts_ref, ctl_ref, tile_ref, cols_ref):
     step = pl.program_id(0)
     for g in range(group):
         cols_ref[g] = jnp.transpose(pts_ref[g])
@@ -65,7 +63,7 @@
                 at = idx_ref[base + t]
                 dist = None
                 for k in range(3):
-                    gap = own[k] - ctl_ref[pl.ds(at + 16 * k, 1), :]
+                    gap = own[k] - ctl_ref[pl.ds(at + 64 * k, 1), :]
                     dist = gap * gap if dist is None else dist + gap * gap
                 ratio = dist * lax.rsqrt(jnp.maximum(dist, 1e-30))
                 inner = jnp.maximum(1.0 - ratio, 0.0)
@@ -77,34 +75,25 @@
     lax.fori_loop(0, group, one, 0)
 
 
-def make_tiles(idx, pts, ctl, reach, group, count=None, skip=0, into=None):
-    here = pts.shape[0]
-    count = count or here
-    first = skip // group
-    operands = [pts, ctl]
+def make_tiles(idx, pts, ctl, reach, group):
+    count = pts.shape[0]
     in_specs = [pl.BlockSpec((group, 8, BS), lambda m, *_: (m, 0, 0)), whole(ctl.shape)]
-    alias = {}
-    if into is not None:
-        operands.append(into)
-        in_specs.append(pl.BlockSpec(memory_space=pl.ANY))
-        alias = {3: 0}
-    elements = here * reach * BS * BS
+    elements = count * reach * BS * BS
     return pl.pallas_call(
         functools.partial(tiles_kernel, reach, group),
         out_shape=jax.ShapeDtypeStruct((count * reach, BS, BS), jnp.float32),
         grid_spec=pltpu.PrefetchScalarGridSpec(
             num_scalar_prefetch=1,
-            grid=(here // group,),
+            grid=(count // group,),
             in_specs=in_specs,
-            out_specs=pl.BlockSpec((group * reach, BS, BS), lambda m, *_: (m + first, 0, 0)),
+            out_specs=pl.BlockSpec((group * reach, BS, BS), lambda m, *_: (m, 0, 0)),
             scratch_shapes=[pltpu.VMEM((group, BS, 8), jnp.float32)],
         ),
-        input_output_aliases=alias,
         compiler_params=pltpu.CompilerParams(vmem_limit_bytes=VMEM),
         cost_estimate=pl.CostEstimate(
             flops=elements * 24, bytes_accessed=elements * 4, transcendentals=elements
         ),
-    )(idx, *operands)
+    )(idx, pts, ctl)
 
 
 def apply_kernel(reach, group, count, idx_ref, tile_ref, *refs):
@@ -366,43 +355,43 @@
 def body(sensitivity, sens_ids, ctl_coords, partners, node_coords, node_tiles):
     vol, ctl = lax.axis_index("vol"), lax.axis_index("ctl")
     device = vol * 16 + ctl
-    own_coords = lax.dynamic_slice_in_dim(ctl_coords.reshape(3, 128, BS), vol * 16, 16, 1)
+    blocks = ctl_coords.reshape(3, 128, BS)
+    own_coords = lax.dynamic_slice_in_dim(blocks, vol * 16, 16, 1)
     ids = slot(sens_ids).astype(jnp.float32)
     lanes = jnp.arange(BS) // 16 == device % 8
     id_row = jnp.where(lanes, jnp.tile(ids, 8), 0.0)[None]
     payload = jnp.concatenate(
-        [
-            own_coords.reshape(48, BS),
-            sensitivity.reshape(48, BS),
-            jnp.pad(id_row, ((0, 7), (0, 0))),
-        ],
-        axis=0,
-    )
-    near = over_ctl(copies(payload))
-    coords = over_vol(near[:, :48])
-    sens = over_vol(near[:, 48:])
-    coords_rows = coords.reshape(128 * 48, BS)
+        [sensitivity.reshape(48, BS), jnp.pad(id_row, ((0, 7), (0, 0)))], axis=0
+    )
+    core = vol % 2
+    half = lax.dynamic_slice_in_dim(blocks, core * 64, 64, 1).reshape(192, BS)
+    near, half = lax.optimization_barrier((over_ctl(copies(payload)), copies(half)))
+    sens = over_vol(near)
+    half = over_ctl(half)
+    other = lax.ppermute(half, "vol", [(i, i ^ 1) for i in range(lax.axis_size("vol"))])
+    coords_rows = jnp.concatenate([half, other], axis=0).reshape(2 * 16 * 192, BS)
 
     own = ctl * 128 + vol * 16 + jnp.arange(16, dtype=jnp.int32)
     mates = lax.dynamic_slice_in_dim(partners, vol * 16, 16, 0)
     lists = jnp.concatenate([own[:, None], mates], axis=1).reshape(-1)
+    node_lists = node_tiles.reshape(-1)
     op_at = place(lists)
-    node_at = place(node_tiles.reshape(-1))
-
-    op_tiles = make_tiles(op_at, padded(own_coords), coords_rows, 9, 4)
+    node_at = place(node_lists)
+
+    def coord_at(block):
+        return ((((block >> 6) & 1) ^ core) * 16 + (block >> 7)) * 192 + (block & 63)
+
+    op_tiles = make_tiles(coord_at(lists), padded(own_coords), coords_rows, 9, 4)
     points = padded(node_coords.reshape(3, 64, BS))
-    head_at, tail_at = node_at[: HEAD * 9], node_at[HEAD * 9 :]
-    tiles = make_tiles(head_at, points[:HEAD], coords_rows, 9, 8, count=64)
-    sens, tiles = lax.optimization_barrier((sens, tiles))
     want = jnp.broadcast_to(slot(lists).astype(jnp.float32)[:, None], (144, BS))
     f_own, image = spread_and_apply(want, sens, op_tiles)
     image, sens = lax.optimization_barrier((copies(image), sens))
     near_image = over_ctl(image)
     f_all = spread_all(sens)
-    near_image, f_all = lax.optimization_barrier((near_image, f_all))
+    near_image, f_all, coords_rows = lax.optimization_barrier((near_image, f_all, coords_rows))
     image_all = over_vol(near_image).reshape(128 * 48, BS)
     f_rows = f_all.reshape(128 * 48, BS)
-    tiles = make_tiles(tail_at, points[HEAD:], coords_rows, 9, 8, 64, HEAD, tiles)
+    tiles = make_tiles(coord_at(node_lists), points, coords_rows, 9, 8)
     image_all, tiles = lax.optimization_barrier((image_all, tiles))
     p_rows, coef, dot_row = step_and_apply(op_at, f_rows, image_all, op_tiles)
 

time: 215 us -> 203 us (0.944)
  waiting for transfers between devices: 33.2 us -> 11.2 us
  starting transfers between devices: 14.4 us -> 24.6 us
  Pallas kernels: 114 us -> 110 us
  blocking collectives: 21.6 us -> 24.1 us
    all_gather x3 -> x2, waiting for transfers between devices: 33.2 us -> 0.01 us  [over_vol(): return lax.all_gather(x, 'vol', axis=0, tiled=True)]
    all_to_all x1 -> x2, waiting for transfers between devices: 0.01 us -> 9.75 us  [over_ctl(): return lax.all_to_all(x, 'ctl', 0, 0, tiled=True)]
    all_to_all x1 -> x2, starting transfers between devices: 6.53 us -> 11.3 us  [over_ctl(): return lax.all_to_all(x, 'ctl', 0, 0, tiled=True)]
    pallas_call x3 -> x2, Pallas kernels: 50.3 us -> 45.7 us  [make_tiles(): pl.pallas_call(functools.partial(tiles_kernel, reach, group), out_shape=j...]
    slice x8 -> x0, local copies, waits for them, and re-layouts: 3.87 us -> none  [the longest x5 1.57 us: body(): head_at, tail_at = (node_at[:HEAD * 9], node_at[HEAD * 9:])]
    ppermute x0 -> x1, starting transfers between devices: none -> 2.77 us  [body(): lax.ppermute(half, 'vol', [(i, i ^ 1) for i in range(lax.axis_size('vol'))])]
    all_to_all x1, starting transfers between devices: 7.76 us -> 10.5 us  [body(): dot_rows = lax.all_to_all(dot_rows, ('vol', 'ctl'), 0, 0, tiled=True)]
    all_to_all x1, blocking collectives: 21.6 us -> 24.1 us  [over_ctl(): return lax.all_to_all(x, 'ctl', 0, 0, tiled=True)]
  transfers between devices with their start and end apart: 5 -> 6, of which waited for: 3 -> 2; matrix products, arithmetic and copies ran while one was open for 3% -> 3% of each run, Pallas kernels for 44% -> 44%
where the time goes in v4:
time: 203 us; the launch traced here: 202 us
  Pallas kernels  110 us (54%)
  starting transfers between devices  24.6 us (12%)
  blocking collectives  24.1 us (12%)
  between operations  14.3 us (7%)
  local copies, waits for them, and re-layouts  13.8 us (7%)
  waiting for transfers between devices  11.2 us (6%)
  other arithmetic  4.51 us (2%)
    pallas_call x2, Pallas kernels, make_tiles(): pl.pallas_call(functools.partial(tiles_kernel, reach, group), out_shape=j...  45.7 us
    pallas_call x1, Pallas kernels, apply_tiles(): pl.pallas_call(functools.partial(apply_kernel, reach, group, len(vecs)),...  29.5 us
    all_to_all x1, blocking collectives, over_ctl(): return lax.all_to_all(x, 'ctl', 0, 0, tiled=True)  24.1 us
    pallas_call x1, Pallas kernels, spread_all(): pl.pallas_call(spread_all_kernel, out_shape=jax.ShapeDtypeStruct((128, 48...  13.6 us
    all_to_all x2, starting transfers between devices, over_ctl(): return lax.all_to_all(x, 'ctl', 0, 0, tiled=True)  11.3 us
    pallas_call x1, Pallas kernels, step_and_apply(): pl.pallas_call(step_kernel, out_shape=[jax.ShapeDtypeStruct(f.shape, jnp....  11 us
    all_to_all x1, starting transfers between devices, body(): dot_rows = lax.all_to_all(dot_rows, ('vol', 'ctl'), 0, 0, tiled=True)  10.5 us
    pallas_call x1, Pallas kernels, spread_and_apply(): pl.pallas_call(spread_kernel, out_shape=[jax.ShapeDtypeStruct((48, BS), j...  9.98 us
  transfers between devices with their start and end apart: 6, of which 2 were waited for; matrix products, arithmetic and copies ran while one was open for 3% of the time, Pallas kernels for 44%

profile of v4, /device:TPU:1, one launch (start us, length us, event | category | flops | bytes accessed | tf_op | source)
XLA Modules:
  0.0 202.2 jit_solution(3450728898055561870)
XLA Ops:
  7.2 0.7 add_convert_fusion.1
  8.0 0.8 reshape.165
  8.8 0.8 broadcast_in_dim.20
  9.6 7.7 %all-to-all-start = ((f32[16,56,128]{2,1,0:T(8,128)}), f32[16,56,128]{2,1,0:T(8,128)S(1)}, u32[]{:S(2)}, u32[]{:S(2)}) async-start(f32[16,56,128]{2,1,0:T(8,128)} %broadcast_in_dim.20), calls=%async_computation | async-start | bytes 917504 | tf_op jit(solution)/shard_map/all_to_all | solution.py:336
  17.5 9.7 %all-to-all-done = f32[16,56,128]{2,1,0:T(8,128)S(1)} async-done(((f32[16,56,128]{2,1,0:T(8,128)}), f32[16,56,128]{2,1,0:T(8,128)S(1)}, u32[]{:S(2)}, u32[]{:S(2)}) %all-to-all-start) | async-done | bytes 458784 | tf_op jit(solution)/shard_map/all_to_all | solution.py:336
  27.2 0.1 broadcast_in_dim.22
  27.4 0.6 copy-done.2
  28.0 24.1 %all_to_all.20 = f32[16,192,128]{2,1,0:T(8,128)S(1)} all-to-all(f32[16,192,128]{2,1,0:T(8,128)S(1)} %broadcast_in_dim.22), channel_id=1, replica_groups=mesh['vol'=8,'ctl'=16] {'ctl'}, dimensions={0} | all-to-all | bytes 3145728 | tf_op jit(solution)/shard_map/all_to_all | solution.py:336
  52.1 2.8 %collective-permute-start = (f32[16,192,128]{2,1,0:T(8,128)S(1)}, f32[16,192,128]{2,1,0:T(8,128)S(1)}, u32[]{:S(2)}, u32[]{:S(2)}) collective-permute-start(f32[16,192,128]{2,1,0:T(8,128)S(1)} %all_to_all.20), channel_id=1, source_target_pairs={{0,16},{16,0},{32,48},{48,32},{64,80},{80,64},{96,112},{112,96},{1... | collective-permute-start | bytes 4718600 | tf_op jit(solution)/shard_map/ppermute | solution.py:371
  55.0 0.7 reshape.194.idx_ref
  55.9 0.6 pad.13.pts_ref
  56.5 1.4 collective-permute-done
  57.9 1.8 pad_maximum_fusion
  59.7 11.6 %shard_map.77.tile_hbm = f32[144,128,128]{2,1,0:T(8,128)} custom-call(s32[144]{0:T(256)} %reshape.194.idx_ref, f32[16,8,128]{2,1,0:T(8,128)} %pad.13.pts_ref, f32[6144,128]{1,0:T(8,128)} %bitcast.39), custom_call_target="tpu_custom_call" | custom-call | flops 56623104 | bytes 9437184 | tf_op jit(solution)/shard_map/pallas_call | solution.py:82
  71.3 0.7 broadcast_in_dim.18.want_ref
  72.0 10.0 %shard_map.78 = (f32[48,128]{1,0:T(8,128)}, f32[48,128]{1,0:T(8,128)}) custom-call(f32[144,128]{1,0:T(8,128)} %broadcast_in_dim.18.want_ref, f32[128,56,128]{2,1,0:T(8,128)} %all-gather.3.cloned.1.call-done.sens_ref, f32[144,128,128]{2,1,0:T(8,128)} %shard_map.77.tile_hbm), custom_call_target="tpu_custom_call" | custom-call | flops 452984832 | bytes 9437184 | tf_op jit(solution)/shard_map/pallas_call | solution.py:196
  82.0 1.5 broadcast_in_dim.23
  83.5 3.6 %all-to-all-start.2 = ((f32[16,48,128]{2,1,0:T(8,128)}), f32[16,48,128]{2,1,0:T(8,128)S(1)}, u32[]{:S(2)}, u32[]{:S(2)}) async-start(f32[16,48,128]{2,1,0:T(8,128)} %broadcast_in_dim.23), calls=%async_computation.2 | async-start | bytes 786432 | tf_op jit(solution)/shard_map/all_to_all | solution.py:336
  87.1 13.6 %shard_map.79 = f32[128,48,128]{2,1,0:T(8,128)} custom-call(f32[128,56,128]{2,1,0:T(8,128)} %all-gather.3.cloned.1.call-done.sens_ref), custom_call_target="tpu_custom_call" | custom-call | flops 6442450944 | bytes 7340032 | tf_op jit(solution)/shard_map/pallas_call | solution.py:235
  100.7 0.8 copy-done.3
  101.6 0.7 reshape.195.idx_ref
  102.4 0.7 pad.14.pts_ref
  103.2 0.7 reshape.192.idx_ref
  103.9 34.1 %shard_map.80.tile_ref = f32[576,128,128]{2,1,0:T(8,128)} custom-call(s32[576]{0:T(1024)} %reshape.195.idx_ref, f32[64,8,128]{2,1,0:T(8,128)} %pad.14.pts_ref, f32[6144,128]{1,0:T(8,128)} %bitcast.40), custom_call_target="tpu_custom_call" | custom-call | flops 226492416 | bytes 37748736 | tf_op jit(solution)/shard_map/pallas_call | solution.py:82
  138.0 11.0 %shard_map.81 = (f32[6144,128]{1,0:T(8,128)}, f32[8,128]{1,0:T(8,128)}, f32[1,128]{1,0:T(1,128)}) custom-call(s32[144]{0:T(256)} %reshape.192.idx_ref, f32[6144,128]{1,0:T(8,128)} %bitcast.41, f32[6144,128]{1,0:T(8,128)} %bitcast.44, f32[144,128,128]{2,1,0:T(8,128)} %shard_map.77.tile_hbm), custom_call_target="tpu_custom_call", output_to_operand_aliasing={{0}: (2, {})} | custom-call | flops 22020096 | bytes 18874368 | tf_op jit(solution)/shard_map/pallas_call | solution.py:314
  149.0 1.1 dynamic-slice_bitcast_fusion
  150.1 1.5 broadcast_in_dim.48
  151.6 10.5 %all-to-all-start.3 = ((f32[128,8,128]{2,1,0:T(8,128)}), f32[128,8,128]{2,1,0:T(8,128)S(1)}, u32[]{:S(2)}, u32[]{:S(2)}) async-start(f32[128,8,128]{2,1,0:T(8,128)} %broadcast_in_dim.48), calls=%async_computation.3 | async-start | bytes 1048576 | tf_op jit(solution)/shard_map/all_to_all | solution.py:407
  162.2 0.7 reshape.196.idx_ref
  162.9 29.5 %shard_map.82 = (f32[64,8,128]{2,1,0:T(8,128)}, f32[64,8,128]{2,1,0:T(8,128)}) custom-call(s32[576]{0:T(1024)} %reshape.196.idx_ref, f32[576,128,128]{2,1,0:T(8,128)} %shard_map.80.tile_ref, f32[6144,128]{1,0:T(8,128)} %bitcast.43, f32[6144,128]{1,0:T(8,128)} %get-tuple-element.39.refs_1_), custom_call_target="tpu_custom_call" | custom-call | flops 113246208 | bytes 37748736 | tf_op jit(solution)/shard_map/pallas_call | solution.py:127
  192.8 0.8 copy.62
  193.6 1.8 multiply_bitcast_fusion
  (46 shorter events, 1.3 us)
Async XLA Ops:
  7.2 10.2 %copy-start = (f32[3,16384]{1,0:T(4,128)S(1)}, f32[3,16384]{1,0:T(4,128)}, u32[]{:S(2)}) copy-start(f32[3,16384]{1,0:T(4,128)} %param.8) | copy-start | bytes 589828
  9.6 45.3 %copy-start.7 = (s32[128,8]{0,1:T(8,128)S(1)}, s32[128,8]{0,1:T(8,128)}, u32[]{:S(2)}) copy-start(s32[128,8]{0,1:T(8,128)} %param.9) | copy-start | bytes 12292
  9.6 17.6 %all-to-all-start = ((f32[16,56,128]{2,1,0:T(8,128)}), f32[16,56,128]{2,1,0:T(8,128)S(1)}, u32[]{:S(2)}, u32[]{:S(2)}) async-start(f32[16,56,128]{2,1,0:T(8,128)} %broadcast_in_dim.20), calls=%async_computation | async-start | bytes 917504 | tf_op jit(solution)/shard_map/all_to_all | solution.py:336
  17.3 53.9 %all-gather.3.cloned.1.call-start = ((), (), s32[]{:S(2)}) async-start(), calls=%async_computation.4 | async-start | bytes 4128768 | tf_op jit(solution)/shard_map/all_gather | solution.py:340
  27.2 0.8 copy-start.2
  52.1 5.8 %collective-permute-start = (f32[16,192,128]{2,1,0:T(8,128)S(1)}, f32[16,192,128]{2,1,0:T(8,128)S(1)}, u32[]{:S(2)}, u32[]{:S(2)}) collective-permute-start(f32[16,192,128]{2,1,0:T(8,128)S(1)} %all_to_all.20), channel_id=1, source_target_pairs={{0,16},{16,0},{32,48},{48,32},{64,80},{80,64},{96,112},{112,96},{1... | collective-permute-start | bytes 4718600 | tf_op jit(solution)/shard_map/ppermute | solution.py:371
  83.5 17.2 %all-to-all-start.2 = ((f32[16,48,128]{2,1,0:T(8,128)}), f32[16,48,128]{2,1,0:T(8,128)S(1)}, u32[]{:S(2)}, u32[]{:S(2)}) async-start(f32[16,48,128]{2,1,0:T(8,128)} %broadcast_in_dim.23), calls=%async_computation.2 | async-start | bytes 786432 | tf_op jit(solution)/shard_map/all_to_all | solution.py:336
  87.1 14.5 %copy-start.5 = (s32[64,9]{0,1:T(8,128)S(1)}, s32[64,9]{0,1:T(8,128)}, u32[]{:S(2)}) copy-start(s32[64,9]{0,1:T(8,128)} %param.11) | copy-start | bytes 6916
  87.1 15.3 %copy-start.4 = (f32[3,8192]{1,0:T(4,128)S(1)}, f32[3,8192]{1,0:T(4,128)}, u32[]{:S(2)}) copy-start(f32[3,8192]{1,0:T(4,128)} %param.10) | copy-start | bytes 294916
  87.1 50.9 %all-gather.5.cloned.1.call-start = ((), (), s32[]{:S(2)}) async-start(), calls=%async_computation.5 | async-start | bytes 3538944 | tf_op jit(solution)/shard_map/all_gather | solution.py:340
  100.7 0.8 copy-start.3
  151.6 41.0 %all-to-all-start.3 = ((f32[128,8,128]{2,1,0:T(8,128)}), f32[128,8,128]{2,1,0:T(8,128)S(1)}, u32[]{:S(2)}, u32[]{:S(2)}) async-start(f32[128,8,128]{2,1,0:T(8,128)} %broadcast_in_dim.48), calls=%async_computation.3 | async-start | bytes 1048576 | tf_op jit(solution)/shard_map/all_to_all | solution.py:407
  162.9 29.5 %copy-start.6 = (f32[8,128]{1,0:T(8,128)S(1)}, f32[8,128]{1,0:T(8,128)}, u32[]{:S(2)}) copy-start(f32[8,128]{1,0:T(8,128)} %get-tuple-element.33) | copy-start | bytes 12292
  162.9 32.5 %copy-start.1 = (f32[3,16384]{1,0:T(4,128)S(1)}, f32[3,16384]{1,0:T(4,128)}, u32[]{:S(2)}) copy-start(f32[3,16384]{1,0:T(4,128)} %param.8) | copy-start | bytes 589828
Sparse Core Ops, SparseCore 0:
  28.1 30.2 all-gather.2
  101.6 30.5 all-gather.4

commit v5 on v4

--- a/solution.py
+++ b/solution.py
@@ -12,6 +12,8 @@
 NODE_SCALE = 0.25
 VMEM = 56 * 1024 * 1024
 CHUNK = 32
+STORED = 56
+UNROLL = 7
 
 
 def whole(shape):
@@ -19,32 +21,30 @@
 
 
 def lane_sums(group, acc_ref):
-    ones = jnp.ones((BS, BS), jnp.bfloat16)
-    eye = lax.broadcasted_iota(jnp.int32, (BS, BS), 0) == lax.broadcasted_iota(jnp.int32, (BS, BS), 1)
-    out = []
-    for k in range(3):
-        part = acc_ref[k]
-        high = part.astype(jnp.bfloat16)
-        rest = (part - high.astype(jnp.float32)).astype(jnp.bfloat16)
-        total = jnp.dot(high, ones, preferred_element_type=jnp.float32)
-        total = total + jnp.dot(rest, ones, preferred_element_type=jnp.float32)
-        out.append(
-            [
-                jnp.sum(jnp.where(eye, total[g * BS : (g + 1) * BS], 0.0), axis=0, keepdims=True)
-                for g in range(group)
-            ]
-        )
-    return out
-
-
-def store_sums(group, acc_ref, sum_ref):
-    rows = lax.broadcasted_iota(jnp.int32, (8, BS), 0)
-    found = lane_sums(group, acc_ref)
-    for g in range(group):
-        out = jnp.zeros((8, BS), jnp.float32)
-        for k in range(3):
-            out = jnp.where(rows == k, found[k][g], out)
-        sum_ref[g] = out
+    return [
+        [
+            jnp.sum(jnp.transpose(acc_ref[k, g * BS : (g + 1) * BS, :]), axis=0, keepdims=True)
+            for g in range(group)
+        ]
+        for k in range(3)
+    ]
+
+
+def phi_block(g, base, reach, idx_ref, cols_ref, ctl_ref, tile_ref):
+    for lo in range(0, BS, CHUNK):
+        own = [
+            jnp.broadcast_to(cols_ref[g, lo : lo + CHUNK, k : k + 1], (CHUNK, BS)) for k in range(3)
+        ]
+        for t in range(reach):
+            at = idx_ref[base + t]
+            dist = None
+            for k in range(3):
+                gap = own[k] - ctl_ref[pl.ds(at + 64 * k, 1), :]
+                dist = gap * gap if dist is None else dist + gap * gap
+            ratio = dist * lax.rsqrt(jnp.maximum(dist, 1e-30))
+            inner = jnp.maximum(1.0 - ratio, 0.0)
+            sq = inner * inner
+            tile_ref[g * reach + t, lo : lo + CHUNK, :] = (sq * sq) * (4.0 * ratio + 1.0)
 
 
 def tiles_kernel(reach, group, idx_ref, pts_ref, ctl_ref, tile_ref, cols_ref):
@@ -53,23 +53,7 @@
         cols_ref[g] = jnp.transpose(pts_ref[g])
 
     def one(g, carry):
-        base = (step * group + g) * reach
-        for lo in range(0, BS, CHUNK):
-            own = [
-                jnp.broadcast_to(cols_ref[g, lo : lo + CHUNK, k : k + 1], (CHUNK, BS))
-                for k in range(3)
-            ]
-            for t in range(reach):
-                at = idx_ref[base + t]
-                dist = None
-                for k in range(3):
-                    gap = own[k] - ctl_ref[pl.ds(at + 64 * k, 1), :]
-                    dist = gap * gap if dist is None else dist + gap * gap
-                ratio = dist * lax.rsqrt(jnp.maximum(dist, 1e-30))
-                inner = jnp.maximum(1.0 - ratio, 0.0)
-                sq = inner * inner
-                tile = (sq * sq) * (4.0 * ratio + 1.0)
-                tile_ref[g * reach + t, lo : lo + CHUNK, :] = tile
+        phi_block(g, (step * group + g) * reach, reach, idx_ref, cols_ref, ctl_ref, tile_ref)
         return carry
 
     lax.fori_loop(0, group, one, 0)
@@ -96,50 +80,101 @@
     )(idx, pts, ctl)
 
 
-def apply_kernel(reach, group, count, idx_ref, tile_ref, *refs):
-    vec_refs, sum_refs, acc_refs = refs[:count], refs[count : 2 * count], refs[2 * count :]
+def node_kernel(
+    reach, stored, fresh, total, idx_ref, at_ref, tile_ref, f_ref, p_ref, pts_ref, ctl_ref,
+    sum_ref, more_ref, new_ref, cols_ref, rows_ref, raw_ref,
+):
     step = pl.program_id(0)
-
-    def one(g, carry):
-        base = (step * group + g) * reach
-        start = pl.multiple_of(g * BS, BS)
-        for lo in range(0, BS, CHUNK):
-            acc = [[jnp.zeros((CHUNK, BS), jnp.float32) for _ in range(3)] for _ in vec_refs]
-            for t in range(reach):
-                at = idx_ref[base + t]
-                tile = tile_ref[g * reach + t, lo : lo + CHUNK, :]
-                for n, vec_ref in enumerate(vec_refs):
-                    for k in range(3):
-                        acc[n][k] = acc[n][k] + tile * vec_ref[pl.ds(at + 16 * k, 1), :]
-            for n, acc_ref in enumerate(acc_refs):
-                for k in range(3):
-                    acc_ref[k, pl.ds(start + lo, CHUNK), :] = acc[n][k]
-        return carry
-
-    lax.fori_loop(0, group, one, 0)
-    for acc_ref, sum_ref in zip(acc_refs, sum_refs):
-        store_sums(group, acc_ref, sum_ref)
-
-
-def apply_tiles(idx, tiles, vecs, reach, group):
-    count = tiles.shape[0] // reach
-    elements = tiles.size
+    for g in range(fresh):
+        cols_ref[g] = jnp.transpose(pts_ref[g])
+    rows_ref[...] = jnp.zeros_like(rows_ref)
+
+    def first(g):
+        return jnp.where(g < stored, step * stored + g, total + step * fresh + g - stored) * reach
+
+    def fill(g, carry):
+        base = first(g)
+        for t in range(reach):
+            at = idx_ref[base + t]
+            for k in range(3):
+                rows_ref[g, k : k + 1, t * BS : (t + 1) * BS] = f_ref[pl.ds(at + 16 * k, 1), :]
+                rows_ref[g, k + 3 : k + 4, t * BS : (t + 1) * BS] = p_ref[pl.ds(at + 16 * k, 1), :]
+        return carry
+
+    lax.fori_loop(0, stored + fresh, fill, 0)
+
+    def apply(src_ref, g, slot):
+        rows = rows_ref[slot]
+        high = rows.astype(jnp.bfloat16).astype(jnp.float32)
+        cut = jnp.concatenate([high, rows - high], axis=0).astype(jnp.bfloat16)
+        tile = jnp.concatenate([src_ref[g * reach + t] for t in range(reach)], axis=1)
+        high = tile.astype(jnp.bfloat16)
+        rest = (tile - high.astype(jnp.float32)).astype(jnp.bfloat16)
+        dims = (((1,), (1,)), ((), ()))
+        out = lax.dot_general(high, cut, dims, preferred_element_type=jnp.float32)
+        raw_ref[slot] = out + lax.dot_general(rest, cut, dims, preferred_element_type=jnp.float32)
+
+    def old(g, carry):
+        apply(tile_ref, g, g)
+        return carry
+
+    def make(g, carry):
+        phi_block(
+            g, (total + step * fresh + g) * reach, reach, at_ref, cols_ref, ctl_ref, new_ref
+        )
+        return carry
+
+    lax.fori_loop(0, stored, old, 0, unroll=UNROLL)
+    if fresh:
+        lax.fori_loop(0, fresh, make, 0)
+        for g in range(fresh):
+            apply(new_ref, g, stored + g)
+    for g in range(stored + fresh):
+        both = jnp.transpose(raw_ref[g])
+        both = both[:8] + both[8:]
+        if g < stored:
+            sum_ref[g] = both
+        else:
+            more_ref[g - stored] = both
+
+
+def node_sums(idx, at, tiles, f, p, pts, ctl, reach, steps):
+    total, extra = tiles.shape[0] // reach, pts.shape[0]
+    stored, fresh = total // steps, extra // steps
+    elements = (total + extra) * reach * BS * BS
+
+    def block(count):
+        return pl.BlockSpec((count, 8, BS), lambda m, *_: (m, 0, 0))
+
     return pl.pallas_call(
-        functools.partial(apply_kernel, reach, group, len(vecs)),
-        out_shape=[jax.ShapeDtypeStruct((count, 8, BS), jnp.float32) for _ in vecs],
+        functools.partial(node_kernel, reach, stored, fresh, total),
+        out_shape=[
+            jax.ShapeDtypeStruct((total, 8, BS), jnp.float32),
+            jax.ShapeDtypeStruct((extra, 8, BS), jnp.float32),
+        ],
         grid_spec=pltpu.PrefetchScalarGridSpec(
-            num_scalar_prefetch=1,
-            grid=(count // group,),
-            in_specs=[pl.BlockSpec((group * reach, BS, BS), lambda m, *_: (m, 0, 0))]
-            + [whole(vec.shape) for vec in vecs],
-            out_specs=[pl.BlockSpec((group, 8, BS), lambda m, *_: (m, 0, 0)) for _ in vecs],
-            scratch_shapes=[pltpu.VMEM((3, group * BS, BS), jnp.float32) for _ in vecs],
+            num_scalar_prefetch=2,
+            grid=(steps,),
+            in_specs=[
+                pl.BlockSpec((stored * reach, BS, BS), lambda m, *_: (m, 0, 0)),
+                whole(f.shape),
+                whole(p.shape),
+                block(fresh),
+                whole(ctl.shape),
+            ],
+            out_specs=[block(stored), block(fresh)],
+            scratch_shapes=[
+                pltpu.VMEM((fresh * reach, BS, BS), jnp.float32),
+                pltpu.VMEM((fresh, BS, 8), jnp.float32),
+                pltpu.VMEM((stored + fresh, 8, reach * BS), jnp.float32),
+                pltpu.VMEM((stored + fresh, BS, 16), jnp.float32),
+            ],
         ),
         compiler_params=pltpu.CompilerParams(vmem_limit_bytes=VMEM),
         cost_estimate=pl.CostEstimate(
-            flops=elements * 6 * len(vecs), bytes_accessed=elements * 4, transcendentals=0
-        ),
-    )(idx, tiles, *vecs)
+            flops=elements * 12, bytes_accessed=elements * 4, transcendentals=0
+        ),
+    )(idx, at, tiles, f, p, pts, ctl)
 
 
 def operator_sums(tile_ref, acc_ref, row):
@@ -218,15 +253,15 @@
         for k in range(3):
             part = sens_ref[:, 16 * k : 16 * k + 16, :].reshape(2048, BS)
             high = part.astype(jnp.bfloat16)
-            cut_ref[0, :, k * BS : (k + 1) * BS] = high
-            cut_ref[1, :, k * BS : (k + 1) * BS] = (part - high.astype(jnp.float32)).astype(jnp.bfloat16)
+            cut_ref[:, k * BS : (k + 1) * BS] = high
+            cut_ref[:, (k + 3) * BS : (k + 4) * BS] = (part - high.astype(jnp.float32)).astype(jnp.bfloat16)
 
     want = (lax.broadcasted_iota(jnp.int32, (256, BS), 0) + step * 256).astype(jnp.float32)
     hot = jnp.concatenate(
         [(want == ids_ref[g : g + 1, :]).astype(jnp.bfloat16) for g in range(16)], axis=1
     )
-    acc = jnp.dot(hot, cut_ref[0], preferred_element_type=jnp.float32)
-    acc = acc + jnp.dot(hot, cut_ref[1], preferred_element_type=jnp.float32)
+    acc = jnp.dot(hot, cut_ref[...], preferred_element_type=jnp.float32)
+    acc = acc[:, : 3 * BS] + acc[:, 3 * BS :]
     for k in range(3):
         out_ref[:, 16 * k : 16 * k + 16, :] = acc[:, k * BS : (k + 1) * BS].reshape(16, 16, BS)
 
@@ -239,7 +274,7 @@
         in_specs=[whole(sens.shape)],
         out_specs=pl.BlockSpec((16, 48, BS), lambda m: (m, 0, 0)),
         scratch_shapes=[
-            pltpu.VMEM((2, 2048, 3 * BS), jnp.bfloat16),
+            pltpu.VMEM((2048, 6 * BS), jnp.bfloat16),
             pltpu.VMEM((16, BS), jnp.float32),
         ],
         compiler_params=pltpu.CompilerParams(vmem_limit_bytes=VMEM),
@@ -391,7 +426,7 @@
     near_image, f_all, coords_rows = lax.optimization_barrier((near_image, f_all, coords_rows))
     image_all = over_vol(near_image).reshape(128 * 48, BS)
     f_rows = f_all.reshape(128 * 48, BS)
-    tiles = make_tiles(coord_at(node_lists), points, coords_rows, 9, 8)
+    tiles = make_tiles(coord_at(node_lists), points[:STORED], coords_rows, 9, 8)
     image_all, tiles = lax.optimization_barrier((image_all, tiles))
     p_rows, coef, dot_row = step_and_apply(op_at, f_rows, image_all, op_tiles)
 
@@ -405,16 +440,16 @@
         (jnp.broadcast_to(dot_row[None], (128, 8, BS)), p_rows, f_mine, p_mine)
     )
     dot_rows = lax.all_to_all(dot_rows, ("vol", "ctl"), 0, 0, tiled=True)
-    node_f, node_p = apply_tiles(node_at, tiles, [f_rows, p_rows], 9, 8)
-    dot_rows, node_f, node_p = lax.optimization_barrier((dot_rows, node_f, node_p))
+    sums, more = node_sums(
+        node_at, coord_at(node_lists), tiles, f_rows, p_rows, points[STORED:], coords_rows, 9, 8
+    )
+    dot_rows, sums, more = lax.optimization_barrier((dot_rows, sums, more))
+    sums = jnp.concatenate([sums, more], axis=0).transpose(1, 0, 2)
     alpha1 = coef[4:7, 0] / jnp.sum(dot_rows[:, 0], axis=0)[:3]
-
-    def back(sums):
-        return sums[:, :3].transpose(1, 0, 2)
 
     weights = alpha0[:, None, None] * f_mine + alpha1[:, None, None] * p_mine
     shift = NODE_SCALE * (
-        alpha0[:, None, None] * back(node_f) + alpha1[:, None, None] * back(node_p)
+        alpha0[:, None, None] * sums[0:3] + alpha1[:, None, None] * sums[3:6]
     )
     return weights.reshape(3, -1), shift.reshape(3, -1)
 

time: 203 us -> 190 us (0.936)
  Pallas kernels: 110 us -> 96.5 us
    pallas_call x1, Pallas kernels: 29.5 us -> 23.2 us  [node_sums(): pl.pallas_call(functools.partial(node_kernel, reach, stored, fresh, total...]
    pallas_call x2, Pallas kernels: 45.7 us -> 41.9 us  [make_tiles(): pl.pallas_call(functools.partial(tiles_kernel, reach, group), out_shape=j...]
    pallas_call x1, Pallas kernels: 13.6 us -> 11.4 us  [spread_all(): pl.pallas_call(spread_all_kernel, out_shape=jax.ShapeDtypeStruct((128, 48...]
  transfers between devices with their start and end apart: 6 -> 6, of which waited for: 2 -> 2; matrix products, arithmetic and copies ran while one was open for 3% -> 4% of each run, Pallas kernels for 44% -> 40%
where the time goes in v5:
time: 190 us; the launch traced here: 189 us
  Pallas kernels  96.5 us (51%)
  starting transfers between devices  24.6 us (13%)
  blocking collectives  24.1 us (13%)
  local copies, waits for them, and re-layouts  14.4 us (8%)
  between operations  14.3 us (8%)
  waiting for transfers between devices  11.2 us (6%)
  other arithmetic  4.46 us (2%)
    pallas_call x2, Pallas kernels, make_tiles(): pl.pallas_call(functools.partial(tiles_kernel, reach, group), out_shape=j...  41.9 us
    all_to_all x1, blocking collectives, over_ctl(): return lax.all_to_all(x, 'ctl', 0, 0, tiled=True)  24.1 us
    pallas_call x1, Pallas kernels, node_sums(): pl.pallas_call(functools.partial(node_kernel, reach, stored, fresh, total...  23.2 us
    pallas_call x1, Pallas kernels, spread_all(): pl.pallas_call(spread_all_kernel, out_shape=jax.ShapeDtypeStruct((128, 48...  11.4 us
    all_to_all x2, starting transfers between devices, over_ctl(): return lax.all_to_all(x, 'ctl', 0, 0, tiled=True)  11.3 us
    pallas_call x1, Pallas kernels, step_and_apply(): pl.pallas_call(step_kernel, out_shape=[jax.ShapeDtypeStruct(f.shape, jnp....  10.8 us
    all_to_all x1, starting transfers between devices, body(): dot_rows = lax.all_to_all(dot_rows, ('vol', 'ctl'), 0, 0, tiled=True)  10.5 us
    all_to_all x2, waiting for transfers between devices, over_ctl(): return lax.all_to_all(x, 'ctl', 0, 0, tiled=True)  9.75 us
  transfers between devices with their start and end apart: 6, of which 2 were waited for; matrix products, arithmetic and copies ran while one was open for 4% of the time, Pallas kernels for 40%

profile of v5, /device:TPU:1, one launch (start us, length us, event | category | flops | bytes accessed | tf_op | source)
XLA Modules:
  0.0 189.5 jit_solution(5884254519744412104)
XLA Ops:
  7.2 0.7 add_convert_fusion.1
  8.0 0.8 reshape.165
  8.8 0.8 broadcast_in_dim.20
  9.6 7.7 %all-to-all-start = ((f32[16,56,128]{2,1,0:T(8,128)}), f32[16,56,128]{2,1,0:T(8,128)S(1)}, u32[]{:S(2)}, u32[]{:S(2)}) async-start(f32[16,56,128]{2,1,0:T(8,128)} %broadcast_in_dim.20), calls=%async_computation | async-start | bytes 917504 | tf_op jit(solution)/shard_map/all_to_all | solution.py:371
  17.5 9.7 %all-to-all-done = f32[16,56,128]{2,1,0:T(8,128)S(1)} async-done(((f32[16,56,128]{2,1,0:T(8,128)}), f32[16,56,128]{2,1,0:T(8,128)S(1)}, u32[]{:S(2)}, u32[]{:S(2)}) %all-to-all-start) | async-done | bytes 458784 | tf_op jit(solution)/shard_map/all_to_all | solution.py:371
  28.0 24.1 %all_to_all.20 = f32[16,192,128]{2,1,0:T(8,128)S(1)} all-to-all(f32[16,192,128]{2,1,0:T(8,128)S(1)} %broadcast_in_dim.22), channel_id=1, replica_groups=mesh['vol'=8,'ctl'=16] {'ctl'}, dimensions={0} | all-to-all | bytes 3145728 | tf_op jit(solution)/shard_map/all_to_all | solution.py:371
  52.1 2.8 %collective-permute-start = (f32[16,192,128]{2,1,0:T(8,128)S(1)}, f32[16,192,128]{2,1,0:T(8,128)S(1)}, u32[]{:S(2)}, u32[]{:S(2)}) collective-permute-start(f32[16,192,128]{2,1,0:T(8,128)S(1)} %all_to_all.20), channel_id=1, source_target_pairs={{0,16},{16,0},{32,48},{48,32},{64,80},{80,64},{96,112},{112,96},{1... | collective-permute-start | bytes 4718600 | tf_op jit(solution)/shard_map/ppermute | solution.py:406
  55.0 0.7 reshape.194.idx_ref
  55.9 0.6 pad.13.pts_ref
  56.5 1.4 collective-permute-done
  57.9 1.8 pad_maximum_fusion
  59.7 11.5 %shard_map.77.tile_hbm = f32[144,128,128]{2,1,0:T(8,128)} custom-call(s32[144]{0:T(256)} %reshape.194.idx_ref, f32[16,8,128]{2,1,0:T(8,128)} %pad.13.pts_ref, f32[6144,128]{1,0:T(8,128)} %bitcast.39), custom_call_target="tpu_custom_call" | custom-call | flops 56623104 | bytes 9437184 | tf_op jit(solution)/shard_map/pallas_call | solution.py:66
  71.2 0.7 broadcast_in_dim.18.want_ref
  72.0 9.2 %shard_map.78 = (f32[48,128]{1,0:T(8,128)}, f32[48,128]{1,0:T(8,128)}) custom-call(f32[144,128]{1,0:T(8,128)} %broadcast_in_dim.18.want_ref, f32[128,56,128]{2,1,0:T(8,128)} %all-gather.3.cloned.1.call-done.sens_ref, f32[144,128,128]{2,1,0:T(8,128)} %shard_map.77.tile_hbm), custom_call_target="tpu_custom_call" | custom-call | flops 452984832 | bytes 9437184 | tf_op jit(solution)/shard_map/pallas_call | solution.py:231
  81.2 1.5 broadcast_in_dim.23
  82.7 3.6 %all-to-all-start.2 = ((f32[16,48,128]{2,1,0:T(8,128)}), f32[16,48,128]{2,1,0:T(8,128)S(1)}, u32[]{:S(2)}, u32[]{:S(2)}) async-start(f32[16,48,128]{2,1,0:T(8,128)} %broadcast_in_dim.23), calls=%async_computation.2 | async-start | bytes 786432 | tf_op jit(solution)/shard_map/all_to_all | solution.py:371
  86.4 11.4 %shard_map.79 = f32[128,48,128]{2,1,0:T(8,128)} custom-call(f32[128,56,128]{2,1,0:T(8,128)} %all-gather.3.cloned.1.call-done.sens_ref), custom_call_target="tpu_custom_call" | custom-call | flops 6442450944 | bytes 7340032 | tf_op jit(solution)/shard_map/pallas_call | solution.py:270
  97.8 0.8 copy-done.2
  98.7 0.7 reshape.195.idx_ref.at_ref
  99.5 0.7 reshape.192.idx_ref
  100.1 0.7 pad_slice_fusion.1.pts_ref
  100.8 30.3 %shard_map.80.tile_ref = f32[504,128,128]{2,1,0:T(8,128)} custom-call(s32[576]{0:T(1024)} %reshape.195.idx_ref.at_ref, f32[56,8,128]{2,1,0:T(8,128)} %pad_slice_fusion.1.pts_ref, f32[6144,128]{1,0:T(8,128)} %bitcast.40), custom_call_target="tpu_custom_call" | custom-call | flops 198180864 | bytes 33030144 | tf_op jit(solution)/shard_map/pallas_call | solution.py:66
  131.2 10.8 %shard_map.81 = (f32[6144,128]{1,0:T(8,128)}, f32[8,128]{1,0:T(8,128)}, f32[1,128]{1,0:T(1,128)}) custom-call(s32[144]{0:T(256)} %reshape.192.idx_ref, f32[6144,128]{1,0:T(8,128)} %bitcast.42, f32[6144,128]{1,0:T(8,128)} %bitcast.45, f32[144,128,128]{2,1,0:T(8,128)} %shard_map.77.tile_hbm), custom_call_target="tpu_custom_call", output_to_operand_aliasing={{0}: (2, {})} | custom-call | flops 22020096 | bytes 18874368 | tf_op jit(solution)/shard_map/pallas_call | solution.py:349
  142.0 1.1 dynamic-slice_bitcast_fusion
  143.1 1.5 broadcast_in_dim.48
  144.6 10.5 %all-to-all-start.3 = ((f32[128,8,128]{2,1,0:T(8,128)}), f32[128,8,128]{2,1,0:T(8,128)S(1)}, u32[]{:S(2)}, u32[]{:S(2)}) async-start(f32[128,8,128]{2,1,0:T(8,128)} %broadcast_in_dim.48), calls=%async_computation.3 | async-start | bytes 1048576 | tf_op jit(solution)/shard_map/all_to_all | solution.py:442
  155.2 0.7 reshape.196.idx_ref
  155.9 0.6 pad_slice_fusion.pts_ref
  156.5 23.2 %shard_map.82 = (f32[56,8,128]{2,1,0:T(8,128)}, f32[8,8,128]{2,1,0:T(8,128)}) custom-call(s32[576]{0:T(1024)} %reshape.196.idx_ref, s32[576]{0:T(1024)} %reshape.195.idx_ref.at_ref, f32[504,128,128]{2,1,0:T(8,128)} %shard_map.80.tile_ref, f32[6144,128]{1,0:T(8,128)} %bitcast.44, f32[6144,128]{1,0:T(8,128)} %get-tuple-element.39.p_ref, ...), custom_call_target="tpu_custom_call" | custom-call | flops 113246208 | bytes 37748736 | tf_op jit(solution)/shard_map/pallas_call | solution.py:149
  179.9 1.0 maximum_bitcast_fusion
  180.9 0.8 fusion.2
  181.8 0.8 copy.62
  (46 shorter events, 2.0 us)
Async XLA Ops:
  7.2 10.2 %copy-start = (f32[3,16384]{1,0:T(4,128)S(1)}, f32[3,16384]{1,0:T(4,128)}, u32[]{:S(2)}) copy-start(f32[3,16384]{1,0:T(4,128)} %param.8) | copy-start | bytes 589828
  9.6 45.2 %copy-start.6 = (s32[128,8]{0,1:T(8,128)S(1)}, s32[128,8]{0,1:T(8,128)}, u32[]{:S(2)}) copy-start(s32[128,8]{0,1:T(8,128)} %param.9) | copy-start | bytes 12292
  9.6 17.6 %all-to-all-start = ((f32[16,56,128]{2,1,0:T(8,128)}), f32[16,56,128]{2,1,0:T(8,128)S(1)}, u32[]{:S(2)}, u32[]{:S(2)}) async-start(f32[16,56,128]{2,1,0:T(8,128)} %broadcast_in_dim.20), calls=%async_computation | async-start | bytes 917504 | tf_op jit(solution)/shard_map/all_to_all | solution.py:371
  17.3 53.9 %all-gather.3.cloned.1.call-start = ((), (), s32[]{:S(2)}) async-start(), calls=%async_computation.4 | async-start | bytes 4128768 | tf_op jit(solution)/shard_map/all_gather | solution.py:375
  27.2 0.8 copy-start.1
  52.1 5.8 %collective-permute-start = (f32[16,192,128]{2,1,0:T(8,128)S(1)}, f32[16,192,128]{2,1,0:T(8,128)S(1)}, u32[]{:S(2)}, u32[]{:S(2)}) collective-permute-start(f32[16,192,128]{2,1,0:T(8,128)S(1)} %all_to_all.20), channel_id=1, source_target_pairs={{0,16},{16,0},{32,48},{48,32},{64,80},{80,64},{96,112},{112,96},{1... | collective-permute-start | bytes 4718600 | tf_op jit(solution)/shard_map/ppermute | solution.py:406
  82.7 15.0 %all-to-all-start.2 = ((f32[16,48,128]{2,1,0:T(8,128)}), f32[16,48,128]{2,1,0:T(8,128)S(1)}, u32[]{:S(2)}, u32[]{:S(2)}) async-start(f32[16,48,128]{2,1,0:T(8,128)} %broadcast_in_dim.23), calls=%async_computation.2 | async-start | bytes 786432 | tf_op jit(solution)/shard_map/all_to_all | solution.py:371
  86.3 12.3 %copy-start.4 = (s32[64,9]{0,1:T(8,128)S(1)}, s32[64,9]{0,1:T(8,128)}, u32[]{:S(2)}) copy-start(s32[64,9]{0,1:T(8,128)} %param.11) | copy-start | bytes 6916
  86.3 13.8 %copy-start.3 = (f32[3,8192]{1,0:T(4,128)S(1)}, f32[3,8192]{1,0:T(4,128)}, u32[]{:S(2)}) copy-start(f32[3,8192]{1,0:T(4,128)} %param.10) | copy-start | bytes 294916
  86.3 44.9 %all-gather.5.cloned.1.call-start = ((), (), s32[]{:S(2)}) async-start(), calls=%async_computation.5 | async-start | bytes 3538944 | tf_op jit(solution)/shard_map/all_gather | solution.py:375
  97.8 0.8 copy-start.2
  144.6 35.2 %all-to-all-start.3 = ((f32[128,8,128]{2,1,0:T(8,128)}), f32[128,8,128]{2,1,0:T(8,128)S(1)}, u32[]{:S(2)}, u32[]{:S(2)}) async-start(f32[128,8,128]{2,1,0:T(8,128)} %broadcast_in_dim.48), calls=%async_computation.3 | async-start | bytes 1048576 | tf_op jit(solution)/shard_map/all_to_all | solution.py:442
  156.5 23.2 %copy-start.5 = (f32[8,128]{1,0:T(8,128)S(1)}, f32[8,128]{1,0:T(8,128)}, u32[]{:S(2)}) copy-start(f32[8,128]{1,0:T(8,128)} %get-tuple-element.33) | copy-start | bytes 12292
Sparse Core Ops, SparseCore 0:
  28.1 30.2 all-gather.2
  98.7 30.5 all-gather.4

commit v6 on v5

--- a/solution.py
+++ b/solution.py
@@ -224,13 +224,18 @@
         for g in range(16):
             own = near_ref[144 * k + 9 * g : 144 * k + 9 * g + 1, :]
             own_ref[16 * k + g : 16 * k + g + 1, :] = own
-            image_ref[16 * k + g : 16 * k + g + 1, :] = own + sums[k][g] * COUPLING
+            image_ref[0, 16 * k + g : 16 * k + g + 1, :] = own + sums[k][g] * COUPLING
+    for n in range(1, 16):
+        image_ref[n] = image_ref[0]
 
 
 def spread_and_apply(want, sens, tiles):
     return pl.pallas_call(
         spread_kernel,
-        out_shape=[jax.ShapeDtypeStruct((48, BS), jnp.float32)] * 2,
+        out_shape=[
+            jax.ShapeDtypeStruct((48, BS), jnp.float32),
+            jax.ShapeDtypeStruct((16, 48, BS), jnp.float32),
+        ],
         in_specs=[
             pl.BlockSpec(memory_space=pltpu.VMEM),
             pl.BlockSpec(memory_space=pltpu.VMEM),
@@ -341,7 +346,7 @@
             own = p_ref[pl.ds(idx_ref[9 * g] + 16 * k, 1), :]
             total = total + own * (own + sums[k][g] * COUPLING)
         out = jnp.where(lanes == k, jnp.sum(total, axis=1, keepdims=True), out)
-    dot_ref[...] = out
+    dot_ref[...] = jnp.broadcast_to(out[None], (128, 8, BS))
 
 
 def step_and_apply(idx, f, q, tiles):
@@ -351,7 +356,7 @@
         out_shape=[
             jax.ShapeDtypeStruct(f.shape, jnp.float32),
             jax.ShapeDtypeStruct((8, BS), jnp.float32),
-            jax.ShapeDtypeStruct((1, BS), jnp.float32),
+            jax.ShapeDtypeStruct((128, 8, BS), jnp.float32),
         ],
         in_specs=[pl.BlockSpec(memory_space=pltpu.SMEM), vmem, vmem, pl.BlockSpec(memory_space=pl.ANY)],
         scratch_shapes=OPERATOR_SCRATCH,
@@ -399,34 +404,41 @@
         [sensitivity.reshape(48, BS), jnp.pad(id_row, ((0, 7), (0, 0)))], axis=0
     )
     core = vol % 2
-    half = lax.dynamic_slice_in_dim(blocks, core * 64, 64, 1).reshape(192, BS)
-    near, half = lax.optimization_barrier((over_ctl(copies(payload)), copies(half)))
-    sens = over_vol(near)
-    half = over_ctl(half)
-    other = lax.ppermute(half, "vol", [(i, i ^ 1) for i in range(lax.axis_size("vol"))])
-    coords_rows = jnp.concatenate([half, other], axis=0).reshape(2 * 16 * 192, BS)
-
     own = ctl * 128 + vol * 16 + jnp.arange(16, dtype=jnp.int32)
     mates = lax.dynamic_slice_in_dim(partners, vol * 16, 16, 0)
     lists = jnp.concatenate([own[:, None], mates], axis=1).reshape(-1)
     node_lists = node_tiles.reshape(-1)
-    op_at = place(lists)
-    node_at = place(node_lists)
 
     def coord_at(block):
         return ((((block >> 6) & 1) ^ core) * 16 + (block >> 7)) * 192 + (block & 63)
 
-    op_tiles = make_tiles(coord_at(lists), padded(own_coords), coords_rows, 9, 4)
     points = padded(node_coords.reshape(3, 64, BS))
-    want = jnp.broadcast_to(slot(lists).astype(jnp.float32)[:, None], (144, BS))
+    ready = (
+        place(lists),
+        place(node_lists),
+        coord_at(lists),
+        coord_at(node_lists),
+        padded(own_coords),
+        points[:STORED],
+        points[STORED:],
+        jnp.broadcast_to(slot(lists).astype(jnp.float32)[:, None], (144, BS)),
+    )
+    half = copies(lax.dynamic_slice_in_dim(blocks, core * 64, 64, 1).reshape(192, BS))
+    sens = over_vol(over_ctl(copies(payload)))
+    half = over_ctl(half)
+    half, ready = lax.optimization_barrier((half, ready))
+    op_at, node_at, op_coord_at, node_coord_at, own_points, points, more_points, want = ready
+    other = lax.ppermute(half, "vol", [(i, i ^ 1) for i in range(lax.axis_size("vol"))])
+    coords_rows = jnp.concatenate([half, other], axis=0).reshape(2 * 16 * 192, BS)
+    op_tiles = make_tiles(op_coord_at, own_points, coords_rows, 9, 4)
     f_own, image = spread_and_apply(want, sens, op_tiles)
-    image, sens = lax.optimization_barrier((copies(image), sens))
+    image, sens = lax.optimization_barrier((image, sens))
     near_image = over_ctl(image)
     f_all = spread_all(sens)
     near_image, f_all, coords_rows = lax.optimization_barrier((near_image, f_all, coords_rows))
     image_all = over_vol(near_image).reshape(128 * 48, BS)
     f_rows = f_all.reshape(128 * 48, BS)
-    tiles = make_tiles(coord_at(node_lists), points[:STORED], coords_rows, 9, 8)
+    tiles = make_tiles(node_coord_at, points, coords_rows, 9, 8)
     image_all, tiles = lax.optimization_barrier((image_all, tiles))
     p_rows, coef, dot_row = step_and_apply(op_at, f_rows, image_all, op_tiles)
 
@@ -437,11 +449,11 @@
     f_mine, p_mine = mine(f_rows), mine(p_rows)
     alpha0 = coef[0:3, 0]
     dot_rows, p_rows, f_mine, p_mine = lax.optimization_barrier(
-        (jnp.broadcast_to(dot_row[None], (128, 8, BS)), p_rows, f_mine, p_mine)
+        (dot_row, p_rows, f_mine, p_mine)
     )
     dot_rows = lax.all_to_all(dot_rows, ("vol", "ctl"), 0, 0, tiled=True)
     sums, more = node_sums(
-        node_at, coord_at(node_lists), tiles, f_rows, p_rows, points[STORED:], coords_rows, 9, 8
+        node_at, node_coord_at, tiles, f_rows, p_rows, more_points, coords_rows, 9, 8
     )
     dot_rows, sums, more = lax.optimization_barrier((dot_rows, sums, more))
     sums = jnp.concatenate([sums, more], axis=0).transpose(1, 0, 2)

time: 190 us -> 185 us (0.974)
  waiting for transfers between devices: 11.2 us -> 18.8 us
  blocking collectives: 24.1 us -> 17.4 us
  local copies, waits for them, and re-layouts: 14.4 us -> 11.1 us
  starting transfers between devices: 24.6 us -> 21.3 us
    all_to_all x1, blocking collectives: 24.1 us -> 17.4 us  [over_ctl(): return lax.all_to_all(x, 'ctl', 0, 0, tiled=True)]
    all_to_all x2, waiting for transfers between devices: 9.75 us -> 15.3 us  [over_ctl(): return lax.all_to_all(x, 'ctl', 0, 0, tiled=True)]
    all_to_all x2, starting transfers between devices: 11.3 us -> 7.27 us  [over_ctl(): return lax.all_to_all(x, 'ctl', 0, 0, tiled=True)]
  transfers between devices with their start and end apart: 6 -> 6, of which waited for: 2 -> 3; matrix products, arithmetic and copies ran while one was open for 4% -> 5% of each run, Pallas kernels for 40% -> 41%
where the time goes in v6:
time: 185 us; the launch traced here: 184 us
  Pallas kernels  96.8 us (52%)
  starting transfers between devices  21.3 us (12%)
  waiting for transfers between devices  18.8 us (10%)
  blocking collectives  17.4 us (9%)
  between operations  14.3 us (8%)
  local copies, waits for them, and re-layouts  11.1 us (6%)
  other arithmetic  4.66 us (3%)
    pallas_call x2, Pallas kernels, make_tiles(): pl.pallas_call(functools.partial(tiles_kernel, reach, group), out_shape=j...  41.9 us
    pallas_call x1, Pallas kernels, node_sums(): pl.pallas_call(functools.partial(node_kernel, reach, stored, fresh, total...  23 us
    all_to_all x1, blocking collectives, over_ctl(): return lax.all_to_all(x, 'ctl', 0, 0, tiled=True)  17.4 us
    all_to_all x2, waiting for transfers between devices, over_ctl(): return lax.all_to_all(x, 'ctl', 0, 0, tiled=True)  15.3 us
    pallas_call x1, Pallas kernels, spread_all(): pl.pallas_call(spread_all_kernel, out_shape=jax.ShapeDtypeStruct((128, 48...  11.4 us
    pallas_call x1, Pallas kernels, step_and_apply(): pl.pallas_call(step_kernel, out_shape=[jax.ShapeDtypeStruct(f.shape, jnp....  11.1 us
    all_to_all x1, starting transfers between devices, body(): dot_rows = lax.all_to_all(dot_rows, ('vol', 'ctl'), 0, 0, tiled=True)  10.1 us
    pallas_call x1, Pallas kernels, spread_and_apply(): pl.pallas_call(spread_kernel, out_shape=[jax.ShapeDtypeStruct((48, BS), j...  9.44 us
  transfers between devices with their start and end apart: 6, of which 3 were waited for; matrix products, arithmetic and copies ran while one was open for 5% of the time, Pallas kernels for 41%

profile of v6, /device:TPU:1, one launch (start us, length us, event | category | flops | bytes accessed | tf_op | source)
XLA Modules:
  0.0 184.3 jit_solution(14393502580577984776)
XLA Ops:
  7.2 0.7 add_convert_fusion.1
  8.0 0.8 reshape.165
  8.9 17.4 %all_to_all.20 = f32[16,56,128]{2,1,0:T(8,128)} all-to-all(f32[16,56,128]{2,1,0:T(8,128)S(1)} %broadcast_in_dim.16), channel_id=1, replica_groups=mesh['vol'=8,'ctl'=16] {'ctl'}, dimensions={0} | all-to-all | bytes 917504 | tf_op jit(solution)/shard_map/all_to_all | solution.py:376
  26.4 1.3 broadcast_in_dim.13
  27.7 3.7 %all-to-all-start = ((f32[16,192,128]{2,1,0:T(8,128)}), f32[16,192,128]{2,1,0:T(8,128)S(1)}, u32[]{:S(2)}, u32[]{:S(2)}) async-start(f32[16,192,128]{2,1,0:T(8,128)} %broadcast_in_dim.13), calls=%async_computation | async-start | bytes 3145728 | tf_op jit(solution)/shard_map/all_to_all | solution.py:376
  31.8 0.7 reshape.192.idx_ref
  32.5 0.6 reshape.190.idx_ref
  33.3 0.7 reshape.193.idx_ref.at_ref
  34.1 0.7 reshape.191.idx_ref
  34.8 0.6 pad.12.pts_ref
  35.4 0.6 pad_slice_fusion.pts_ref
  36.0 0.7 pad_slice_fusion.1.pts_ref
  36.7 15.3 %all-to-all-done = f32[16,192,128]{2,1,0:T(8,128)S(1)} async-done(((f32[16,192,128]{2,1,0:T(8,128)}), f32[16,192,128]{2,1,0:T(8,128)S(1)}, u32[]{:S(2)}, u32[]{:S(2)}) %all-to-all-start) | async-done | bytes 1572896 | tf_op jit(solution)/shard_map/all_to_all | solution.py:376
  52.0 0.7 broadcast_in_dim.14.want_ref
  52.8 3.9 %collective-permute-start = (f32[16,192,128]{2,1,0:T(8,128)S(1)}, f32[16,192,128]{2,1,0:T(8,128)S(1)}, u32[]{:S(2)}, u32[]{:S(2)}) collective-permute-start(f32[16,192,128]{2,1,0:T(8,128)S(1)} %all-to-all-done), channel_id=1, source_target_pairs={{0,16},{16,0},{32,48},{48,32},{64,80},{80,64},{96,112},{112,96},{1... | collective-permute-start | bytes 4718600 | tf_op jit(solution)/shard_map/ppermute | solution.py:431
  56.6 3.0 %collective-permute-done = f32[16,192,128]{2,1,0:T(8,128)S(1)} collective-permute-done((f32[16,192,128]{2,1,0:T(8,128)S(1)}, f32[16,192,128]{2,1,0:T(8,128)S(1)}, u32[]{:S(2)}, u32[]{:S(2)}) %collective-permute-start) | collective-permute-done | bytes 1572896 | tf_op jit(solution)/shard_map/ppermute | solution.py:431
  59.7 1.9 %pad_maximum_fusion = f32[32,192,128]{2,1,0:T(8,128)} fusion(f32[16,192,128]{2,1,0:T(8,128)S(1)} %collective-permute-done, f32[16,192,128]{2,1,0:T(8,128)S(1)} %all-to-all-done), kind=kLoop, calls=%fused_computation | loop fusion | flops 786432 | bytes 6291456 | tf_op jit(solution)/shard_map/concatenate | solution.py:432
  61.6 11.5 %shard_map.77.tile_hbm = f32[144,128,128]{2,1,0:T(8,128)} custom-call(s32[144]{0:T(256)} %reshape.192.idx_ref, f32[16,8,128]{2,1,0:T(8,128)} %pad.12.pts_ref, f32[6144,128]{1,0:T(8,128)} %bitcast.37), custom_call_target="tpu_custom_call" | custom-call | flops 56623104 | bytes 9437184 | tf_op jit(solution)/shard_map/pallas_call | solution.py:66
  73.2 9.4 %shard_map.78 = (f32[48,128]{1,0:T(8,128)}, f32[16,48,128]{2,1,0:T(8,128)}) custom-call(f32[144,128]{1,0:T(8,128)} %broadcast_in_dim.14.want_ref, f32[128,56,128]{2,1,0:T(8,128)} %all-gather.3.cloned.1.call-done.sens_ref, f32[144,128,128]{2,1,0:T(8,128)} %shard_map.77.tile_hbm), custom_call_target="tpu_custom_call" | custom-call | flops 452984832 | bytes 9437184 | tf_op jit(solution)/shard_map/pallas_call | solution.py:233
  82.6 3.6 %all-to-all-start.2 = ((f32[16,48,128]{2,1,0:T(8,128)}), f32[16,48,128]{2,1,0:T(8,128)S(1)}, u32[]{:S(2)}, u32[]{:S(2)}) async-start(f32[16,48,128]{2,1,0:T(8,128)} %get-tuple-element.37), calls=%async_computation.2 | async-start | bytes 786432 | tf_op jit(solution)/shard_map/all_to_all | solution.py:376
  86.2 11.4 %shard_map.79 = f32[128,48,128]{2,1,0:T(8,128)} custom-call(f32[128,56,128]{2,1,0:T(8,128)} %all-gather.3.cloned.1.call-done.sens_ref), custom_call_target="tpu_custom_call" | custom-call | flops 6442450944 | bytes 7340032 | tf_op jit(solution)/shard_map/pallas_call | solution.py:275
  97.6 0.8 copy-done.1
  98.4 30.3 %shard_map.80.tile_ref = f32[504,128,128]{2,1,0:T(8,128)} custom-call(s32[576]{0:T(1024)} %reshape.193.idx_ref.at_ref, f32[56,8,128]{2,1,0:T(8,128)} %pad_slice_fusion.1.pts_ref, f32[6144,128]{1,0:T(8,128)} %bitcast.38), custom_call_target="tpu_custom_call" | custom-call | flops 198180864 | bytes 33030144 | tf_op jit(solution)/shard_map/pallas_call | solution.py:66
  128.8 0.4 all-gather.5.cloned.1.call-done
  129.1 11.1 %shard_map.81 = (f32[6144,128]{1,0:T(8,128)}, f32[8,128]{1,0:T(8,128)}, f32[128,8,128]{2,1,0:T(8,128)}) custom-call(s32[144]{0:T(256)} %reshape.190.idx_ref, f32[6144,128]{1,0:T(8,128)} %bitcast.40, f32[6144,128]{1,0:T(8,128)} %bitcast.43, f32[144,128,128]{2,1,0:T(8,128)} %shard_map.77.tile_hbm), custom_call_target="tpu_custom_call", output_to_operand_aliasing={{0}: (2, {})} | custom-call | flops 22020096 | bytes 18874368 | tf_op jit(solution)/shard_map/pallas_call | solution.py:354
  140.2 1.1 dynamic-slice_bitcast_fusion
  141.3 10.1 %all-to-all-start.3 = ((f32[128,8,128]{2,1,0:T(8,128)}), f32[128,8,128]{2,1,0:T(8,128)S(1)}, u32[]{:S(2)}, u32[]{:S(2)}) async-start(f32[128,8,128]{2,1,0:T(8,128)} %get-tuple-element.49), calls=%async_computation.3 | async-start | bytes 1048576 | tf_op jit(solution)/shard_map/all_to_all | solution.py:454
  151.4 23.0 %shard_map.82 = (f32[56,8,128]{2,1,0:T(8,128)}, f32[8,8,128]{2,1,0:T(8,128)}) custom-call(s32[576]{0:T(1024)} %reshape.191.idx_ref, s32[576]{0:T(1024)} %reshape.193.idx_ref.at_ref, f32[504,128,128]{2,1,0:T(8,128)} %shard_map.80.tile_ref, f32[6144,128]{1,0:T(8,128)} %bitcast.42, f32[6144,128]{1,0:T(8,128)} %get-tuple-element.52.p_ref, ...), custom_call_target="tpu_custom_call" | custom-call | flops 113246208 | bytes 37748736 | tf_op jit(solution)/shard_map/pallas_call | solution.py:149
  174.6 0.1 slice_reduce_fusion
  174.9 0.8 copy.41
  175.7 1.0 maximum_bitcast_fusion
  176.7 0.8 fusion.2
  (41 shorter events, 1.2 us)
Async XLA Ops:
  7.2 19.1 %copy-start = (f32[3,16384]{1,0:T(4,128)S(1)}, f32[3,16384]{1,0:T(4,128)}, u32[]{:S(2)}) copy-start(f32[3,16384]{1,0:T(4,128)} %param.8) | copy-start | bytes 589828
  7.2 66.0 %all-gather.3.cloned.1.call-start = ((), (), s32[]{:S(2)}) async-start(), calls=%async_computation.4 | async-start | bytes 4128768 | tf_op jit(solution)/shard_map/all_gather | solution.py:380
  8.9 22.5 %copy-start.5 = (s32[128,8]{0,1:T(8,128)S(1)}, s32[128,8]{0,1:T(8,128)}, u32[]{:S(2)}) copy-start(s32[128,8]{0,1:T(8,128)} %param.9) | copy-start | bytes 12292
  26.3 6.9 %copy-start.3 = (s32[64,9]{0,1:T(8,128)S(1)}, s32[64,9]{0,1:T(8,128)}, u32[]{:S(2)}) copy-start(s32[64,9]{0,1:T(8,128)} %param.11) | copy-start | bytes 6916
  26.3 9.2 %copy-start.2 = (f32[3,8192]{1,0:T(4,128)S(1)}, f32[3,8192]{1,0:T(4,128)}, u32[]{:S(2)}) copy-start(f32[3,8192]{1,0:T(4,128)} %param.10) | copy-start | bytes 294916
  27.7 24.4 %all-to-all-start = ((f32[16,192,128]{2,1,0:T(8,128)}), f32[16,192,128]{2,1,0:T(8,128)S(1)}, u32[]{:S(2)}, u32[]{:S(2)}) async-start(f32[16,192,128]{2,1,0:T(8,128)} %broadcast_in_dim.13), calls=%async_computation | async-start | bytes 3145728 | tf_op jit(solution)/shard_map/all_to_all | solution.py:376
  52.8 6.9 %collective-permute-start = (f32[16,192,128]{2,1,0:T(8,128)S(1)}, f32[16,192,128]{2,1,0:T(8,128)S(1)}, u32[]{:S(2)}, u32[]{:S(2)}) collective-permute-start(f32[16,192,128]{2,1,0:T(8,128)S(1)} %all-to-all-done), channel_id=1, source_target_pairs={{0,16},{16,0},{32,48},{48,32},{64,80},{80,64},{96,112},{112,96},{1... | collective-permute-start | bytes 4718600 | tf_op jit(solution)/shard_map/ppermute | solution.py:431
  82.6 15.0 %all-to-all-start.2 = ((f32[16,48,128]{2,1,0:T(8,128)}), f32[16,48,128]{2,1,0:T(8,128)S(1)}, u32[]{:S(2)}, u32[]{:S(2)}) async-start(f32[16,48,128]{2,1,0:T(8,128)} %get-tuple-element.37), calls=%async_computation.2 | async-start | bytes 786432 | tf_op jit(solution)/shard_map/all_to_all | solution.py:376
  86.2 43.0 %all-gather.5.cloned.1.call-start = ((), (), s32[]{:S(2)}) async-start(), calls=%async_computation.5 | async-start | bytes 3538944 | tf_op jit(solution)/shard_map/all_gather | solution.py:380
  97.6 0.8 copy-start.1
  141.3 33.3 %all-to-all-start.3 = ((f32[128,8,128]{2,1,0:T(8,128)}), f32[128,8,128]{2,1,0:T(8,128)S(1)}, u32[]{:S(2)}, u32[]{:S(2)}) async-start(f32[128,8,128]{2,1,0:T(8,128)} %get-tuple-element.49), calls=%async_computation.3 | async-start | bytes 1048576 | tf_op jit(solution)/shard_map/all_to_all | solution.py:454
  151.4 23.1 %copy-start.4 = (f32[8,128]{1,0:T(8,128)S(1)}, f32[8,128]{1,0:T(8,128)}, u32[]{:S(2)}) copy-start(f32[8,128]{1,0:T(8,128)} %get-tuple-element.45) | copy-start | bytes 12292
Sparse Core Ops, SparseCore 0:
  26.4 30.2 all-gather.2
  98.5 30.5 all-gather.4

commit v7 on v6

--- a/solution.py
+++ b/solution.py
@@ -202,9 +202,36 @@
 ]
 
 
-def spread_kernel(want_ref, sens_ref, tile_hbm, own_ref, image_ref, near_ref, tile_ref, acc_ref, sem):
-    copy = pltpu.make_async_copy(tile_hbm, tile_ref, sem)
-    copy.start()
+def spread_kernel(
+    idx_ref, want_ref, pts_ref, half_hbm, other_hbm, sens_hbm,
+    own_ref, image_ref, tile_hbm, ctl_hbm,
+    near_ref, sens_ref, ctl_ref, cols_ref, half_sem, tile_sem, tile_ref, acc_ref, sem,
+):
+    size = half_hbm.shape[0]
+    first = pltpu.make_async_copy(half_hbm, ctl_ref.at[pl.ds(0, size), :], half_sem.at[0])
+    second = pltpu.make_async_copy(other_hbm, ctl_ref.at[pl.ds(size, size), :], half_sem.at[1])
+    sens_copy = pltpu.make_async_copy(sens_hbm, sens_ref, sem)
+    ctl_copy = pltpu.make_async_copy(ctl_ref, ctl_hbm, half_sem.at[2])
+    first.start()
+    second.start()
+    sens_copy.start()
+    for g in range(16):
+        cols_ref[g] = jnp.transpose(pts_ref[g])
+    first.wait()
+    second.wait()
+    ctl_copy.start()
+
+    def tile_copy(g):
+        rows = pl.ds(g * 9, 9)
+        return pltpu.make_async_copy(tile_ref.at[rows], tile_hbm.at[rows], tile_sem.at[g])
+
+    def make(g, carry):
+        phi_block(g, g * 9, 9, idx_ref, cols_ref, ctl_ref, tile_ref)
+        tile_copy(g).start()
+        return carry
+
+    lax.fori_loop(0, 16, make, 0)
+    sens_copy.wait()
     ids = jnp.sum(sens_ref[:, 48, :].reshape(16, 8, BS), axis=1)
     want = want_ref[...]
     acc = [jnp.zeros((144, BS), jnp.float32) for _ in range(3)]
@@ -218,7 +245,6 @@
             acc[k] = acc[k] + jnp.dot(hot, rest, preferred_element_type=jnp.float32)
     for k in range(3):
         near_ref[144 * k : 144 * k + 144] = acc[k]
-    copy.wait()
     sums = operator_sums(tile_ref, acc_ref, lambda n, k: near_ref[pl.ds(n + 144 * k, 1), :])
     for k in range(3):
         for g in range(16):
@@ -227,26 +253,39 @@
             image_ref[0, 16 * k + g : 16 * k + g + 1, :] = own + sums[k][g] * COUPLING
     for n in range(1, 16):
         image_ref[n] = image_ref[0]
-
-
-def spread_and_apply(want, sens, tiles):
+    ctl_copy.wait()
+    for g in range(16):
+        tile_copy(g).wait()
+
+
+def spread_and_apply(idx, want, pts, half, other, sens):
+    vmem, hbm = pl.BlockSpec(memory_space=pltpu.VMEM), pl.BlockSpec(memory_space=pl.ANY)
+    tiles = (144, BS, BS)
+    coords = (2 * half.shape[0], BS)
     return pl.pallas_call(
         spread_kernel,
         out_shape=[
             jax.ShapeDtypeStruct((48, BS), jnp.float32),
             jax.ShapeDtypeStruct((16, 48, BS), jnp.float32),
+            jax.ShapeDtypeStruct(tiles, jnp.float32),
+            jax.ShapeDtypeStruct(coords, jnp.float32),
         ],
-        in_specs=[
-            pl.BlockSpec(memory_space=pltpu.VMEM),
-            pl.BlockSpec(memory_space=pltpu.VMEM),
-            pl.BlockSpec(memory_space=pl.ANY),
-        ],
-        scratch_shapes=[pltpu.VMEM((3 * 144, BS), jnp.float32)] + OPERATOR_SCRATCH,
+        in_specs=[pl.BlockSpec(memory_space=pltpu.SMEM), vmem, vmem, hbm, hbm, hbm],
+        out_specs=[vmem, vmem, hbm, hbm],
+        scratch_shapes=[
+            pltpu.VMEM((3 * 144, BS), jnp.float32),
+            pltpu.VMEM(sens.shape, jnp.float32),
+            pltpu.VMEM(coords, jnp.float32),
+            pltpu.VMEM((16, BS, 8), jnp.float32),
+            pltpu.SemaphoreType.DMA((3,)),
+            pltpu.SemaphoreType.DMA((16,)),
+        ]
+        + OPERATOR_SCRATCH,
         compiler_params=pltpu.CompilerParams(vmem_limit_bytes=VMEM),
         cost_estimate=pl.CostEstimate(
-            flops=144 * 2048 * 384 * 4, bytes_accessed=tiles.size * 4, transcendentals=0
-        ),
-    )(want, sens, tiles)
+            flops=144 * 2048 * 384 * 4, bytes_accessed=144 * BS * BS * 4, transcendentals=0
+        ),
+    )(idx, want, pts, half, other, sens)
 
 
 def spread_all_kernel(sens_ref, out_ref, cut_ref, ids_ref):
@@ -429,9 +468,9 @@
     half, ready = lax.optimization_barrier((half, ready))
     op_at, node_at, op_coord_at, node_coord_at, own_points, points, more_points, want = ready
     other = lax.ppermute(half, "vol", [(i, i ^ 1) for i in range(lax.axis_size("vol"))])
-    coords_rows = jnp.concatenate([half, other], axis=0).reshape(2 * 16 * 192, BS)
-    op_tiles = make_tiles(op_coord_at, own_points, coords_rows, 9, 4)
-    f_own, image = spread_and_apply(want, sens, op_tiles)
+    f_own, image, op_tiles, coords_rows = spread_and_apply(
+        op_coord_at, want, own_points, half.reshape(-1, BS), other.reshape(-1, BS), sens
+    )
     image, sens = lax.optimization_barrier((image, sens))
     near_image = over_ctl(image)
     f_all = spread_all(sens)

time: 185 us -> 179 us (0.968)
  Pallas kernels: 96.8 us -> 91.3 us
  other arithmetic: 4.66 us -> 2.74 us
    pallas_call x2 -> x1, Pallas kernels: 41.9 us -> 30.3 us  [make_tiles(): pl.pallas_call(functools.partial(tiles_kernel, reach, group), out_shape=j...]
    pallas_call x1, Pallas kernels: 9.44 us -> 15.5 us  [spread_and_apply(): pl.pallas_call(spread_kernel, out_shape=[jax.ShapeDtypeStruct((48, BS), j...]
    concatenate x1 -> x0, other arithmetic: 1.92 us -> none  [body(): jnp.concatenate([half, other], axis=0).reshape(2 * 16 * 192, BS)]
  transfers between devices with their start and end apart: 6 -> 6, of which waited for: 3 -> 3; matrix products, arithmetic and copies ran while one was open for 5% -> 4% of each run, Pallas kernels for 41% -> 36%
where the time goes in v7:
time: 179 us; the launch traced here: 178 us
  Pallas kernels  91.3 us (51%)
  starting transfers between devices  21.3 us (12%)
  waiting for transfers between devices  18.8 us (11%)
  blocking collectives  17.4 us (10%)
  between operations  14.3 us (8%)
  local copies, waits for them, and re-layouts  12.4 us (7%)
  other arithmetic  2.74 us (2%)
    pallas_call x1, Pallas kernels, make_tiles(): pl.pallas_call(functools.partial(tiles_kernel, reach, group), out_shape=j...  30.3 us
    pallas_call x1, Pallas kernels, node_sums(): pl.pallas_call(functools.partial(node_kernel, reach, stored, fresh, total...  23 us
    all_to_all x1, blocking collectives, over_ctl(): return lax.all_to_all(x, 'ctl', 0, 0, tiled=True)  17.4 us
    pallas_call x1, Pallas kernels, spread_and_apply(): pl.pallas_call(spread_kernel, out_shape=[jax.ShapeDtypeStruct((48, BS), j...  15.5 us
    all_to_all x2, waiting for transfers between devices, over_ctl(): return lax.all_to_all(x, 'ctl', 0, 0, tiled=True)  15.3 us
    pallas_call x1, Pallas kernels, spread_all(): pl.pallas_call(spread_all_kernel, out_shape=jax.ShapeDtypeStruct((128, 48...  11.4 us
    pallas_call x1, Pallas kernels, step_and_apply(): pl.pallas_call(step_kernel, out_shape=[jax.ShapeDtypeStruct(f.shape, jnp....  11.1 us
    all_to_all x1, starting transfers between devices, body(): dot_rows = lax.all_to_all(dot_rows, ('vol', 'ctl'), 0, 0, tiled=True)  10 us
  transfers between devices with their start and end apart: 6, of which 3 were waited for; matrix products, arithmetic and copies ran while one was open for 4% of the time, Pallas kernels for 36%

profile of v7, /device:TPU:1, one launch (start us, length us, event | category | flops | bytes accessed | tf_op | source)
XLA Modules:
  0.0 178.2 jit_solution(12424726278223900097)
XLA Ops:
  7.2 0.7 add_convert_fusion.1
  8.0 0.8 reshape.170
  8.9 17.4 %all_to_all.20 = f32[16,56,128]{2,1,0:T(8,128)} all-to-all(f32[16,56,128]{2,1,0:T(8,128)S(1)} %broadcast_in_dim.16), channel_id=1, replica_groups=mesh['vol'=8,'ctl'=16] {'ctl'}, dimensions={0} | all-to-all | bytes 917504 | tf_op jit(solution)/shard_map/all_to_all | solution.py:415
  26.4 1.3 broadcast_in_dim.13
  27.7 3.7 %all-to-all-start = ((f32[16,192,128]{2,1,0:T(8,128)}), f32[16,192,128]{2,1,0:T(8,128)S(1)}, u32[]{:S(2)}, u32[]{:S(2)}) async-start(f32[16,192,128]{2,1,0:T(8,128)} %broadcast_in_dim.13), calls=%async_computation | async-start | bytes 3145728 | tf_op jit(solution)/shard_map/all_to_all | solution.py:415
  31.8 0.7 reshape.196.idx_ref
  32.5 0.7 reshape.194.idx_ref
  33.3 0.7 reshape.197.idx_ref.at_ref
  34.1 0.7 reshape.195.idx_ref
  34.9 0.6 pad.12.pts_ref
  35.5 0.6 pad_slice_fusion.pts_ref
  36.1 0.7 pad_slice_fusion.1.pts_ref
  36.8 15.3 %all-to-all-done = f32[16,192,128]{2,1,0:T(8,128)S(1)} async-done(((f32[16,192,128]{2,1,0:T(8,128)}), f32[16,192,128]{2,1,0:T(8,128)S(1)}, u32[]{:S(2)}, u32[]{:S(2)}) %all-to-all-start) | async-done | bytes 1572896 | tf_op jit(solution)/shard_map/all_to_all | solution.py:415
  52.1 0.8 broadcast_in_dim.14.want_ref
  52.9 3.9 %collective-permute-start = (f32[16,192,128]{2,1,0:T(8,128)S(1)}, f32[16,192,128]{2,1,0:T(8,128)S(1)}, u32[]{:S(2)}, u32[]{:S(2)}) collective-permute-start(f32[16,192,128]{2,1,0:T(8,128)S(1)} %all-to-all-done), channel_id=1, source_target_pairs={{0,16},{16,0},{32,48},{48,32},{64,80},{80,64},{96,112},{112,96},{1... | collective-permute-start | bytes 4718600 | tf_op jit(solution)/shard_map/ppermute | solution.py:470
  56.8 3.0 %collective-permute-done = f32[16,192,128]{2,1,0:T(8,128)S(1)} collective-permute-done((f32[16,192,128]{2,1,0:T(8,128)S(1)}, f32[16,192,128]{2,1,0:T(8,128)S(1)}, u32[]{:S(2)}, u32[]{:S(2)}) %collective-permute-start) | collective-permute-done | bytes 1572896 | tf_op jit(solution)/shard_map/ppermute | solution.py:470
  59.8 1.2 copy-done.3
  61.0 15.5 %shard_map.77 = (f32[48,128]{1,0:T(8,128)}, f32[16,48,128]{2,1,0:T(8,128)}, f32[144,128,128]{2,1,0:T(8,128)}, f32[6144,128]{1,0:T(8,128)}) custom-call(s32[144]{0:T(256)} %reshape.196.idx_ref, f32[144,128]{1,0:T(8,128)} %broadcast_in_dim.14.want_ref, f32[16,8,128]{2,1,0:T(8,128)} %pad.12.pts_ref, f32[3072,128]{1,0:T(8,128)} %bitcast.43, ...), custom_call_target="tpu_custom_call" | custom-call | flops 452984832 | bytes 9437184 | tf_op jit(solution)/shard_map/pallas_call | solution.py:265
  76.5 3.6 %all-to-all-start.2 = ((f32[16,48,128]{2,1,0:T(8,128)}), f32[16,48,128]{2,1,0:T(8,128)S(1)}, u32[]{:S(2)}, u32[]{:S(2)}) async-start(f32[16,48,128]{2,1,0:T(8,128)} %get-tuple-element.39), calls=%async_computation.2 | async-start | bytes 786432 | tf_op jit(solution)/shard_map/all_to_all | solution.py:415
  80.1 11.4 %shard_map.78 = f32[128,48,128]{2,1,0:T(8,128)} custom-call(f32[128,56,128]{2,1,0:T(8,128)} %all-gather.3.cloned.1.call-done.sens_hbm.sens_ref), custom_call_target="tpu_custom_call" | custom-call | flops 6442450944 | bytes 7340032 | tf_op jit(solution)/shard_map/pallas_call | solution.py:314
  91.5 0.7 copy-done.2
  92.3 30.3 %shard_map.79.tile_ref = f32[504,128,128]{2,1,0:T(8,128)} custom-call(s32[576]{0:T(1024)} %reshape.197.idx_ref.at_ref, f32[56,8,128]{2,1,0:T(8,128)} %pad_slice_fusion.1.pts_ref, f32[6144,128]{1,0:T(8,128)} %get-tuple-element.46.ctl_ref), custom_call_target="tpu_custom_call" | custom-call | flops 198180864 | bytes 33030144 | tf_op jit(solution)/shard_map/pallas_call | solution.py:66
  122.6 0.4 all-gather.5.cloned.1.call-done
  123.1 11.1 %shard_map.80 = (f32[6144,128]{1,0:T(8,128)}, f32[8,128]{1,0:T(8,128)}, f32[128,8,128]{2,1,0:T(8,128)}) custom-call(s32[144]{0:T(256)} %reshape.194.idx_ref, f32[6144,128]{1,0:T(8,128)} %bitcast.38, f32[6144,128]{1,0:T(8,128)} %bitcast.41, f32[144,128,128]{2,1,0:T(8,128)} %get-tuple-element.48.tile_hbm), custom_call_target="tpu_custom_call", output_to_operand_aliasing={{0}: (2, {})} | custom-call | flops 22020096 | bytes 18874368 | tf_op jit(solution)/shard_map/pallas_call | solution.py:393
  134.1 1.1 dynamic-slice_bitcast_fusion
  135.2 10.0 %all-to-all-start.3 = ((f32[128,8,128]{2,1,0:T(8,128)}), f32[128,8,128]{2,1,0:T(8,128)S(1)}, u32[]{:S(2)}, u32[]{:S(2)}) async-start(f32[128,8,128]{2,1,0:T(8,128)} %get-tuple-element.53), calls=%async_computation.3 | async-start | bytes 1048576 | tf_op jit(solution)/shard_map/all_to_all | solution.py:493
  145.3 23.0 %shard_map.81 = (f32[56,8,128]{2,1,0:T(8,128)}, f32[8,8,128]{2,1,0:T(8,128)}) custom-call(s32[576]{0:T(1024)} %reshape.195.idx_ref, s32[576]{0:T(1024)} %reshape.197.idx_ref.at_ref, f32[504,128,128]{2,1,0:T(8,128)} %shard_map.79.tile_ref, f32[6144,128]{1,0:T(8,128)} %bitcast.40, f32[6144,128]{1,0:T(8,128)} %get-tuple-element.56.p_ref, ...), custom_call_target="tpu_custom_call" | custom-call | flops 113246208 | bytes 37748736 | tf_op jit(solution)/shard_map/pallas_call | solution.py:149
  168.3 0.1 slice_reduce_fusion.2
  168.5 0.1 slice_reduce_fusion
  168.8 0.8 copy.41
  169.6 1.0 maximum_bitcast_fusion
  170.6 0.8 fusion.2
  (43 shorter events, 1.1 us)
Async XLA Ops:
  7.2 19.1 %copy-start = (f32[3,16384]{1,0:T(4,128)S(1)}, f32[3,16384]{1,0:T(4,128)}, u32[]{:S(2)}) copy-start(f32[3,16384]{1,0:T(4,128)} %param.8) | copy-start | bytes 589828
  7.2 52.6 %all-gather.3.cloned.1.call-start = ((), (), s32[]{:S(2)}) async-start(), calls=%async_computation.4 | async-start | bytes 4128768 | tf_op jit(solution)/shard_map/all_gather | solution.py:419
  8.9 22.5 %copy-start.7 = (s32[128,8]{0,1:T(8,128)S(1)}, s32[128,8]{0,1:T(8,128)}, u32[]{:S(2)}) copy-start(s32[128,8]{0,1:T(8,128)} %param.9) | copy-start | bytes 12292
  26.3 6.9 %copy-start.5 = (s32[64,9]{0,1:T(8,128)S(1)}, s32[64,9]{0,1:T(8,128)}, u32[]{:S(2)}) copy-start(s32[64,9]{0,1:T(8,128)} %param.11) | copy-start | bytes 6916
  26.3 9.2 %copy-start.4 = (f32[3,8192]{1,0:T(4,128)S(1)}, f32[3,8192]{1,0:T(4,128)}, u32[]{:S(2)}) copy-start(f32[3,8192]{1,0:T(4,128)} %param.10) | copy-start | bytes 294916
  27.7 24.4 %all-to-all-start = ((f32[16,192,128]{2,1,0:T(8,128)}), f32[16,192,128]{2,1,0:T(8,128)S(1)}, u32[]{:S(2)}, u32[]{:S(2)}) async-start(f32[16,192,128]{2,1,0:T(8,128)} %broadcast_in_dim.13), calls=%async_computation | async-start | bytes 3145728 | tf_op jit(solution)/shard_map/all_to_all | solution.py:415
  52.1 7.7 %copy-start.1 = (f32[16,192,128]{2,1,0:T(8,128)}, f32[16,192,128]{2,1,0:T(8,128)S(1)}, u32[]{:S(2)}) copy-start(f32[16,192,128]{2,1,0:T(8,128)S(1)} %all-to-all-done) | copy-start | bytes 4718596
  52.9 6.9 %collective-permute-start = (f32[16,192,128]{2,1,0:T(8,128)S(1)}, f32[16,192,128]{2,1,0:T(8,128)S(1)}, u32[]{:S(2)}, u32[]{:S(2)}) collective-permute-start(f32[16,192,128]{2,1,0:T(8,128)S(1)} %all-to-all-done), channel_id=1, source_target_pairs={{0,16},{16,0},{32,48},{48,32},{64,80},{80,64},{96,112},{112,96},{1... | collective-permute-start | bytes 4718600 | tf_op jit(solution)/shard_map/ppermute | solution.py:470
  59.8 1.2 copy-start.3
  76.5 15.0 %all-to-all-start.2 = ((f32[16,48,128]{2,1,0:T(8,128)}), f32[16,48,128]{2,1,0:T(8,128)S(1)}, u32[]{:S(2)}, u32[]{:S(2)}) async-start(f32[16,48,128]{2,1,0:T(8,128)} %get-tuple-element.39), calls=%async_computation.2 | async-start | bytes 786432 | tf_op jit(solution)/shard_map/all_to_all | solution.py:415
  80.1 43.0 %all-gather.5.cloned.1.call-start = ((), (), s32[]{:S(2)}) async-start(), calls=%async_computation.5 | async-start | bytes 3538944 | tf_op jit(solution)/shard_map/all_gather | solution.py:419
  91.5 0.7 copy-start.2
  135.2 33.2 %all-to-all-start.3 = ((f32[128,8,128]{2,1,0:T(8,128)}), f32[128,8,128]{2,1,0:T(8,128)S(1)}, u32[]{:S(2)}, u32[]{:S(2)}) async-start(f32[128,8,128]{2,1,0:T(8,128)} %get-tuple-element.53), calls=%async_computation.3 | async-start | bytes 1048576 | tf_op jit(solution)/shard_map/all_to_all | solution.py:493
  145.3 23.0 %copy-start.6 = (f32[8,128]{1,0:T(8,128)S(1)}, f32[8,128]{1,0:T(8,128)}, u32[]{:S(2)}) copy-start(f32[8,128]{1,0:T(8,128)} %get-tuple-element.49) | copy-start | bytes 12292
Sparse Core Ops, SparseCore 0:
  26.4 30.2 all-gather.2
  92.4 30.5 all-gather.4

commit v8 on v7

--- a/solution.py
+++ b/solution.py
@@ -89,19 +89,12 @@
         cols_ref[g] = jnp.transpose(pts_ref[g])
     rows_ref[...] = jnp.zeros_like(rows_ref)
 
-    def first(g):
-        return jnp.where(g < stored, step * stored + g, total + step * fresh + g - stored) * reach
-
-    def fill(g, carry):
-        base = first(g)
+    def fill(g, base):
         for t in range(reach):
             at = idx_ref[base + t]
             for k in range(3):
                 rows_ref[g, k : k + 1, t * BS : (t + 1) * BS] = f_ref[pl.ds(at + 16 * k, 1), :]
                 rows_ref[g, k + 3 : k + 4, t * BS : (t + 1) * BS] = p_ref[pl.ds(at + 16 * k, 1), :]
-        return carry
-
-    lax.fori_loop(0, stored + fresh, fill, 0)
 
     def apply(src_ref, g, slot):
         rows = rows_ref[slot]
@@ -115,6 +108,7 @@
         raw_ref[slot] = out + lax.dot_general(rest, cut, dims, preferred_element_type=jnp.float32)
 
     def old(g, carry):
+        fill(g, (step * stored + g) * reach)
         apply(tile_ref, g, g)
         return carry
 
@@ -128,6 +122,7 @@
     if fresh:
         lax.fori_loop(0, fresh, make, 0)
         for g in range(fresh):
+            fill(stored + g, (total + step * fresh + g) * reach)
             apply(new_ref, g, stored + g)
     for g in range(stored + fresh):
         both = jnp.transpose(raw_ref[g])

time: 179 us -> 178 us (level)
  no operation moved by 1% of the time
where the time goes in v8:
time: 178 us; the launch traced here: 177 us
  Pallas kernels  90.2 us (51%)
  starting transfers between devices  21.3 us (12%)
  waiting for transfers between devices  18.8 us (11%)
  blocking collectives  17.4 us (10%)
  between operations  14.3 us (8%)
  local copies, waits for them, and re-layouts  12.4 us (7%)
  other arithmetic  2.74 us (2%)
    pallas_call x1, Pallas kernels, make_tiles(): pl.pallas_call(functools.partial(tiles_kernel, reach, group), out_shape=j...  30.3 us
    pallas_call x1, Pallas kernels, node_sums(): pl.pallas_call(functools.partial(node_kernel, reach, stored, fresh, total...  21.9 us
    all_to_all x1, blocking collectives, over_ctl(): return lax.all_to_all(x, 'ctl', 0, 0, tiled=True)  17.4 us
    pallas_call x1, Pallas kernels, spread_and_apply(): pl.pallas_call(spread_kernel, out_shape=[jax.ShapeDtypeStruct((48, BS), j...  15.5 us
    all_to_all x2, waiting for transfers between devices, over_ctl(): return lax.all_to_all(x, 'ctl', 0, 0, tiled=True)  15.3 us
    pallas_call x1, Pallas kernels, spread_all(): pl.pallas_call(spread_all_kernel, out_shape=jax.ShapeDtypeStruct((128, 48...  11.4 us
    pallas_call x1, Pallas kernels, step_and_apply(): pl.pallas_call(step_kernel, out_shape=[jax.ShapeDtypeStruct(f.shape, jnp....  11 us
    all_to_all x1, starting transfers between devices, body(): dot_rows = lax.all_to_all(dot_rows, ('vol', 'ctl'), 0, 0, tiled=True)  10.1 us
  transfers between devices with their start and end apart: 6, of which 3 were waited for; matrix products, arithmetic and copies ran while one was open for 4% of the time, Pallas kernels for 36%

profile of v8, /device:TPU:1, one launch (start us, length us, event | category | flops | bytes accessed | tf_op | source)
XLA Modules:
  0.0 177.1 jit_solution(13198873691407221011)
XLA Ops:
  7.2 0.7 add_convert_fusion.1
  8.0 0.8 reshape.170
  8.9 17.4 %all_to_all.20 = f32[16,56,128]{2,1,0:T(8,128)} all-to-all(f32[16,56,128]{2,1,0:T(8,128)S(1)} %broadcast_in_dim.16), channel_id=1, replica_groups=mesh['vol'=8,'ctl'=16] {'ctl'}, dimensions={0} | all-to-all | bytes 917504 | tf_op jit(solution)/shard_map/all_to_all | solution.py:410
  26.4 1.3 broadcast_in_dim.13
  27.7 3.7 %all-to-all-start = ((f32[16,192,128]{2,1,0:T(8,128)}), f32[16,192,128]{2,1,0:T(8,128)S(1)}, u32[]{:S(2)}, u32[]{:S(2)}) async-start(f32[16,192,128]{2,1,0:T(8,128)} %broadcast_in_dim.13), calls=%async_computation | async-start | bytes 3145728 | tf_op jit(solution)/shard_map/all_to_all | solution.py:410
  31.8 0.7 reshape.196.idx_ref
  32.5 0.7 reshape.194.idx_ref
  33.3 0.7 reshape.197.idx_ref.at_ref
  34.1 0.7 reshape.195.idx_ref
  34.9 0.6 pad.12.pts_ref
  35.5 0.6 pad_slice_fusion.pts_ref
  36.1 0.7 pad_slice_fusion.1.pts_ref
  36.8 15.3 %all-to-all-done = f32[16,192,128]{2,1,0:T(8,128)S(1)} async-done(((f32[16,192,128]{2,1,0:T(8,128)}), f32[16,192,128]{2,1,0:T(8,128)S(1)}, u32[]{:S(2)}, u32[]{:S(2)}) %all-to-all-start) | async-done | bytes 1572896 | tf_op jit(solution)/shard_map/all_to_all | solution.py:410
  52.1 0.8 broadcast_in_dim.14.want_ref
  52.9 3.9 %collective-permute-start = (f32[16,192,128]{2,1,0:T(8,128)S(1)}, f32[16,192,128]{2,1,0:T(8,128)S(1)}, u32[]{:S(2)}, u32[]{:S(2)}) collective-permute-start(f32[16,192,128]{2,1,0:T(8,128)S(1)} %all-to-all-done), channel_id=1, source_target_pairs={{0,16},{16,0},{32,48},{48,32},{64,80},{80,64},{96,112},{112,96},{1... | collective-permute-start | bytes 4718600 | tf_op jit(solution)/shard_map/ppermute | solution.py:465
  56.8 3.0 %collective-permute-done = f32[16,192,128]{2,1,0:T(8,128)S(1)} collective-permute-done((f32[16,192,128]{2,1,0:T(8,128)S(1)}, f32[16,192,128]{2,1,0:T(8,128)S(1)}, u32[]{:S(2)}, u32[]{:S(2)}) %collective-permute-start) | collective-permute-done | bytes 1572896 | tf_op jit(solution)/shard_map/ppermute | solution.py:465
  59.8 1.2 copy-done.3
  61.0 15.5 %shard_map.77 = (f32[48,128]{1,0:T(8,128)}, f32[16,48,128]{2,1,0:T(8,128)}, f32[144,128,128]{2,1,0:T(8,128)}, f32[6144,128]{1,0:T(8,128)}) custom-call(s32[144]{0:T(256)} %reshape.196.idx_ref, f32[144,128]{1,0:T(8,128)} %broadcast_in_dim.14.want_ref, f32[16,8,128]{2,1,0:T(8,128)} %pad.12.pts_ref, f32[3072,128]{1,0:T(8,128)} %bitcast.43, ...), custom_call_target="tpu_custom_call" | custom-call | flops 452984832 | bytes 9437184 | tf_op jit(solution)/shard_map/pallas_call | solution.py:260
  76.5 3.6 %all-to-all-start.2 = ((f32[16,48,128]{2,1,0:T(8,128)}), f32[16,48,128]{2,1,0:T(8,128)S(1)}, u32[]{:S(2)}, u32[]{:S(2)}) async-start(f32[16,48,128]{2,1,0:T(8,128)} %get-tuple-element.39), calls=%async_computation.2 | async-start | bytes 786432 | tf_op jit(solution)/shard_map/all_to_all | solution.py:410
  80.1 11.4 %shard_map.78 = f32[128,48,128]{2,1,0:T(8,128)} custom-call(f32[128,56,128]{2,1,0:T(8,128)} %all-gather.3.cloned.1.call-done.sens_hbm.sens_ref), custom_call_target="tpu_custom_call" | custom-call | flops 6442450944 | bytes 7340032 | tf_op jit(solution)/shard_map/pallas_call | solution.py:309
  91.5 0.7 copy-done.2
  92.3 30.3 %shard_map.79.tile_ref = f32[504,128,128]{2,1,0:T(8,128)} custom-call(s32[576]{0:T(1024)} %reshape.197.idx_ref.at_ref, f32[56,8,128]{2,1,0:T(8,128)} %pad_slice_fusion.1.pts_ref, f32[6144,128]{1,0:T(8,128)} %get-tuple-element.46.ctl_ref), custom_call_target="tpu_custom_call" | custom-call | flops 198180864 | bytes 33030144 | tf_op jit(solution)/shard_map/pallas_call | solution.py:66
  122.6 0.4 all-gather.5.cloned.1.call-done
  123.1 11.0 %shard_map.80 = (f32[6144,128]{1,0:T(8,128)}, f32[8,128]{1,0:T(8,128)}, f32[128,8,128]{2,1,0:T(8,128)}) custom-call(s32[144]{0:T(256)} %reshape.194.idx_ref, f32[6144,128]{1,0:T(8,128)} %bitcast.38, f32[6144,128]{1,0:T(8,128)} %bitcast.41, f32[144,128,128]{2,1,0:T(8,128)} %get-tuple-element.48.tile_hbm), custom_call_target="tpu_custom_call", output_to_operand_aliasing={{0}: (2, {})} | custom-call | flops 22020096 | bytes 18874368 | tf_op jit(solution)/shard_map/pallas_call | solution.py:388
  134.1 1.1 dynamic-slice_bitcast_fusion
  135.2 10.1 %all-to-all-start.3 = ((f32[128,8,128]{2,1,0:T(8,128)}), f32[128,8,128]{2,1,0:T(8,128)S(1)}, u32[]{:S(2)}, u32[]{:S(2)}) async-start(f32[128,8,128]{2,1,0:T(8,128)} %get-tuple-element.53), calls=%async_computation.3 | async-start | bytes 1048576 | tf_op jit(solution)/shard_map/all_to_all | solution.py:488
  145.3 21.9 %shard_map.81 = (f32[56,8,128]{2,1,0:T(8,128)}, f32[8,8,128]{2,1,0:T(8,128)}) custom-call(s32[576]{0:T(1024)} %reshape.195.idx_ref, s32[576]{0:T(1024)} %reshape.197.idx_ref.at_ref, f32[504,128,128]{2,1,0:T(8,128)} %shard_map.79.tile_ref, f32[6144,128]{1,0:T(8,128)} %bitcast.40, f32[6144,128]{1,0:T(8,128)} %get-tuple-element.56.p_ref, ...), custom_call_target="tpu_custom_call" | custom-call | flops 113246208 | bytes 37748736 | tf_op jit(solution)/shard_map/pallas_call | solution.py:144
  167.3 0.1 slice_reduce_fusion.2
  167.4 0.1 slice_reduce_fusion
  167.7 0.8 copy.41
  168.5 1.0 maximum_bitcast_fusion
  169.5 0.8 fusion.2
  (43 shorter events, 1.1 us)
Async XLA Ops:
  7.2 19.1 %copy-start = (f32[3,16384]{1,0:T(4,128)S(1)}, f32[3,16384]{1,0:T(4,128)}, u32[]{:S(2)}) copy-start(f32[3,16384]{1,0:T(4,128)} %param.8) | copy-start | bytes 589828
  7.2 52.6 %all-gather.3.cloned.1.call-start = ((), (), s32[]{:S(2)}) async-start(), calls=%async_computation.4 | async-start | bytes 4128768 | tf_op jit(solution)/shard_map/all_gather | solution.py:414
  8.9 22.5 %copy-start.7 = (s32[128,8]{0,1:T(8,128)S(1)}, s32[128,8]{0,1:T(8,128)}, u32[]{:S(2)}) copy-start(s32[128,8]{0,1:T(8,128)} %param.9) | copy-start | bytes 12292
  26.3 6.9 %copy-start.5 = (s32[64,9]{0,1:T(8,128)S(1)}, s32[64,9]{0,1:T(8,128)}, u32[]{:S(2)}) copy-start(s32[64,9]{0,1:T(8,128)} %param.11) | copy-start | bytes 6916
  26.3 9.2 %copy-start.4 = (f32[3,8192]{1,0:T(4,128)S(1)}, f32[3,8192]{1,0:T(4,128)}, u32[]{:S(2)}) copy-start(f32[3,8192]{1,0:T(4,128)} %param.10) | copy-start | bytes 294916
  27.7 24.4 %all-to-all-start = ((f32[16,192,128]{2,1,0:T(8,128)}), f32[16,192,128]{2,1,0:T(8,128)S(1)}, u32[]{:S(2)}, u32[]{:S(2)}) async-start(f32[16,192,128]{2,1,0:T(8,128)} %broadcast_in_dim.13), calls=%async_computation | async-start | bytes 3145728 | tf_op jit(solution)/shard_map/all_to_all | solution.py:410
  52.1 7.7 %copy-start.1 = (f32[16,192,128]{2,1,0:T(8,128)}, f32[16,192,128]{2,1,0:T(8,128)S(1)}, u32[]{:S(2)}) copy-start(f32[16,192,128]{2,1,0:T(8,128)S(1)} %all-to-all-done) | copy-start | bytes 4718596
  52.9 6.9 %collective-permute-start = (f32[16,192,128]{2,1,0:T(8,128)S(1)}, f32[16,192,128]{2,1,0:T(8,128)S(1)}, u32[]{:S(2)}, u32[]{:S(2)}) collective-permute-start(f32[16,192,128]{2,1,0:T(8,128)S(1)} %all-to-all-done), channel_id=1, source_target_pairs={{0,16},{16,0},{32,48},{48,32},{64,80},{80,64},{96,112},{112,96},{1... | collective-permute-start | bytes 4718600 | tf_op jit(solution)/shard_map/ppermute | solution.py:465
  59.8 1.2 copy-start.3
  76.5 15.0 %all-to-all-start.2 = ((f32[16,48,128]{2,1,0:T(8,128)}), f32[16,48,128]{2,1,0:T(8,128)S(1)}, u32[]{:S(2)}, u32[]{:S(2)}) async-start(f32[16,48,128]{2,1,0:T(8,128)} %get-tuple-element.39), calls=%async_computation.2 | async-start | bytes 786432 | tf_op jit(solution)/shard_map/all_to_all | solution.py:410
  80.1 43.0 %all-gather.5.cloned.1.call-start = ((), (), s32[]{:S(2)}) async-start(), calls=%async_computation.5 | async-start | bytes 3538944 | tf_op jit(solution)/shard_map/all_gather | solution.py:414
  91.5 0.7 copy-start.2
  135.2 32.2 %all-to-all-start.3 = ((f32[128,8,128]{2,1,0:T(8,128)}), f32[128,8,128]{2,1,0:T(8,128)S(1)}, u32[]{:S(2)}, u32[]{:S(2)}) async-start(f32[128,8,128]{2,1,0:T(8,128)} %get-tuple-element.53), calls=%async_computation.3 | async-start | bytes 1048576 | tf_op jit(solution)/shard_map/all_to_all | solution.py:488
  145.3 22.0 %copy-start.6 = (f32[8,128]{1,0:T(8,128)S(1)}, f32[8,128]{1,0:T(8,128)}, u32[]{:S(2)}) copy-start(f32[8,128]{1,0:T(8,128)} %get-tuple-element.49) | copy-start | bytes 12292
Sparse Core Ops, SparseCore 0:
  26.4 30.2 all-gather.2
  92.4 30.5 all-gather.4
